TPU v7x, 32 devices: a whole 2x2x4 slice. The times are simulated.
32 devices in a mesh: cp: 8 (over z, x), tp: 4 (over y, core).
Axes of the slice: x: 2, y: 2, z: 4, core: 2. Of those that a mesh axis runs over, the one named last changes fastest.
Arguments:
- layer_input: bfloat16 [4096, 1536], P('cp'), may hold values from -6 to 6
- norm1_gain: float32 [1536], replicated, may hold values from 0.1 to 1.9
- w_query: bfloat16 [1536, 1536], P(None, 'tp'), may hold values from -0.15625 to 0.15625
- b_query: float32 [1536], P('tp'), may hold values from -3 to 3
- w_key: bfloat16 [1536, 256], replicated, may hold values from -0.15625 to 0.15625
- b_key: float32 [256], replicated, may hold values from -3 to 3
- w_value: bfloat16 [1536, 256], replicated, may hold values from -0.15625 to 0.15625
- b_value: float32 [256], replicated, may hold values from -3 to 3
- w_out: bfloat16 [1536, 1536], P('tp'), may hold values from -0.4375 to 0.4375
- norm2_gain: float32 [1536], replicated, may hold values from 0.1 to 1.9
- w_gate: bfloat16 [1536, 8960], P(None, 'tp'), may hold values from -0.15625 to 0.15625
- w_up: bfloat16 [1536, 8960], P(None, 'tp'), may hold values from -0.15625 to 0.15625
- w_down: bfloat16 [8960, 1536], P('tp'), may hold values from -0.125 to 0.125
- doc_ids: int32 [4096], replicated, may hold values from 0 to 2, as said below
- positions: int32 [4096], replicated, may hold values from 0 to 2047, as said below
- cotangent: bfloat16 [4096, 1536], P('cp'), may hold values from -6 to 6
Outputs:
- output: bfloat16 [4096, 1536], P('cp')
- grad_x: bfloat16 [4096, 1536], P('cp')
- grad_norm1_gain: float32 [1536], replicated
- grad_w_query: float32 [1536, 1536], P('cp', 'tp')
- grad_b_query: float32 [1536], P('tp')
- grad_w_key: float32 [1536, 256], P('cp')
- grad_b_key: float32 [256], replicated
- grad_w_value: float32 [1536, 256], P('cp')
- grad_b_value: float32 [256], replicated
- grad_w_out: float32 [1536, 1536], P('tp', 'cp')
- grad_norm2_gain: float32 [1536], replicated
- grad_w_gate: float32 [1536, 8960], P('cp', 'tp')
- grad_w_up: float32 [1536, 8960], P('cp', 'tp')
- grad_w_down: float32 [8960, 1536], P('tp', 'cp')
Inputs may be any that keep to these rules, and one draw needn't show every extreme that they name: `doc_ids`: document 0 has 2048 tokens in 16 blocks of 128; index i of cp holds block i as its first 128 tokens and block 15 - i as its last. Between them each index i holds 256 tokens of document 1 if i is below a cut c (1 <= c < 8, drawn), else of document 2; documents 1 and 2 run in order over the indices, index i holding their block i, resp. i - c. `positions`: each token's place in its document; documents are laid out as doc_ids states, every document's places starting at 0.
All inputs are finite; a program needn't handle non-finite values.
Results may differ from a plain program's by a relative error of at most 0.025.
Values may be sent and summed in bfloat16 or wider, within the bound.
A program may use at most 192 MiB of HBM per device.

v0:
```python
import math

import jax
import jax.numpy as jnp
from jax import lax
from jax.sharding import PartitionSpec as P

H = 12
HD = 128


EPSILON = 1e-06
ROPE_BASE = 10000.0
MASKED = -1e30


def matmul(left, right):
    return jnp.dot(left, right, preferred_element_type=jnp.float32)


def contract_rows(left, right):
    return lax.dot_general(
        left, right, (((0,), (0,)), ((), ())), preferred_element_type=jnp.float32
    )


def contract_cols(left, right):
    return lax.dot_general(
        left, right, (((1,), (1,)), ((), ())), preferred_element_type=jnp.float32
    )


def rope_tables(tok_pos, width):
    half = width // 2
    freq = ROPE_BASE ** (-(jnp.arange(half, dtype=jnp.float32) * 2.0 / width))
    angle = tok_pos.astype(jnp.float32)[:, None] * freq[None, :]
    cosine = jnp.concatenate([jnp.cos(angle), jnp.cos(angle)], -1)[:, None, :]
    sine = jnp.concatenate([jnp.sin(angle), jnp.sin(angle)], -1)[:, None, :]
    return (cosine, sine)


def rotary(values, cosine, sine):
    half = values.shape[-1] // 2
    return values * cosine + jnp.concatenate([-values[..., half:], values[..., :half]], -1) * sine


def rotary_back(grads, cosine, sine):
    half = grads.shape[-1] // 2
    scaled = grads * sine
    return grads * cosine + jnp.concatenate([scaled[..., half:], -scaled[..., :half]], -1)


def sweep(step_fn, carry, piece):
    count = piece.shape[0]
    size = math.gcd(count, 1024)
    blocks = piece.reshape(count // size, size, piece.shape[1])

    def advance(state, item):
        index, block_rows = item
        return (step_fn(state, block_rows, index * size), None)

    carry, unused = lax.scan(advance, carry, (jnp.arange(count // size, dtype=jnp.int32), blocks))
    return carry


def on_device(
    layer_input,
    norm1_gain,
    w_query,
    b_query,
    w_key,
    b_key,
    w_value,
    b_value,
    w_out,
    norm2_gain,
    w_gate,
    w_up,
    w_down,
    doc_ids,
    positions,
    cotangent,
):
    tok_rows = layer_input.shape[0]
    head_dim = HD
    q_heads = w_query.shape[1] // head_dim
    kv_heads = w_key.shape[1] // head_dim
    group_size = H // kv_heads
    scale = head_dim ** (-0.5)
    shard = lax.axis_index("cp")
    kv_index = lax.axis_index("tp") * q_heads // group_size
    my_doc = lax.dynamic_slice_in_dim(doc_ids, shard * tok_rows, tok_rows)
    my_pos = lax.dynamic_slice_in_dim(positions, shard * tok_rows, tok_rows)
    cosine, sine = rope_tables(my_pos, head_dim)
    query_doc = jnp.tile(my_doc, q_heads)
    query_pos = jnp.tile(my_pos, q_heads)
    flat_rows = q_heads * tok_rows
    inputs = layer_input.astype(jnp.float32)
    scale1 = lax.rsqrt(jnp.mean(inputs * inputs, axis=-1, keepdims=True) + EPSILON)
    normed1 = (inputs * scale1 * norm1_gain).astype(jnp.bfloat16)
    q_pre = matmul(normed1, w_query) + b_query
    k_pre = matmul(normed1, w_key) + b_key
    v_pre = matmul(normed1, w_value) + b_value
    q_rot = rotary(q_pre.reshape(tok_rows, q_heads, head_dim), cosine, sine).astype(jnp.bfloat16)
    k_rot = rotary(k_pre.reshape(tok_rows, kv_heads, head_dim), cosine, sine).astype(jnp.bfloat16)
    v_low = v_pre.astype(jnp.bfloat16).reshape(tok_rows, kv_heads, head_dim)
    k_mine = lax.dynamic_index_in_dim(k_rot, kv_index, 1, keepdims=False)
    v_mine = lax.dynamic_index_in_dim(v_low, kv_index, 1, keepdims=False)
    kv_mine = jnp.concatenate([k_mine, v_mine], 1)
    q_flat = q_rot.transpose(1, 0, 2).reshape(flat_rows, head_dim)

    def key_mask(start, count):
        key_doc = lax.dynamic_slice_in_dim(doc_ids, start, count)
        key_pos = lax.dynamic_slice_in_dim(positions, start, count)
        return (query_doc[:, None] == key_doc[None, :]) & (key_pos[None, :] <= query_pos[:, None])

    def attend_block(carry, piece, start):
        peak, total, accum = carry
        count = piece.shape[0]
        allowed = key_mask(start, count)
        scores = jnp.where(allowed, contract_cols(q_flat, piece[:, :head_dim]) * scale, MASKED)
        fresh = jnp.maximum(peak, jnp.max(scores, axis=1))
        shrink = jnp.exp(peak - fresh)
        weights = jnp.where(allowed, jnp.exp(scores - fresh[:, None]), 0.0)
        total = total * shrink + jnp.sum(weights, axis=1)
        accum = accum * shrink[:, None] + matmul(weights.astype(jnp.bfloat16), piece[:, head_dim:])
        return (fresh, total, accum)

    start_state = (
        jnp.full((flat_rows,), MASKED, jnp.float32),
        jnp.zeros((flat_rows,), jnp.float32),
        jnp.zeros((flat_rows, head_dim), jnp.float32),
    )
    peak, total, accum = sweep(
        attend_block, start_state, lax.all_gather(kv_mine, "cp", axis=0, tiled=True)
    )
    attn_full = accum / total[:, None]
    log_total = peak + jnp.log(total)
    attn_low = (
        attn_full.astype(jnp.bfloat16)
        .reshape(q_heads, tok_rows, head_dim)
        .transpose(1, 0, 2)
        .reshape(tok_rows, flat_rows // tok_rows * head_dim)
    )
    attn_sum = lax.psum(matmul(attn_low, w_out).astype(jnp.bfloat16), "tp").astype(jnp.float32)
    middle = inputs + attn_sum
    scale2 = lax.rsqrt(jnp.mean(middle * middle, axis=-1, keepdims=True) + EPSILON)
    normed2 = (middle * scale2 * norm2_gain).astype(jnp.bfloat16)
    gate = matmul(normed2, w_gate)
    up_part = matmul(normed2, w_up)
    sigma = jax.nn.sigmoid(gate)
    swish = gate * sigma
    hidden = (swish * up_part).astype(jnp.bfloat16)
    ffn_sum = lax.psum(matmul(hidden, w_down).astype(jnp.bfloat16), "tp").astype(jnp.float32)
    output = (middle + ffn_sum).astype(jnp.bfloat16)
    grad_out = cotangent.astype(jnp.float32)
    grad_hidden = contract_cols(cotangent, w_down)
    grad_w_down = contract_rows(hidden, cotangent)
    grad_gate = (grad_hidden * up_part * sigma * (1.0 + gate * (1.0 - sigma))).astype(jnp.bfloat16)
    grad_up = (grad_hidden * swish).astype(jnp.bfloat16)
    grad_w_gate = contract_rows(normed2, grad_gate)
    grad_w_up = contract_rows(normed2, grad_up)
    grad_normed2 = lax.psum(
        (contract_cols(grad_gate, w_gate) + contract_cols(grad_up, w_up)).astype(jnp.bfloat16), "tp"
    ).astype(jnp.float32)
    weighted2 = grad_normed2 * norm2_gain
    gain2_part = jnp.sum(grad_normed2 * middle * scale2, axis=0)
    grad_middle = (
        grad_out
        + scale2 * weighted2
        - middle * scale2**3 * jnp.mean(weighted2 * middle, axis=-1, keepdims=True)
    )
    grad_branch = grad_middle.astype(jnp.bfloat16)
    grad_w_out = contract_rows(attn_low, grad_branch)
    grad_attn = contract_cols(grad_branch, w_out).astype(jnp.bfloat16)
    grad_attn_flat = (
        grad_attn.reshape(tok_rows, q_heads, head_dim)
        .transpose(1, 0, 2)
        .reshape(flat_rows, head_dim)
    )
    delta = jnp.sum(grad_attn_flat.astype(jnp.float32) * attn_full, axis=-1)

    def attend_back_block(carry, piece, start):
        grad_query, grad_pairs = carry
        count = piece.shape[0]
        keys = piece[:, :head_dim]
        values = piece[:, head_dim:]
        allowed = key_mask(start, count)
        scores = jnp.where(allowed, contract_cols(q_flat, keys) * scale, MASKED)
        probs = jnp.where(allowed, jnp.exp(scores - log_total[:, None]), 0.0)
        grad_probs = contract_cols(grad_attn_flat, values)
        grad_scores = (probs * (grad_probs - delta[:, None])).astype(jnp.bfloat16)
        grad_query = grad_query + matmul(grad_scores, keys) * scale
        grad_keys = contract_rows(grad_scores, q_flat) * scale
        grad_values = contract_rows(probs.astype(jnp.bfloat16), grad_attn_flat)
        previous = lax.dynamic_slice_in_dim(grad_pairs, start, count, 0)
        grad_pairs = lax.dynamic_update_slice_in_dim(
            grad_pairs, previous + jnp.concatenate([grad_keys, grad_values], 1), start, 0
        )
        return (grad_query, grad_pairs)

    start_back = (
        jnp.zeros((flat_rows, head_dim), jnp.float32),
        jnp.zeros((tok_rows * lax.axis_size("cp"), 2 * head_dim), jnp.float32),
    )
    grad_q_rot, grad_pairs = sweep(
        attend_back_block, start_back, lax.all_gather(kv_mine, "cp", axis=0, tiled=True)
    )
    pair_sum = lax.psum_scatter(
        grad_pairs.astype(jnp.bfloat16), "cp", scatter_dimension=0, tiled=True
    ).astype(jnp.float32)
    head_hit = (jnp.arange(kv_heads) == kv_index)[None, :, None]
    spread = jnp.where(head_hit, pair_sum[:, None, :], 0.0).reshape(
        tok_rows, kv_heads * 2 * head_dim
    )
    pair_all = (
        lax.psum(spread.astype(jnp.bfloat16), "tp")
        .astype(jnp.float32)
        .reshape(tok_rows, kv_heads, 2 * head_dim)
    )
    grad_k_pre = (
        rotary_back(pair_all[:, :, :head_dim], cosine, sine)
        .reshape(tok_rows, kv_heads * head_dim)
        .astype(jnp.bfloat16)
    )
    grad_v_low = (
        pair_all[:, :, head_dim:].reshape(tok_rows, kv_heads * head_dim).astype(jnp.bfloat16)
    )
    grad_q_heads = grad_q_rot.reshape(q_heads, tok_rows, head_dim).transpose(1, 0, 2)
    grad_q_pre = (
        rotary_back(grad_q_heads, cosine, sine)
        .reshape(tok_rows, q_heads * head_dim)
        .astype(jnp.bfloat16)
    )
    grad_w_query = contract_rows(normed1, grad_q_pre)
    grad_w_key = contract_rows(normed1, grad_k_pre)
    grad_w_value = contract_rows(normed1, grad_v_low)
    bias_query = jnp.sum(grad_q_pre.astype(jnp.float32), axis=0)
    bias_key = jnp.sum(grad_k_pre.astype(jnp.float32), axis=0)
    bias_value = jnp.sum(grad_v_low.astype(jnp.float32), axis=0)
    grad_normed1 = lax.psum(contract_cols(grad_q_pre, w_query).astype(jnp.bfloat16), "tp").astype(
        jnp.float32
    )
    grad_normed1 = (
        grad_normed1 + contract_cols(grad_k_pre, w_key) + contract_cols(grad_v_low, w_value)
    )
    weighted1 = grad_normed1 * norm1_gain
    gain1_part = jnp.sum(grad_normed1 * inputs * scale1, axis=0)
    grad_input = (
        grad_middle
        + scale1 * weighted1
        - inputs * scale1**3 * jnp.mean(weighted1 * inputs, axis=-1, keepdims=True)
    ).astype(jnp.bfloat16)
    gain1_sum, bias_query, bias_key, bias_value, gain2_sum = lax.psum(
        (gain1_part, bias_query, bias_key, bias_value, gain2_part), "cp"
    )
    grad_w_query, grad_w_key, grad_w_value, grad_w_out, grad_w_gate, grad_w_up, grad_w_down = (
        lax.psum_scatter(
            grad_w_query.astype(jnp.bfloat16), "cp", scatter_dimension=0, tiled=True
        ).astype(jnp.float32),
        lax.psum_scatter(
            grad_w_key.astype(jnp.bfloat16), "cp", scatter_dimension=0, tiled=True
        ).astype(jnp.float32),
        lax.psum_scatter(
            grad_w_value.astype(jnp.bfloat16), "cp", scatter_dimension=0, tiled=True
        ).astype(jnp.float32),
        lax.psum_scatter(
            grad_w_out.astype(jnp.bfloat16), "cp", scatter_dimension=1, tiled=True
        ).astype(jnp.float32),
        lax.psum_scatter(
            grad_w_gate.astype(jnp.bfloat16), "cp", scatter_dimension=0, tiled=True
        ).astype(jnp.float32),
        lax.psum_scatter(
            grad_w_up.astype(jnp.bfloat16), "cp", scatter_dimension=0, tiled=True
        ).astype(jnp.float32),
        lax.psum_scatter(
            grad_w_down.astype(jnp.bfloat16), "cp", scatter_dimension=1, tiled=True
        ).astype(jnp.float32),
    )
    return (
        output,
        grad_input,
        gain1_sum,
        grad_w_query,
        bias_query,
        grad_w_key,
        bias_key,
        grad_w_value,
        bias_value,
        grad_w_out,
        gain2_sum,
        grad_w_gate,
        grad_w_up,
        grad_w_down,
    )


def solution(mesh):
    return jax.shard_map(
        on_device,
        mesh=mesh,
        in_specs=(
            P("cp", None),
            P(),
            P(None, "tp"),
            P("tp"),
            P(),
            P(),
            P(),
            P(),
            P("tp", None),
            P(),
            P(None, "tp"),
            P(None, "tp"),
            P("tp", None),
            P(),
            P(),
            P("cp", None),
        ),
        out_specs=(
            P("cp", None),
            P("cp", None),
            P(),
            P("cp", "tp"),
            P("tp"),
            P("cp", None),
            P(),
            P("cp", None),
            P(),
            P("tp", "cp"),
            P(),
            P("cp", "tp"),
            P("cp", "tp"),
            P("tp", "cp"),
        ),
        check_vma=False,
    )
```

profile of v0, /device:TPU:0, one launch (start us, length us, event | category | flops | bytes accessed | tf_op | source)
XLA Modules:
  0.0 1185.3 jit_solution(848007194295818206)
XLA Ops:
  32.1 46.2 %all-gather.2.cloned.1.call-done = bf16[4096,256]{1,0:T(8,128)(2,1)} async-done(((bf16[512,256]{1,0:T(8,128)(2,1)}), bf16[4096,256]{1,0:T(8,128)(2,1)}) %all-gather.2.cloned.1.call-update) | async-done | bytes 2097168 | tf_op jit(solution)/shard_map/all_gather | solution.py:135
  78.3 74.3 %while.28 = (s32[]{:T(128)}, f32[1536]{0:T(1024)S(1)}, f32[1536]{0:T(1024)S(1)}, f32[1536,128]{1,0:T(8,128)}, s32[4]{0:T(128)S(1)}, /*index=5*/s32[4096]{0:T(102...) while((s32[]{:T(128)}, f32[1536]{0:T(1024)S(1)}, ...), condition=%wide.region_4.5_spmd.clone, body=%wide.region_1.4_spmd.clone.sunk | while | flops 840506880 | bytes 47808760 | solution.py:62
  156.9 41.0 %all-reduce.6.cloned.1.call-done = bf16[512,1536]{1,0:T(8,128)(2,1)} async-done(((bf16[512,1536]{1,0:T(8,128)(2,1)}), bf16[512,1536]{1,0:T(8,128)(2,1)}) %all-reduce.6.cloned.1.call-update) | async-done | bytes 1572880 | tf_op jit(solution)/shard_map/psum | solution.py:145
  200.7 6.9 fusion.79
  207.7 5.5 fusion.80
  213.2 11.3 multiply_convert_fusion
  224.5 5.7 fusion.81
  230.3 5.2 fusion.51
  236.3 42.2 %all-reduce.8.cloned.1.call-done = bf16[512,1536]{1,0:T(8,128)(2,1)} async-done(((bf16[512,1536]{1,0:T(8,128)(2,1)}), bf16[512,1536]{1,0:T(8,128)(2,1)}) %all-reduce.8.cloned.1.call-update) | async-done | bytes 1572880 | tf_op jit(solution)/shard_map/psum | solution.py:163
  288.4 75.5 %while.29 = (s32[]{:T(128)}, f32[1536,128]{1,0:T(8,128)}, f32[4096,256]{0,1:T(8,128)}, s32[4]{0:T(128)S(1)}, s32[4096]{0:T(1024)}, /*index=5*/s32[4096]{0:T(1024...) while((s32[]{:T(128)}, f32[1536,128]{1,0:T(8,128)}, ...), condition=%wide.region_12.13_spmd.clone, body=%wide.region_11.12_spmd.clone.sunk | while | flops 2031812608 | bytes 39678220 | solution.py:62
  368.0 8.7 convolution_convert_fusion.4
  380.4 55.4 %reduce-scatter.9.cloned.1.call-done = bf16[512,256]{0,1:T(8,128)(2,1)} async-done(((bf16[4096,256]{0,1:T(8,128)(2,1)}), bf16[512,256]{0,1:T(8,128)(2,1)}) %reduce-scatter.9.cloned.1.call-update) | async-done | bytes 262160 | tf_op jit(solution)/shard_map/reduce_scatter | solution.py:209
  444.4 70.9 %all-reduce.10.cloned.1.call-done = (bf16[512,1536]{1,0:T(8,128)(2,1)}, bf16[512,2,256]{2,0,1:T(8,128)(2,1)}, bf16[512,1536]{1,0:T(8,128)(2,1)}) async-done(((bf16[512,1536]{1,0:T(8,128)(2,1)}, bf16[512,2,256]{2,0,1:T(8,128)(2,1)}, bf16[512,1536]{1,0:T(8,128)(2,1)}), (bf16[512,1536]{1,0:T(8,128)(2,1)}, bf16[512,2,256]{2,0,1:T(8,128)(2,1)}, bf16[512,1536]{1,0:T(8,128)(2,1)})) %all-reduce.10.cloned.1.call-update) | async-done | bytes 3670032 | tf_op jit(solution)/shard_map/psum | solution.py:154
  525.1 7.7 convolution_convert_fusion.2
  533.1 7.7 convolution_convert_fusion.1
  542.2 7.5 convolution_convert_fusion
  549.8 33.6 %reduce-scatter.11.cloned.1.call-done = bf16[192,384]{1,0:T(8,128)(2,1)} async-done(((bf16[1536,384]{1,0:T(8,128)(2,1)}), bf16[192,384]{1,0:T(8,128)(2,1)}) %reduce-scatter.11.cloned.1.call-update) | async-done | bytes 147472 | tf_op jit(solution)/shard_map/reduce_scatter | solution.py:258
  585.0 65.3 %reduce-scatter.17.cloned.1.call-done = bf16[384,192]{0,1:T(8,128)(2,1)} async-done(((bf16[384,1536]{0,1:T(8,128)(2,1)}), bf16[384,192]{0,1:T(8,128)(2,1)}) %reduce-scatter.17.cloned.1.call-update) | async-done | bytes 147472 | tf_op jit(solution)/shard_map/reduce_scatter | solution.py:267
  656.8 35.8 %all-reduce = (f32[1536]{0:T(1024)}, f32[384]{0:T(512)}, f32[256]{0:T(256)}, f32[256]{0:T(256)}, f32[1536]{0:T(1024)}) all-reduce(f32[1536]{0:T(1024)S(1)} %get-tuple-element.238, f32[384]{0:T(512)S(1)} %bitcast.160, f32[256]{0:T(256)S(1)} %bitcast.161, f32[256]{0:T(256)S(1)} %bitcast.162, ...), channel_id=1, replica_groups=mesh['cp'=8,'tp'=4] {'cp'}, use_global_device_ids=true, to_apply=%region_18.19 | all-reduce | flops 3968 | bytes 31744 | tf_op jit(solution)/shard_map/psum | solution.py:254
  697.8 17.2 %reduce-scatter.13.cloned.1.call-done = bf16[192,256]{1,0:T(8,128)(2,1)} async-done(((bf16[1536,256]{1,0:T(8,128)(2,1)}), bf16[192,256]{1,0:T(8,128)(2,1)}) %reduce-scatter.13.cloned.1.call-update) | async-done | bytes 98320 | tf_op jit(solution)/shard_map/reduce_scatter | solution.py:261
  716.6 63.5 %reduce-scatter.15.cloned.1.call-done = bf16[192,256]{1,0:T(8,128)(2,1)} async-done(((bf16[1536,256]{1,0:T(8,128)(2,1)}), bf16[192,256]{1,0:T(8,128)(2,1)}) %reduce-scatter.15.cloned.1.call-update) | async-done | bytes 98320 | tf_op jit(solution)/shard_map/reduce_scatter | solution.py:264
  781.7 129.9 %reduce-scatter.19.cloned.1.call-done = bf16[192,2240]{1,0:T(8,128)(2,1)} async-done(((bf16[1536,2240]{1,0:T(8,128)(2,1)}), bf16[192,2240]{1,0:T(8,128)(2,1)}) %reduce-scatter.19.cloned.1.call-update) | async-done | bytes 860176 | tf_op jit(solution)/shard_map/reduce_scatter | solution.py:270
  914.2 129.7 %reduce-scatter.21.cloned.1.call-done = bf16[192,2240]{1,0:T(8,128)(2,1)} async-done(((bf16[1536,2240]{1,0:T(8,128)(2,1)}), bf16[192,2240]{1,0:T(8,128)(2,1)}) %reduce-scatter.21.cloned.1.call-update) | async-done | bytes 860176 | tf_op jit(solution)/shard_map/reduce_scatter | solution.py:273
  1046.4 129.2 %reduce-scatter.23.cloned.1.call-done = bf16[2240,192]{0,1:T(8,128)(2,1)} async-done(((bf16[2240,1536]{0,1:T(8,128)(2,1)}), bf16[2240,192]{0,1:T(8,128)(2,1)}) %reduce-scatter.23.cloned.1.call-update) | async-done | bytes 860176 | tf_op jit(solution)/shard_map/reduce_scatter | solution.py:276
  (312 shorter events, 238.2 us)
Async XLA Ops:
  7.2 147.1 %copy-start = (bf16[384,1536]{1,0:T(8,128)(2,1)S(1)}, bf16[384,1536]{1,0:T(8,128)(2,1)}, u32[]{:S(2)}) copy-start(bf16[384,1536]{1,0:T(8,128)(2,1)} %param.28) | copy-start | bytes 3538948
  7.2 71.1 %all-gather.2.cloned.1.call-start = ((), (), s32[]{:S(2)}) async-start(), calls=%async_computation.8 | async-start | bytes 2359296 | tf_op jit(solution)/shard_map/all_gather | solution.py:135
  26.2 171.8 %all-reduce.6.cloned.1.call-start = ((), (), s32[]{:S(2)}) async-start(), calls=%async_computation.9 | async-start | bytes 3145728 | tf_op jit(solution)/shard_map/psum | solution.py:145
  154.2 45.8 %copy-start.16 = (bf16[512,3,128]{0,2,1:T(8,128)(2,1)}, bf16[512,3,128]{0,2,1:T(8,128)(2,1)S(1)}, u32[]{:S(2)}) copy-start(bf16[512,3,128]{0,2,1:T(8,128)(2,1)S(1)} %copy.52) | copy-start | bytes 1179652
  156.4 43.7 %copy-start.30 = (f32[1536]{0:T(1024)S(1)}, f32[1536]{0:T(1024)}, u32[]{:S(2)}) copy-start(f32[1536]{0:T(1024)} %param.29) | copy-start | bytes 18436
  156.4 122.1 %all-reduce.8.cloned.1.call-start = ((), (), s32[]{:S(2)}) async-start(), calls=%async_computation.10 | async-start | bytes 3145728 | tf_op jit(solution)/shard_map/psum | solution.py:163
  207.7 16.8 %slice-start = ((s8[6881280]{0:T(1024)(128)(4,1)}), s8[4194304]{0:T(1024)(128)(4,1)S(1)}, s32[]{:S(2)}) async-start(s8[6881280]{0:T(1024)(128)(4,1)} %bitcast.163), calls=%async_computation.20 | async-start | bytes 8388608
  213.2 11.3 slice-start.1
  235.5 200.3 %reduce-scatter.9.cloned.1.call-start = ((), (), s32[]{:S(2)}) async-start(), calls=%async_computation.11 | async-start | bytes 2359296 | tf_op jit(solution)/shard_map/reduce_scatter | solution.py:209
  367.6 147.6 %all-reduce.10.cloned.1.call-start = ((), (), s32[]{:S(2)}) async-start(), calls=%async_computation.19 | async-start | bytes 7340032 | tf_op jit(solution)/shard_map/psum | solution.py:154
  380.4 57.6 %copy-start.4 = (bf16[512,1536]{1,0:T(8,128)(2,1)S(1)}, bf16[512,1536]{1,0:T(8,128)(2,1)}, u32[]{:S(2)}) copy-start(bf16[512,1536]{1,0:T(8,128)(2,1)} %param.20) | copy-start | bytes 4718596
  380.4 57.6 %copy-start.33 = (f32[1536]{0:T(1024)S(1)}, f32[1536]{0:T(1024)}, u32[]{:S(2)}) copy-start(f32[1536]{0:T(1024)} %param.21) | copy-start | bytes 18436
  380.4 57.6 %copy-start.35 = (f32[512]{0:T(512)S(1)}, f32[512]{0:T(512)}, u32[]{:S(2)}) copy-start(f32[512]{0:T(512)} %copy-done.34) | copy-start | bytes 6148
  438.0 145.4 %reduce-scatter.11.cloned.1.call-start = ((), (), s32[]{:S(2)}) async-start(), calls=%async_computation.12 | async-start | bytes 1327104 | tf_op jit(solution)/shard_map/reduce_scatter | solution.py:258
  440.3 210.0 %reduce-scatter.17.cloned.1.call-start = ((), (), s32[]{:S(2)}) async-start(), calls=%async_computation.15 | async-start | bytes 1327104 | tf_op jit(solution)/shard_map/reduce_scatter | solution.py:267
  444.3 270.7 %reduce-scatter.13.cloned.1.call-start = ((), (), s32[]{:S(2)}) async-start(), calls=%async_computation.13 | async-start | bytes 884736 | tf_op jit(solution)/shard_map/reduce_scatter | solution.py:261
  518.7 261.4 %reduce-scatter.15.cloned.1.call-start = ((), (), s32[]{:S(2)}) async-start(), calls=%async_computation.14 | async-start | bytes 884736 | tf_op jit(solution)/shard_map/reduce_scatter | solution.py:264
  525.0 386.6 %reduce-scatter.19.cloned.1.call-start = ((), (), s32[]{:S(2)}) async-start(), calls=%async_computation.16 | async-start | bytes 7962624 | tf_op jit(solution)/shard_map/reduce_scatter | solution.py:270
  532.8 511.1 %reduce-scatter.21.cloned.1.call-start = ((), (), s32[]{:S(2)}) async-start(), calls=%async_computation.17 | async-start | bytes 7962624 | tf_op jit(solution)/shard_map/reduce_scatter | solution.py:273
  540.8 634.7 %reduce-scatter.23.cloned.1.call-start = ((), (), s32[]{:S(2)}) async-start(), calls=%async_computation.18 | async-start | bytes 7962624 | tf_op jit(solution)/shard_map/reduce_scatter | solution.py:276
  549.7 102.3 %copy-start.21 = (bf16[512,1536]{1,0:T(8,128)(2,1)S(1)}, bf16[512,1536]{1,0:T(8,128)(2,1)}, u32[]{:S(2)}) copy-start(bf16[512,1536]{1,0:T(8,128)(2,1)} %get-tuple-element.295) | copy-start | bytes 4718596
  653.8 38.8 %copy-start.10 = (bf16[512,1536]{1,0:T(8,128)(2,1)S(1)}, bf16[512,1536]{1,0:T(8,128)(2,1)}, u32[]{:S(2)}) copy-start(bf16[512,1536]{1,0:T(8,128)(2,1)} %all-reduce.6.cloned.1.call-done) | copy-start | bytes 4718596
  653.9 38.8 %copy-start.36 = (f32[512]{0:T(512)S(1)}, f32[512]{0:T(512)}, u32[]{:S(2)}) copy-start(f32[512]{0:T(512)} %get-tuple-element.323) | copy-start | bytes 6148
  911.7 266.4 %copy-start.1 = (bf16[384,1536]{1,0:T(8,128)(2,1)S(1)}, bf16[384,1536]{1,0:T(8,128)(2,1)}, u32[]{:S(2)}) copy-start(bf16[384,1536]{1,0:T(8,128)(2,1)} %param.28) | copy-start | bytes 3538948
  (36 other events, 166.5 us)
Sparse Core Ops, SparseCore 0:
  26.3 51.9 all-gather.1
  156.5 41.3 all-reduce.5
  235.6 42.8 all-reduce.7
  367.8 67.9 reduce-scatter.8
  438.8 76.4 all-reduce.9
  519.1 64.2 reduce-scatter.10
  587.3 62.9 reduce-scatter.16
  653.6 61.3 reduce-scatter.12
  718.7 61.3 reduce-scatter.14
  783.7 127.9 reduce-scatter.18
  915.8 128.0 reduce-scatter.20
  1047.4 128.0 reduce-scatter.22
where the time goes:
time: 1200 us; the launch traced here: 1190 us
  waiting for transfers between devices  824 us (69%)
  matrix products  172 us (14%)
  other arithmetic  76 us (6%)
  local copies, waits for them, and re-layouts  54.2 us (5%)
  blocking collectives  35.8 us (3%)
  between operations  15.3 us (1%)
    reduce_scatter x1, waiting for transfers between devices, on_device(): lax.psum_scatter(grad_w_gate.astype(jnp.bfloat16), 'cp', scatter_dimensio...  130 us
    reduce_scatter x1, waiting for transfers between devices, on_device(): lax.psum_scatter(grad_w_up.astype(jnp.bfloat16), 'cp', scatter_dimension=...  130 us
    reduce_scatter x1, waiting for transfers between devices, on_device(): lax.psum_scatter(grad_w_down.astype(jnp.bfloat16), 'cp', scatter_dimensio...  129 us
    psum x1, waiting for transfers between devices, on_device(): lax.psum(matmul(hidden, w_down).astype(jnp.bfloat16), 'tp')  70.9 us
    dot_general x19, matrix products, contract_cols(): lax.dot_general(left, right, (((1,), (1,)), ((), ())), preferred_element_...  67.3 us
    reduce_scatter x1, waiting for transfers between devices, on_device(): lax.psum_scatter(grad_w_out.astype(jnp.bfloat16), 'cp', scatter_dimension...  65.3 us
    reduce_scatter x1, waiting for transfers between devices, on_device(): lax.psum_scatter(grad_w_value.astype(jnp.bfloat16), 'cp', scatter_dimensi...  63.5 us
    dot_general x15, matrix products, matmul(): return jnp.dot(left, right, preferred_element_type=jnp.float32)  58.5 us
  transfers between devices with their start and end apart: 12, of which 12 were waited for; matrix products, arithmetic and copies ran while one was open for 7% of the time, Pallas kernels for 0%

commit v1 on v0

v1 whole, which is shorter than its diff:
```python
import functools
import math

import jax
import jax.numpy as jnp
from jax import lax
from jax.experimental import pallas as pl
from jax.experimental.pallas import tpu as pltpu
from jax.sharding import PartitionSpec as P

H = 12
HD = 128
HALF = 128
EPSILON = 1e-06
ROPE_BASE = 10000.0
MASKED = -1e30
LOG2E = 1.4426950408889634
TILE = 256
CHUNK_TILES = 3
VMEM_LIMIT = 56 * 1024 * 1024
TP_ORDER = (0, 2, 1, 3)


def matmul(left, right):
    return jnp.dot(left, right, preferred_element_type=jnp.float32)


def contract_rows(left, right):
    return lax.dot_general(
        left, right, (((0,), (0,)), ((), ())), preferred_element_type=jnp.float32
    )


def contract_cols(left, right):
    return lax.dot_general(
        left, right, (((1,), (1,)), ((), ())), preferred_element_type=jnp.float32
    )


def rope_tables(tok_pos, width):
    half = width // 2
    freq = ROPE_BASE ** (-(jnp.arange(half, dtype=jnp.float32) * 2.0 / width))
    angle = tok_pos.astype(jnp.float32)[:, None] * freq[None, :]
    cosine = jnp.concatenate([jnp.cos(angle), jnp.cos(angle)], -1)
    sine = jnp.concatenate([jnp.sin(angle), jnp.sin(angle)], -1)
    return (cosine, sine)


def rotary(values, cosine, sine):
    half = values.shape[-1] // 2
    return values * cosine + jnp.concatenate([-values[..., half:], values[..., :half]], -1) * sine


def rotary_back(grads, cosine, sine):
    half = grads.shape[-1] // 2
    scaled = grads * sine
    return grads * cosine + jnp.concatenate([scaled[..., half:], -scaled[..., :half]], -1)


def swap(value, axis, bit):
    size = lax.axis_size(axis)
    return lax.ppermute(value, axis, [(i, i ^ bit) for i in range(size)])


def after(value, *earlier):
    return lax.optimization_barrier((value, *earlier))[0]


def bits_of(size):
    return size.bit_length() - 1


def reverse_bits(index, bits):
    out = 0
    for i in range(bits):
        out = out | (((index >> i) & 1) << (bits - 1 - i))
    return out


def params(**more):
    return pltpu.CompilerParams(vmem_limit_bytes=VMEM_LIMIT, **more)


SMEM = pl.BlockSpec(memory_space=pltpu.SMEM)
VMEM = pl.BlockSpec(memory_space=pltpu.VMEM)


def spread_kernel(shards, place_ref, rows_ref, own_ref, send_ref, turned):
    me, core = place_ref[0], place_ref[1]
    turned[...] = rows_ref[...].T
    width = turned.shape[0] // shards
    bits = bits_of(shards)
    for i in range(shards // 2):
        far = reverse_bits(i, bits)
        block = pl.multiple_of((me ^ far) * width, 16)
        own_ref[i * width : (i + 1) * width, :] = turned[pl.ds(block, width), :]
    for i in range(shards // 4):
        far = reverse_bits(core * (shards // 4) + i, bits) | 1
        block = pl.multiple_of((me ^ far) * width, 16)
        send_ref[i * width : (i + 1) * width, :] = turned[pl.ds(block, width), :]


def spread(place, rows, shards):
    count, width = rows.shape
    return pl.pallas_call(
        functools.partial(spread_kernel, shards),
        out_shape=(
            jax.ShapeDtypeStruct((width // 2, count), rows.dtype),
            jax.ShapeDtypeStruct((width // 4, count), rows.dtype),
        ),
        in_specs=[SMEM, VMEM],
        out_specs=(VMEM, VMEM),
        scratch_shapes=[pltpu.VMEM((width, count), rows.dtype)],
        compiler_params=params(),
        cost_estimate=pl.CostEstimate(flops=0, bytes_accessed=4 * rows.size, transcendentals=0),
    )(place, rows)


def share(place, rows, shards):
    own, send = spread(place, rows, shards)
    near = swap(send, "cp", 1)
    return own, near, swap(near, "tp", 1)


def weigh_kernel(place_ref, own_ref, near_ref, far_ref, mine_ref, theirs_ref, send_ref, keep_ref, joined):
    core = place_ref[1]

    @pl.when(pl.program_id(0) == 0)
    def _():
        joined[core] = near_ref[...]
        joined[1 - core] = far_ref[...]

    half = send_ref.shape[0]
    mine, theirs = mine_ref[...], theirs_ref[...]
    send_ref[...] = (
        matmul(own_ref[half:, :], mine) + matmul(joined[1], theirs)
    ).astype(send_ref.dtype)
    keep_ref[...] = (
        matmul(own_ref[:half, :], mine) + matmul(joined[0], theirs)
    ).astype(keep_ref.dtype)


def weigh(place, shared, mine, theirs):
    own, near, far = shared
    half, count = near.shape
    width = mine.shape[1]
    tile = min(width, 512)
    whole = lambda j: (0, 0)
    column = lambda j: (0, j)
    return pl.pallas_call(
        weigh_kernel,
        grid=(pl.cdiv(width, tile),),
        out_shape=(jax.ShapeDtypeStruct((half, width), jnp.bfloat16),) * 2,
        in_specs=[
            SMEM,
            pl.BlockSpec((2 * half, count), whole),
            pl.BlockSpec((half, count), whole),
            pl.BlockSpec((half, count), whole),
            pl.BlockSpec((count, tile), column),
            pl.BlockSpec((count, tile), column),
        ],
        out_specs=(pl.BlockSpec((half, tile), column),) * 2,
        scratch_shapes=[pltpu.VMEM((2, half, count), jnp.bfloat16)],
        compiler_params=params(),
        cost_estimate=pl.CostEstimate(
            flops=8 * half * count * width,
            bytes_accessed=4 * (2 * half * count + count * width + half * width),
            transcendentals=0,
        ),
    )(place, own, near, far, mine, theirs)


def weight_grad(place, shared, mine, shards):
    theirs = swap(mine, "cp", 1)
    send, keep = weigh(place, shared, mine, theirs)
    terms = [keep]
    bit = 2
    while bit < shards:
        terms.append(swap(send, "cp", bit))
        bit *= 2
        if bit < shards:
            rows = terms[0].shape[0] // 2
            send = sum(t[rows:].astype(jnp.float32) for t in terms).astype(jnp.bfloat16)
            terms = [t[:rows] for t in terms]
    return sum(t.astype(jnp.float32) for t in terms)


def hidden_kernel(first, last, offset, units, *refs):
    place_ref, rows_ref, cot_ref, gate_ref, up_ref, down_ref = refs[:6]
    refs = refs[6:]
    if not first:
        before_ref, refs = refs[0], refs[1:]
    hidden_ref, grads_ref, sum_ref, total = refs
    step = pl.program_id(0)

    @pl.when(step == 0)
    def _():
        total[...] = jnp.zeros_like(total) if first else before_ref[...]

    rows = rows_ref[...]
    w_gate, w_up, w_down = gate_ref[...], up_ref[...], down_ref[...]
    if last:
        left = units - (offset + step) * TILE
        inside = lax.broadcasted_iota(jnp.int32, w_gate.shape, 1) < left
        w_gate = jnp.where(inside, w_gate, 0)
        w_up = jnp.where(inside, w_up, 0)
        inside = lax.broadcasted_iota(jnp.int32, w_down.shape, 0) < left
        w_down = jnp.where(inside, w_down, 0)
    gate = matmul(rows, w_gate)
    up_part = matmul(rows, w_up)
    grad_hidden = contract_cols(cot_ref[...], w_down)
    sigma = jax.nn.sigmoid(gate)
    swish = gate * sigma
    hidden_ref[...] = (swish * up_part).astype(jnp.bfloat16)
    grad_gate = (grad_hidden * up_part * sigma * (1.0 + gate * (1.0 - sigma))).astype(jnp.bfloat16)
    grad_up = (grad_hidden * swish).astype(jnp.bfloat16)
    grads_ref[:, :TILE] = grad_gate
    grads_ref[:, TILE:] = grad_up
    total[...] += contract_cols(grad_gate, w_gate) + contract_cols(grad_up, w_up)

    @pl.when(step == pl.num_programs(0) - 1)
    def _():
        if last:
            part = total.shape[0] // len(TP_ORDER)
            for i, far in enumerate(TP_ORDER):
                block = pl.multiple_of((place_ref[2] ^ far) * part, part)
                sum_ref[i * part : (i + 1) * part, :] = total[pl.ds(block, part), :].astype(
                    sum_ref.dtype
                )
        else:
            sum_ref[...] = total[...]


def hidden_chunk(place, rows, cotangent, w_gate, w_up, w_down, before, index):
    count, width = rows.shape
    units = w_gate.shape[1]
    tiles = pl.cdiv(units, TILE)
    offset = index * CHUNK_TILES
    steps = min(CHUNK_TILES, tiles - offset)
    first, last = index == 0, offset + steps == tiles
    inner = min(steps * TILE, units - offset * TILE)
    outer = (steps - 1) * 2 * TILE + TILE + inner - (steps - 1) * TILE
    whole = lambda j: (0, 0)
    column = lambda j: (0, j)
    in_specs = [
        SMEM,
        pl.BlockSpec((count, width), whole),
        pl.BlockSpec((count, width), whole),
        pl.BlockSpec((width, TILE), lambda j: (0, offset + j)),
        pl.BlockSpec((width, TILE), lambda j: (0, offset + j)),
        pl.BlockSpec((TILE, width), lambda j: (offset + j, 0)),
    ]
    operands = [place, rows, cotangent, w_gate, w_up, w_down]
    if not first:
        in_specs.append(pl.BlockSpec((count, width), whole))
        operands.append(before)
    return pl.pallas_call(
        functools.partial(hidden_kernel, first, last, offset, units),
        grid=(steps,),
        out_shape=(
            jax.ShapeDtypeStruct((count, inner), jnp.bfloat16),
            jax.ShapeDtypeStruct((count, outer), jnp.bfloat16),
            jax.ShapeDtypeStruct((count, width), jnp.bfloat16 if last else jnp.float32),
        ),
        in_specs=in_specs,
        out_specs=(
            pl.BlockSpec((count, TILE), column),
            pl.BlockSpec((count, 2 * TILE), column),
            pl.BlockSpec((count, width), whole),
        ),
        scratch_shapes=[pltpu.VMEM((count, width), jnp.float32)],
        compiler_params=params(),
        cost_estimate=pl.CostEstimate(
            flops=10 * count * width * inner,
            bytes_accessed=6 * width * inner + 12 * count * width,
            transcendentals=count * inner,
        ),
    )(*operands)


def region_rows(ref, start, count):
    return ref[:, start : start + count, :].reshape(-1, HD)


def triangle(rows, keys):
    row = lax.broadcasted_iota(jnp.int32, (rows, keys), 0) & (keys - 1)
    return row >= lax.broadcasted_iota(jnp.int32, (rows, keys), 1)


def regions(place_ref, shards, tok_rows):
    me, start = place_ref[0], place_ref[3]
    bits = bits_of(shards)

    def of_first(block):
        low = block < shards
        device = jnp.where(low, block, 2 * shards - 1 - block)
        return reverse_bits(device ^ me, bits), jnp.where(low, 0, tok_rows - HALF)

    def of_middle(block):
        return reverse_bits((start + block) ^ me, bits), HALF

    return (
        (0, HALF, me, of_first),
        (tok_rows - HALF, HALF, 2 * shards - 1 - me, of_first),
        (HALF, tok_rows - 2 * HALF, me - start, of_middle),
    )


def attend_kernel(shards, place_ref, q_ref, mine_ref, other_ref, low_ref, full_ref, log_ref, pair):
    core = place_ref[1]
    pair[core] = mine_ref[...]
    pair[1 - core] = other_ref[...]
    heads, tok_rows = q_ref.shape[0], q_ref.shape[1]
    factor = HD**-0.5 * LOG2E
    for begin, count, blocks, locate in regions(place_ref, shards, tok_rows):
        query = region_rows(q_ref, begin, count)
        rows = heads * count

        def read(which, block):
            slot, offset = locate(block)
            return pair[which, slot, pl.ds(pl.multiple_of(offset, HALF), count), :]

        mask = triangle(rows, count)
        last = jnp.where(mask, contract_cols(query, read(0, blocks)), MASKED)
        peak = lax.fori_loop(
            0, blocks, lambda t, top: jnp.maximum(top, contract_cols(query, read(0, t))), last
        )
        peak = jnp.max(peak, axis=1, keepdims=True) * factor

        def add(block, carry, scores):
            total, accum = carry
            weights = jnp.exp2(scores * factor - peak)
            return total + weights, accum + matmul(weights.astype(jnp.bfloat16), read(1, block))

        carry = add(blocks, (jnp.zeros((rows, count), jnp.float32), jnp.zeros((rows, HD), jnp.float32)), last)
        total, accum = lax.fori_loop(
            0, blocks, lambda t, held: add(t, held, contract_cols(query, read(0, t))), carry
        )
        total = jnp.sum(total, axis=1, keepdims=True)
        full = accum / total
        log_total = jnp.broadcast_to(peak + jnp.log2(total), (rows, HD))
        for head in range(heads):
            part = slice(head * count, (head + 1) * count)
            lanes = slice(head * HD, (head + 1) * HD)
            low_ref[begin : begin + count, lanes] = full[part].astype(jnp.bfloat16)
            full_ref[head, begin : begin + count, :] = full[part]
            log_ref[head, begin : begin + count, :] = log_total[part]


def attend(place, query, mine, other):
    heads, tok_rows, _ = query.shape
    shards = mine.shape[0]
    pairs = heads * tok_rows * tok_rows * shards // 4
    return pl.pallas_call(
        functools.partial(attend_kernel, shards),
        out_shape=(
            jax.ShapeDtypeStruct((tok_rows, heads * HD), jnp.bfloat16),
            jax.ShapeDtypeStruct((heads, tok_rows, HD), jnp.float32),
            jax.ShapeDtypeStruct((heads, tok_rows, HD), jnp.float32),
        ),
        in_specs=[SMEM, VMEM, VMEM, VMEM],
        out_specs=(VMEM, VMEM, VMEM),
        scratch_shapes=[pltpu.VMEM((2,) + mine.shape, jnp.bfloat16)],
        compiler_params=params(),
        cost_estimate=pl.CostEstimate(
            flops=6 * pairs * HD, bytes_accessed=4 * mine.size, transcendentals=pairs
        ),
    )(place, query, mine, other)


def attend_back_kernel(
    shards, place_ref, q_ref, mine_ref, other_ref, low_ref, full_ref, log_ref, cos_ref, sin_ref,
    query_ref, keep_ref, send_ref, pair, grads,
):
    core = place_ref[1]
    pair[core] = mine_ref[...]
    pair[1 - core] = other_ref[...]
    grads[...] = jnp.zeros_like(grads)
    heads, tok_rows = q_ref.shape[0], q_ref.shape[1]
    scale = HD**-0.5
    factor = scale * LOG2E
    sign = jnp.where(lax.broadcasted_iota(jnp.int32, (1, HD), 1) < HD // 2, 1.0, -1.0)
    for begin, count, blocks, locate in regions(place_ref, shards, tok_rows):
        query = region_rows(q_ref, begin, count)
        rows = heads * count
        incoming = jnp.concatenate(
            [low_ref[begin : begin + count, h * HD : (h + 1) * HD] for h in range(heads)], 0
        )
        full = region_rows(full_ref, begin, count)
        log_total = region_rows(log_ref, begin, count)[:, :1]
        delta = jnp.sum(incoming.astype(jnp.float32) * full, axis=1, keepdims=True)

        def add(block, grad_query, mask=None):
            slot, offset = locate(block)
            place = pl.ds(pl.multiple_of(offset, HALF), count)
            keys, values = pair[0, slot, place, :], pair[1, slot, place, :]
            probs = jnp.exp2(contract_cols(query, keys) * factor - log_total)
            if mask is not None:
                probs = jnp.where(mask, probs, 0.0)
            grad_scores = (probs * (contract_cols(incoming, values) - delta)).astype(jnp.bfloat16)
            grads[0, slot, place, :] += contract_rows(grad_scores, query)
            grads[1, slot, place, :] += contract_rows(probs.astype(jnp.bfloat16), incoming)
            return grad_query + matmul(grad_scores, keys)

        grad_query = add(blocks, jnp.zeros((rows, HD), jnp.float32), triangle(rows, count))
        grad_query = lax.fori_loop(0, blocks, add, grad_query) * scale
        cosine, sine = cos_ref[begin : begin + count, :], sin_ref[begin : begin + count, :]
        for head in range(heads):
            part = grad_query[head * count : (head + 1) * count]
            turned = part * cosine + pltpu.roll(part * sine, HD // 2, 1) * sign
            query_ref[begin : begin + count, head * HD : (head + 1) * HD] = turned.astype(
                jnp.bfloat16
            )
    is_key = core == 0
    keep_ref[...] = (grads[core] * jnp.where(is_key, scale, 1.0)).astype(jnp.bfloat16)
    send_ref[...] = (grads[1 - core] * jnp.where(is_key, 1.0, scale)).astype(jnp.bfloat16)


def attend_back(place, query, mine, other, low, full, log_total, cosine, sine):
    heads, tok_rows, _ = query.shape
    shards = mine.shape[0]
    pairs = heads * tok_rows * tok_rows * shards // 4
    return pl.pallas_call(
        functools.partial(attend_back_kernel, shards),
        out_shape=(
            jax.ShapeDtypeStruct((tok_rows, heads * HD), jnp.bfloat16),
            jax.ShapeDtypeStruct(mine.shape, jnp.bfloat16),
            jax.ShapeDtypeStruct(mine.shape, jnp.bfloat16),
        ),
        in_specs=[SMEM] + [VMEM] * 8,
        out_specs=(VMEM, VMEM, VMEM),
        scratch_shapes=[
            pltpu.VMEM((2,) + mine.shape, jnp.bfloat16),
            pltpu.VMEM((2,) + mine.shape, jnp.float32),
        ],
        compiler_params=params(),
        cost_estimate=pl.CostEstimate(
            flops=10 * pairs * HD, bytes_accessed=8 * mine.size, transcendentals=pairs
        ),
    )(place, query, mine, other, low, full, log_total, cosine, sine)


def gather_tp(value, axis):
    value = jnp.concatenate([value, swap(value, "tp", 2)], axis)
    return jnp.concatenate([value, swap(value, "tp", 1)], axis)


def scatter_tp(value):
    half, part = value.shape[0] // 2, value.shape[0] // 4
    other = swap(value[half:], "tp", 1)
    send = (value[part:half].astype(jnp.float32) + other[part:].astype(jnp.float32)).astype(
        jnp.bfloat16
    )
    last = swap(send, "tp", 2)
    return (
        value[:part].astype(jnp.float32)
        + other[:part].astype(jnp.float32)
        + last.astype(jnp.float32)
    )


def in_order(value, me):
    part = value.shape[0] // 4
    return jnp.concatenate(
        [
            lax.dynamic_slice_in_dim(value, reverse_bits(me ^ i, 2) * part, part, 0)
            for i in range(4)
        ],
        0,
    )


def on_device(
    layer_input,
    norm1_gain,
    w_query,
    b_query,
    w_key,
    b_key,
    w_value,
    b_value,
    w_out,
    norm2_gain,
    w_gate,
    w_up,
    w_down,
    doc_ids,
    positions,
    cotangent,
):
    tok_rows, width = layer_input.shape
    shards = lax.axis_size("cp")
    heads = w_query.shape[1] // HD
    kv_heads = w_key.shape[1] // HD
    me = lax.axis_index("cp")
    lane = lax.axis_index("tp")
    core = lane % 2
    kv_index = lane * heads // (H // kv_heads)
    is_key = core == 0

    middle_docs = doc_ids.reshape(shards, tok_rows)[:, HALF]
    my_doc = middle_docs[me]
    start = jnp.sum((middle_docs < my_doc).astype(jnp.int32))
    place = jnp.stack([me, core, lane, start]).astype(jnp.int32)
    my_pos = lax.dynamic_slice_in_dim(positions, me * tok_rows, tok_rows)
    cosine, sine = rope_tables(my_pos, HD)

    inputs = layer_input.astype(jnp.float32)
    scale1 = lax.rsqrt(jnp.mean(inputs * inputs, axis=-1, keepdims=True) + EPSILON)
    normed1 = (inputs * scale1 * norm1_gain).astype(jnp.bfloat16)

    def pair_weight(index):
        head = index * heads // (H // kv_heads)
        source = jnp.where(index % 2 == 0, w_key, w_value)
        return lax.dynamic_slice_in_dim(source, head * HD, HD, 1)

    pair_bias = lax.dynamic_slice_in_dim(jnp.where(is_key, b_key, b_value), kv_index * HD, HD)
    pair_cos = jnp.where(is_key, cosine, 1.0)
    pair_sin = jnp.where(is_key, sine, 0.0)
    pair_pre = matmul(normed1, pair_weight(lane)) + pair_bias
    pair = rotary(pair_pre, pair_cos, pair_sin).astype(jnp.bfloat16)[None]
    bit = shards // 2
    while bit:
        pair = jnp.concatenate([pair, swap(pair, "cp", bit)], 0)
        bit //= 2
    other = swap(pair, "tp", 1)

    q_pre = matmul(normed1, w_query) + b_query
    query = rotary(
        q_pre.reshape(tok_rows, heads, HD), cosine[:, None, :], sine[:, None, :]
    ).astype(jnp.bfloat16)
    query = query.transpose(1, 0, 2)

    attn, attn_full, log_total = attend(place, query, pair, other)
    w_out_all = gather_tp(w_out, 0)
    w_query_all = gather_tp(after(w_query, w_out_all), 1)
    cot_shared = share(place, after(cotangent, other), shards)
    normed1_shared = share(place, after(normed1, other), shards)

    middle = inputs + matmul(gather_tp(attn, 1), w_out_all)
    scale2 = lax.rsqrt(jnp.mean(middle * middle, axis=-1, keepdims=True) + EPSILON)
    normed2 = (middle * scale2 * norm2_gain).astype(jnp.bfloat16)

    units = w_gate.shape[1]
    chunks = pl.cdiv(pl.cdiv(units, TILE), CHUNK_TILES)
    hiddens, grads, total = [], [], None
    for index in range(chunks):
        hidden, grad, total = hidden_chunk(
            place, normed2, cotangent, w_gate, w_up, w_down, total, index
        )
        hiddens.append(hidden)
        grads.append(grad)
    normed2_shared = share(place, normed2, shards)

    downs, gates, ups = [], [], []
    for hidden, grad in zip(hiddens, grads):
        downs.append(weight_grad(place, cot_shared, hidden, shards).T)
        both = weight_grad(place, normed2_shared, grad, shards)
        span = hidden.shape[1]
        for at in range(0, span, TILE):
            size = min(TILE, span - at)
            gates.append(both[:, 2 * at : 2 * at + size])
            ups.append(both[:, 2 * at + TILE : 2 * at + TILE + size])
    grad_w_down = jnp.concatenate(downs, 0)
    grad_w_gate = jnp.concatenate(gates, 1)
    grad_w_up = jnp.concatenate(ups, 1)

    grad_normed2 = in_order(gather_tp(scatter_tp(total).astype(jnp.bfloat16), 0), lane).astype(
        jnp.float32
    )
    weighted2 = grad_normed2 * norm2_gain
    gain2_part = jnp.sum(grad_normed2 * middle * scale2, axis=0)
    grad_middle = (
        cotangent.astype(jnp.float32)
        + scale2 * weighted2
        - middle * scale2**3 * jnp.mean(weighted2 * middle, axis=-1, keepdims=True)
    )
    grad_branch = grad_middle.astype(jnp.bfloat16)
    grad_attn = contract_cols(grad_branch, w_out).astype(jnp.bfloat16)
    grad_query, keep, send = attend_back(
        place, query, pair, other, grad_attn, attn_full, log_total, cosine, sine
    )

    part = tok_rows // 4
    ffn = sum(matmul(h, lax.slice_in_dim(w_down, i * CHUNK_TILES * TILE, i * CHUNK_TILES * TILE + h.shape[1])) for i, h in enumerate(hiddens))
    ffn = after(ffn.astype(jnp.bfloat16), grad_middle)
    ffn_rel = jnp.concatenate(
        [lax.dynamic_slice_in_dim(ffn, (lane ^ far) * part, part, 0) for far in TP_ORDER], 0
    )
    out_part = scatter_tp(ffn_rel) + lax.dynamic_slice_in_dim(middle, lane * part, part, 0)
    output = in_order(gather_tp(out_part.astype(jnp.bfloat16), 0), lane)

    summed = keep.astype(jnp.float32) + swap(send, "tp", 1).astype(jnp.float32)
    bit = 1
    while bit < shards:
        count = summed.shape[0] // 2
        summed = summed[:count] + swap(summed[count:].astype(jnp.bfloat16), "cp", bit).astype(
            jnp.float32
        )
        bit *= 2
    grad_pair = rotary_back(summed[0], pair_cos, pair_sin).astype(jnp.bfloat16)

    branch_shared = share(place, grad_branch, shards)
    grad_w_out = weight_grad(place, branch_shared, attn, shards).T
    grad_w_query = weight_grad(place, normed1_shared, grad_query, shards)
    grad_w_pair = weight_grad(place, normed1_shared, grad_pair, shards)

    pairs_all = gather_tp(grad_pair, 1)
    grad_normed1 = contract_cols(gather_tp(grad_query, 1), w_query_all)
    for i, far in enumerate(TP_ORDER):
        grad_normed1 = grad_normed1 + contract_cols(
            pairs_all[:, i * HD : (i + 1) * HD], pair_weight(lane ^ far)
        )
    weighted1 = grad_normed1 * norm1_gain
    gain1_part = jnp.sum(grad_normed1 * inputs * scale1, axis=0)
    grad_input = (
        grad_middle
        + scale1 * weighted1
        - inputs * scale1**3 * jnp.mean(weighted1 * inputs, axis=-1, keepdims=True)
    ).astype(jnp.bfloat16)

    small = jnp.concatenate(
        [
            gain1_part,
            gain2_part,
            jnp.sum(grad_query.astype(jnp.float32), axis=0),
            jnp.sum(grad_pair.astype(jnp.float32), axis=0),
        ]
    ).reshape(-1, HD)
    bit = 1
    while bit < shards:
        small = small + swap(small, "cp", bit)
        bit *= 2
    wide = width // HD
    gain1_sum = small[:wide].reshape(-1)
    gain2_sum = small[wide : 2 * wide].reshape(-1)
    bias_query = small[2 * wide : 2 * wide + heads].reshape(-1)

    def assemble(parts, axis):
        at = lambda index: lax.dynamic_index_in_dim(parts, reverse_bits(lane ^ index, 2), 0, keepdims=False)
        return (
            jnp.concatenate([at(0), at(2)], axis),
            jnp.concatenate([at(1), at(3)], axis),
        )

    bias_key, bias_value = assemble(gather_tp(small[None, 2 * wide + heads], 0), 0)
    grad_w_key, grad_w_value = assemble(gather_tp(grad_w_pair[None], 0), 1)
    return (
        output,
        grad_input,
        gain1_sum,
        grad_w_query,
        bias_query,
        grad_w_key,
        bias_key,
        grad_w_value,
        bias_value,
        grad_w_out,
        gain2_sum,
        grad_w_gate,
        grad_w_up,
        grad_w_down,
    )


def solution(mesh):
    return jax.shard_map(
        on_device,
        mesh=mesh,
        in_specs=(
            P("cp", None),
            P(),
            P(None, "tp"),
            P("tp"),
            P(),
            P(),
            P(),
            P(),
            P("tp", None),
            P(),
            P(None, "tp"),
            P(None, "tp"),
            P("tp", None),
            P(),
            P(),
            P("cp", None),
        ),
        out_specs=(
            P("cp", None),
            P("cp", None),
            P(),
            P("cp", "tp"),
            P("tp"),
            P("cp", None),
            P(),
            P("cp", None),
            P(),
            P("tp", "cp"),
            P(),
            P("cp", "tp"),
            P("cp", "tp"),
            P("tp", "cp"),
        ),
        check_vma=False,
    )
```

time: 1200 us -> 629 us (0.52)
  waiting for transfers between devices: 824 us -> 239 us
  matrix products: 172 us -> 33.3 us
  Pallas kernels: 0 us -> 132 us
  starting transfers between devices: 1.6 us -> 84.7 us
  blocking collectives: 35.8 us -> 0 us
  between operations: 15.3 us -> 1.87 us
    reduce_scatter x8 -> x0, waiting for transfers between devices: 624 us -> none  [the longest x1 130 us: on_device(): lax.psum_scatter(grad_w_gate.astype(jnp.bfloat16), 'cp', scatter_dimensio...]
    ppermute x0 -> x68, waiting for transfers between devices: none -> 239 us  [swap(): return lax.ppermute(value, axis, [(i, i ^ bit) for i in range(size)])]
    psum x3 -> x0, waiting for transfers between devices: 154 us -> none  [the longest x1 70.9 us: on_device(): lax.psum(matmul(hidden, w_down).astype(jnp.bfloat16), 'tp')]
    pallas_call x0 -> x18, Pallas kernels: none -> 132 us  [the longest x3 51.3 us: hidden_chunk(): pl.pallas_call(functools.partial(hidden_kernel, first, last, offset, unit...]
    ppermute x0 -> x68, starting transfers between devices: none -> 84.7 us  [swap(): return lax.ppermute(value, axis, [(i, i ^ bit) for i in range(size)])]
    dot_general x19 -> x6, matrix products: 67.3 us -> 13.4 us  [contract_cols(): lax.dot_general(left, right, (((1,), (1,)), ((), ())), preferred_element_...]
    dot_general x15 -> x0, matrix products: 46.7 us -> none  [contract_rows(): lax.dot_general(left, right, (((0,), (0,)), ((), ())), preferred_element_...]
    all_gather x1 -> x0, waiting for transfers between devices: 46.2 us -> none  [on_device(): lax.all_gather(kv_mine, 'cp', axis=0, tiled=True)]
  transfers between devices with their start and end apart: 12 -> 68, of which waited for: 12 -> 29; matrix products, arithmetic and copies ran while one was open for 7% -> 25% of each run, Pallas kernels for 0% -> 21%
where the time goes in v1:
time: 629 us; the launch traced here: 622 us
  waiting for transfers between devices  239 us (38%)
  Pallas kernels  132 us (21%)
  starting transfers between devices  84.7 us (13%)
  other arithmetic  69 us (11%)
  local copies, waits for them, and re-layouts  62.2 us (10%)
  matrix products  33.3 us (5%)
    ppermute x68, waiting for transfers between devices, swap(): return lax.ppermute(value, axis, [(i, i ^ bit) for i in range(size)])  239 us
    ppermute x68, starting transfers between devices, swap(): return lax.ppermute(value, axis, [(i, i ^ bit) for i in range(size)])  84.7 us
    pallas_call x3, Pallas kernels, hidden_chunk(): pl.pallas_call(functools.partial(hidden_kernel, first, last, offset, unit...  51.3 us
    pallas_call x9, Pallas kernels, weigh(): pl.pallas_call(weigh_kernel, grid=(pl.cdiv(width, tile),), out_shape=(jax...  40.9 us
    unnamed x156, local copies, waits for them, and re-layouts  38.5 us
    dot_general x6, matrix products, matmul(): return jnp.dot(left, right, preferred_element_type=jnp.float32)  19.9 us
    pallas_call x1, Pallas kernels, attend_back(): pl.pallas_call(functools.partial(attend_back_kernel, shards), out_shape=(...  14.5 us
    pallas_call x1, Pallas kernels, attend(): pl.pallas_call(functools.partial(attend_kernel, shards), out_shape=(jax.S...  13.6 us
  transfers between devices with their start and end apart: 68, of which 29 were waited for; matrix products, arithmetic and copies ran while one was open for 25% of the time, Pallas kernels for 21%

profile of v1, /device:TPU:0, one launch (start us, length us, event | category | flops | bytes accessed | tf_op | source)
XLA Modules:
  0.0 622.3 jit_solution(14813867645427982207)
XLA Ops:
  17.7 6.1 collective-permute-done
  24.6 6.5 %collective-permute-done.1 = bf16[2,512,128]{2,1,0:T(8,128)(2,1)S(1)} collective-permute-done((bf16[2,512,128]{2,1,0:T(8,128)(2,1)S(1)}, bf16[2,512,128]{2,1,0:T(8,128)(2,1)S(1)}, u32[]{:S(2)}, u32[]{:S(2)}) %collective-permute-start.1) | collective-permute-done | bytes 262176 | tf_op jit(solution)/shard_map/ppermute | solution.py:62
  37.0 8.1 %collective-permute-done.2 = bf16[4,512,128]{2,1,0:T(8,128)(2,1)} collective-permute-done((bf16[4,512,128]{2,1,0:T(8,128)(2,1)}, bf16[4,512,128]{2,1,0:T(8,128)(2,1)}, u32[]{:S(2)}, u32[]{:S(2)}) %collective-permute-start.2) | collective-permute-done | bytes 524320 | tf_op jit(solution)/shard_map/ppermute | solution.py:62
  54.1 13.6 %shard_map.263 = (bf16[512,384]{1,0:T(8,128)(2,1)}, f32[3,512,128]{2,1,0:T(8,128)}, f32[3,512,128]{2,1,0:T(8,128)}) custom-call(s32[4]{0:T(128)} %pad_add_fusion.place_ref.refs_0_, bf16[3,512,128]{2,1,0:T(8,128)(2,1)} %fusion.51.q_ref, bf16[8,512,128]{2,1,0:T(8,128)(2,1)} %pad_maximum_fusion.7.mine_ref, bf16[8,512,128]{2,1,0:T(8,128)(2,1)} %collective-permute-done.3.other_ref), custom_call_target="tpu_custom_call" | custom-call | flops 1207959552 | bytes 2097152 | tf_op jit(solution)/shard_map/pallas_call | solution.py:354
  72.8 6.6 %collective-permute-done.4 = bf16[512,384]{1,0:T(8,128)(2,1)S(1)} collective-permute-done((bf16[512,384]{1,0:T(8,128)(2,1)}, bf16[512,384]{1,0:T(8,128)(2,1)S(1)}, u32[]{:S(2)}, u32[]{:S(2)}) %collective-permute-start.4) | collective-permute-done | bytes 393248 | tf_op jit(solution)/shard_map/ppermute | solution.py:62
  80.7 10.2 %copy.92.refs_3_ = bf16[1536,2240]{1,0:T(8,128)(2,1)} copy(bf16[1536,2240]{0,1:T(8,128)(2,1)} %param.26) | data formatting | bytes 13762560 | tf_op args[10]
  90.9 9.7 %copy.93.refs_4_ = bf16[1536,2240]{1,0:T(8,128)(2,1)} copy(bf16[1536,2240]{0,1:T(8,128)(2,1)} %param.27) | data formatting | bytes 13762560 | tf_op args[11]
  116.7 16.7 %shard_map.264 = (bf16[512,768]{1,0:T(8,128)(2,1)}, bf16[512,1536]{1,0:T(8,128)(2,1)}, f32[512,1536]{1,0:T(8,128)}) custom-call(s32[4]{0:T(128)} %pad_add_fusion.place_ref.refs_0_, bf16[512,1536]{1,0:T(8,128)(2,1)} %multiply_convert_fusion.refs_1_.rows_ref, bf16[512,1536]{1,0:T(8,128)(2,1)} %rows_ref, bf16[1536,2240]{1,0:T(8,128)(2,1)} %copy.92.refs_3_, ...), custom_call_target="tpu_custom_call" | custom-call | flops 6039797760 | bytes 16515072 | tf_op jit(solution)/shard_map/pallas_call | solution.py:257
  134.9 17.5 %shard_map.265 = (bf16[512,768]{1,0:T(8,128)(2,1)}, bf16[512,1536]{1,0:T(8,128)(2,1)}, f32[512,1536]{1,0:T(8,128)}) custom-call(s32[4]{0:T(128)} %pad_add_fusion.place_ref.refs_0_, bf16[512,1536]{1,0:T(8,128)(2,1)} %multiply_convert_fusion.refs_1_.rows_ref, bf16[512,1536]{1,0:T(8,128)(2,1)} %rows_ref, bf16[1536,2240]{1,0:T(8,128)(2,1)} %copy.92.refs_3_, ...), custom_call_target="tpu_custom_call" | custom-call | flops 6039797760 | bytes 16515072 | tf_op jit(solution)/shard_map/pallas_call | solution.py:257
  153.0 17.2 %shard_map.266 = (bf16[512,704]{1,0:T(8,128)(2,1)}, bf16[512,1472]{1,0:T(8,128)(2,1)}, bf16[512,1536]{1,0:T(8,128)(2,1)}) custom-call(s32[4]{0:T(128)} %pad_add_fusion.place_ref.refs_0_, bf16[512,1536]{1,0:T(8,128)(2,1)} %multiply_convert_fusion.refs_1_.rows_ref, bf16[512,1536]{1,0:T(8,128)(2,1)} %rows_ref, bf16[1536,2240]{1,0:T(8,128)(2,1)} %copy.92.refs_3_, ...), custom_call_target="tpu_custom_call" | custom-call | flops 5536481280 | bytes 15925248 | tf_op jit(solution)/shard_map/pallas_call | solution.py:257
  229.3 18.4 %collective-permute-done.46.near_ref = bf16[384,512]{1,0:T(8,128)(2,1)S(1)} collective-permute-done((bf16[384,512]{1,0:T(8,128)(2,1)}, bf16[384,512]{1,0:T(8,128)(2,1)S(1)}, u32[]{:S(2)}, u32[]{:S(2)}) %collective-permute-start.46) | collective-permute-done | bytes 393248 | tf_op jit(solution)/shard_map/ppermute | solution.py:62
  275.8 7.0 %collective-permute-start.67 = (bf16[192,704]{1,0:T(8,128)(2,1)}, bf16[192,704]{1,0:T(8,128)(2,1)}, u32[]{:S(2)}, u32[]{:S(2)}) collective-permute-start(bf16[192,704]{1,0:T(8,128)(2,1)} %add_convert_fusion.7), channel_id=1, source_target_pairs={{0,16},{4,20},{8,24},{12,28},{16,0},{20,4},{24,8},{28,12},{1,17},{... | collective-permute-start | bytes 811016 | tf_op jit(solution)/shard_map/ppermute | solution.py:62
  287.3 33.6 %collective-permute-done.29.near_ref = bf16[384,512]{1,0:T(8,128)(2,1)} collective-permute-done((bf16[384,512]{1,0:T(8,128)(2,1)}, bf16[384,512]{1,0:T(8,128)(2,1)}, u32[]{:S(2)}, u32[]{:S(2)}) %collective-permute-start.29) | collective-permute-done | bytes 393248 | tf_op jit(solution)/shard_map/ppermute | solution.py:62
  322.4 5.9 shard_map.276
  333.3 8.4 %collective-permute-start.61 = (bf16[192,768]{1,0:T(8,128)(2,1)}, bf16[192,768]{1,0:T(8,128)(2,1)S(1)}, u32[]{:S(2)}, u32[]{:S(2)}) collective-permute-start(bf16[192,768]{1,0:T(8,128)(2,1)} %add_convert_fusion.9), channel_id=1, source_target_pairs={{0,16},{4,20},{8,24},{12,28},{16,0},{20,4},{24,8},{28,12},{1,17},{... | collective-permute-start | bytes 884744 | tf_op jit(solution)/shard_map/ppermute | solution.py:62
  382.9 14.5 %shard_map.267 = (bf16[512,384]{1,0:T(8,128)(2,1)}, bf16[8,512,128]{2,1,0:T(8,128)(2,1)}, bf16[8,512,128]{2,1,0:T(8,128)(2,1)}) custom-call(s32[4]{0:T(128)} %pad_add_fusion.place_ref.refs_0_, bf16[3,512,128]{2,1,0:T(8,128)(2,1)} %fusion.51.q_ref, bf16[8,512,128]{2,1,0:T(8,128)(2,1)} %pad_maximum_fusion.7.mine_ref, ...), custom_call_target="tpu_custom_call" | custom-call | flops 2013265920 | bytes 4194304 | tf_op jit(solution)/shard_map/pallas_call | solution.py:423
  409.4 6.8 %collective-permute-done.52 = bf16[384,1536]{1,0:T(8,128)(2,1)} collective-permute-done((bf16[384,1536]{1,0:T(8,128)(2,1)}, bf16[384,1536]{1,0:T(8,128)(2,1)}, u32[]{:S(2)}, u32[]{:S(2)}) %collective-permute-start.52) | collective-permute-done | bytes 1179680 | tf_op jit(solution)/shard_map/ppermute | solution.py:62
  420.3 7.9 %collective-permute-done.31.theirs_ref = bf16[512,384]{1,0:T(8,128)(2,1)S(1)} collective-permute-done((bf16[512,384]{1,0:T(8,128)(2,1)S(1)}, bf16[512,384]{1,0:T(8,128)(2,1)S(1)}, u32[]{:S(2)}, u32[]{:S(2)}) %collective-permute-start.31) | collective-permute-done | bytes 393248 | tf_op jit(solution)/shard_map/ppermute | solution.py:62
  432.4 8.4 %collective-permute-done.49 = bf16[384,1536]{1,0:T(8,128)(2,1)} collective-permute-done((bf16[384,1536]{1,0:T(8,128)(2,1)}, bf16[384,1536]{1,0:T(8,128)(2,1)}, u32[]{:S(2)}, u32[]{:S(2)}) %collective-permute-start.49) | collective-permute-done | bytes 1179680 | tf_op jit(solution)/shard_map/ppermute | solution.py:62
  444.7 6.5 %collective-permute-start.56 = (bf16[192,1472]{1,0:T(8,128)(2,1)}, bf16[192,1472]{1,0:T(8,128)(2,1)}, u32[]{:S(2)}, u32[]{:S(2)}) collective-permute-start(bf16[192,1472]{1,0:T(8,128)(2,1)} %add_convert_fusion), channel_id=1, source_target_pairs={{0,16},{4,20},{8,24},{12,28},{16,0},{20,4},{24,8},{28,12},{1,17},{... | collective-permute-start | bytes 1695752 | tf_op jit(solution)/shard_map/ppermute | solution.py:62
  462.4 35.0 %collective-permute-done.33 = bf16[192,384]{1,0:T(8,128)(2,1)} collective-permute-done((bf16[192,384]{1,0:T(8,128)(2,1)S(1)}, bf16[192,384]{1,0:T(8,128)(2,1)}, u32[]{:S(2)}, u32[]{:S(2)}) %collective-permute-start.33) | collective-permute-done | bytes 147488 | tf_op jit(solution)/shard_map/ppermute | solution.py:62
  500.5 34.5 %collective-permute-done.50 = bf16[192,1536]{1,0:T(8,128)(2,1)S(1)} collective-permute-done((bf16[192,1536]{1,0:T(8,128)(2,1)}, bf16[192,1536]{1,0:T(8,128)(2,1)S(1)}, u32[]{:S(2)}, u32[]{:S(2)}) %collective-permute-start.50) | collective-permute-done | bytes 589856 | tf_op jit(solution)/shard_map/ppermute | solution.py:62
  545.0 9.9 %collective-permute-done.21 = bf16[4,512,128]{2,1,0:T(8,128)(2,1)S(1)} collective-permute-done((bf16[4,512,128]{2,1,0:T(8,128)(2,1)S(1)}, bf16[4,512,128]{2,1,0:T(8,128)(2,1)S(1)}, u32[]{:S(2)}, u32[]{:S(2)}) %collective-permute-start.21) | collective-permute-done | bytes 524320 | tf_op jit(solution)/shard_map/ppermute | solution.py:62
  596.9 6.7 %fusion.30 = (f32[1536]{0:T(1024)S(1)}, f32[512]{0:T(512)S(1)}, f32[512,1536]{1,0:T(8,128)S(1)}) fusion(bf16[512,1536]{1,0:T(8,128)(2,1)S(1)} %copy-done.4, f32[512]{0:T(512)S(1)} %copy-done.61, f32[1536]{0:T(1024)S(1)} %copy-done.57, f32[512,1536]{1,0:T(8,128)} %fusion.52, f32[512,1536]{1,0:T(8,128)S(1)} %fusion.54, f32[512,1536]{1,0:T(8,128)S(1)} %fusion.56, ...), kind=kOutput, calls=%fused_computation.34 | convolution fusion | flops 2443442176 | bytes 23609344 | tf_op jit(solution)/shard_map/dot_general | solution.py:35
  (399 shorter events, 304.8 us)
Async XLA Ops:
  37.0 69.4 %collective-permute-start.7 = (bf16[768,1536]{1,0:T(8,128)(2,1)}, bf16[768,1536]{1,0:T(8,128)(2,1)}, u32[]{:S(2)}, u32[]{:S(2)}) collective-permute-start(bf16[768,1536]{1,0:T(8,128)(2,1)} %pad_maximum_fusion), channel_id=1, source_target_pairs={{0,1},{1,0},{2,3},{3,2},{4,5},{5,4},{6,7},{7,6},{8,9},{9,8},{10,11... | collective-permute-start | bytes 7077896 | tf_op jit(solution)/shard_map/ppermute | solution.py:62
  105.9 97.1 %collective-permute-start.58 = (bf16[384,512]{1,0:T(8,128)(2,1)}, bf16[384,512]{1,0:T(8,128)(2,1)}, u32[]{:S(2)}, u32[]{:S(2)}) collective-permute-start(bf16[384,512]{1,0:T(8,128)(2,1)} %collective-permute-done.57.near_ref), channel_id=1, source_target_pairs={{0,1},{1,0},{2,3},{3,2},{4,5},{5,4},{6,7},{7,6},{8,9},{9,8},{10,11... | collective-permute-start | bytes 1179656 | tf_op jit(solution)/shard_map/ppermute | solution.py:62
  133.3 77.9 %collective-permute-start.59 = (bf16[512,768]{1,0:T(8,128)(2,1)}, bf16[512,768]{1,0:T(8,128)(2,1)}, u32[]{:S(2)}, u32[]{:S(2)}) collective-permute-start(bf16[512,768]{1,0:T(8,128)(2,1)} %get-tuple-element.60.mine_ref), channel_id=1, source_target_pairs={{0,4},{4,0},{8,12},{12,8},{16,20},{20,16},{24,28},{28,24},{1,5},{5... | collective-permute-start | bytes 2359304 | tf_op jit(solution)/shard_map/ppermute | solution.py:62
  152.5 63.9 %collective-permute-start.62 = (bf16[512,768]{1,0:T(8,128)(2,1)}, bf16[512,768]{1,0:T(8,128)(2,1)}, u32[]{:S(2)}, u32[]{:S(2)}) collective-permute-start(bf16[512,768]{1,0:T(8,128)(2,1)} %get-tuple-element.62.mine_ref), channel_id=1, source_target_pairs={{0,4},{4,0},{8,12},{12,8},{16,20},{20,16},{24,28},{28,24},{1,5},{5... | collective-permute-start | bytes 2359304 | tf_op jit(solution)/shard_map/ppermute | solution.py:62
  181.8 70.3 %collective-permute-start.18 = (bf16[1536,384]{1,0:T(8,128)(2,1)}, bf16[1536,384]{1,0:T(8,128)(2,1)}, u32[]{:S(2)}, u32[]{:S(2)}) collective-permute-start(bf16[1536,384]{1,0:T(8,128)(2,1)} %param.18), channel_id=1, source_target_pairs={{0,2},{1,3},{2,0},{3,1},{4,6},{5,7},{6,4},{7,5},{8,10},{9,11},{10,... | collective-permute-start | bytes 3538952 | tf_op jit(solution)/shard_map/ppermute | solution.py:62
  203.0 72.8 %collective-permute-start.54 = (bf16[512,1472]{0,1:T(8,128)(2,1)}, bf16[512,1472]{0,1:T(8,128)(2,1)}, u32[]{:S(2)}, u32[]{:S(2)}) collective-permute-start(bf16[512,1472]{0,1:T(8,128)(2,1)} %copy.98), channel_id=1, source_target_pairs={{0,4},{4,0},{8,12},{12,8},{16,20},{20,16},{24,28},{28,24},{1,5},{5... | collective-permute-start | bytes 4521992 | tf_op jit(solution)/shard_map/ppermute | solution.py:62
  216.4 116.9 %collective-permute-start.51 = (bf16[512,1536]{1,0:T(8,128)(2,1)}, bf16[512,1536]{1,0:T(8,128)(2,1)}, u32[]{:S(2)}, u32[]{:S(2)}) collective-permute-start(bf16[512,1536]{1,0:T(8,128)(2,1)} %get-tuple-element.89.mine_ref), channel_id=1, source_target_pairs={{0,4},{4,0},{8,12},{12,8},{16,20},{20,16},{24,28},{28,24},{1,5},{5... | collective-permute-start | bytes 4718600 | tf_op jit(solution)/shard_map/ppermute | solution.py:62
  255.4 92.2 %collective-permute-start.48 = (bf16[512,1536]{1,0:T(8,128)(2,1)}, bf16[512,1536]{1,0:T(8,128)(2,1)}, u32[]{:S(2)}, u32[]{:S(2)}) collective-permute-start(bf16[512,1536]{1,0:T(8,128)(2,1)} %get-tuple-element.86.mine_ref), channel_id=1, source_target_pairs={{0,4},{4,0},{8,12},{12,8},{16,20},{20,16},{24,28},{28,24},{1,5},{5... | collective-permute-start | bytes 4718600 | tf_op jit(solution)/shard_map/ppermute | solution.py:62
  266.7 54.2 %collective-permute-start.29 = (bf16[384,512]{1,0:T(8,128)(2,1)}, bf16[384,512]{1,0:T(8,128)(2,1)}, u32[]{:S(2)}, u32[]{:S(2)}) collective-permute-start(bf16[384,512]{1,0:T(8,128)(2,1)} %get-tuple-element.75), channel_id=1, source_target_pairs={{0,4},{4,0},{8,12},{12,8},{16,20},{20,16},{24,28},{28,24},{1,5},{5... | collective-permute-start | bytes 1179656 | tf_op jit(solution)/shard_map/ppermute | solution.py:62
  274.0 48.5 %collective-permute-start.47 = (bf16[384,512]{1,0:T(8,128)(2,1)}, bf16[384,512]{1,0:T(8,128)(2,1)}, u32[]{:S(2)}, u32[]{:S(2)}) collective-permute-start(bf16[384,512]{1,0:T(8,128)(2,1)} %copy-done.66), channel_id=1, source_target_pairs={{0,1},{1,0},{2,3},{3,2},{4,5},{5,4},{6,7},{7,6},{8,9},{9,8},{10,11... | collective-permute-start | bytes 1179656 | tf_op jit(solution)/shard_map/ppermute | solution.py:62
  275.8 54.9 %collective-permute-start.67 = (bf16[192,704]{1,0:T(8,128)(2,1)}, bf16[192,704]{1,0:T(8,128)(2,1)}, u32[]{:S(2)}, u32[]{:S(2)}) collective-permute-start(bf16[192,704]{1,0:T(8,128)(2,1)} %add_convert_fusion.7), channel_id=1, source_target_pairs={{0,16},{4,20},{8,24},{12,28},{16,0},{20,4},{24,8},{28,12},{1,17},{... | collective-permute-start | bytes 811016 | tf_op jit(solution)/shard_map/ppermute | solution.py:62
  320.9 136.7 %collective-permute-start.43 = (bf16[512,384]{1,0:T(8,128)(2,1)}, bf16[512,384]{1,0:T(8,128)(2,1)}, u32[]{:S(2)}, u32[]{:S(2)}) collective-permute-start(bf16[512,384]{1,0:T(8,128)(2,1)} %get-tuple-element.59.mine_ref), channel_id=1, source_target_pairs={{0,4},{4,0},{8,12},{12,8},{16,20},{20,16},{24,28},{28,24},{1,5},{5... | collective-permute-start | bytes 1179656 | tf_op jit(solution)/shard_map/ppermute | solution.py:62
  322.4 96.5 %collective-permute-start.30 = (bf16[384,512]{1,0:T(8,128)(2,1)}, bf16[384,512]{1,0:T(8,128)(2,1)}, u32[]{:S(2)}, u32[]{:S(2)}) collective-permute-start(bf16[384,512]{1,0:T(8,128)(2,1)} %collective-permute-done.29.near_ref), channel_id=1, source_target_pairs={{0,1},{1,0},{2,3},{3,2},{4,5},{5,4},{6,7},{7,6},{8,9},{9,8},{10,11... | collective-permute-start | bytes 1179656 | tf_op jit(solution)/shard_map/ppermute | solution.py:62
  353.7 46.8 %collective-permute-start.55 = (bf16[384,1472]{0,1:T(8,128)(2,1)S(1)}, bf16[384,1472]{0,1:T(8,128)(2,1)S(1)}, u32[]{:S(2)}, u32[]{:S(2)}) collective-permute-start(bf16[384,1472]{0,1:T(8,128)(2,1)S(1)} %copy-done.26), channel_id=1, source_target_pairs={{0,8},{4,12},{8,0},{12,4},{16,24},{20,28},{24,16},{28,20},{1,9},{5... | collective-permute-start | bytes 3391496 | tf_op jit(solution)/shard_map/ppermute | solution.py:62
  368.5 47.7 %collective-permute-start.52 = (bf16[384,1536]{1,0:T(8,128)(2,1)}, bf16[384,1536]{1,0:T(8,128)(2,1)}, u32[]{:S(2)}, u32[]{:S(2)}) collective-permute-start(bf16[384,1536]{1,0:T(8,128)(2,1)} %get-tuple-element.91), channel_id=1, source_target_pairs={{0,8},{4,12},{8,0},{12,4},{16,24},{20,28},{24,16},{28,20},{1,9},{5... | collective-permute-start | bytes 3538952 | tf_op jit(solution)/shard_map/ppermute | solution.py:62
  371.6 69.2 %collective-permute-start.49 = (bf16[384,1536]{1,0:T(8,128)(2,1)}, bf16[384,1536]{1,0:T(8,128)(2,1)}, u32[]{:S(2)}, u32[]{:S(2)}) collective-permute-start(bf16[384,1536]{1,0:T(8,128)(2,1)} %get-tuple-element.88), channel_id=1, source_target_pairs={{0,8},{4,12},{8,0},{12,4},{16,24},{20,28},{24,16},{28,20},{1,9},{5... | collective-permute-start | bytes 3538952 | tf_op jit(solution)/shard_map/ppermute | solution.py:62
  400.5 42.3 %collective-permute-start.16 = (bf16[512,384]{1,0:T(8,128)(2,1)S(1)}, bf16[512,384]{1,0:T(8,128)(2,1)}, u32[]{:S(2)}, u32[]{:S(2)}) collective-permute-start(bf16[512,384]{1,0:T(8,128)(2,1)S(1)} %copy-done.12), channel_id=1, source_target_pairs={{0,2},{1,3},{2,0},{3,1},{4,6},{5,7},{6,4},{7,5},{8,10},{9,11},{10,... | collective-permute-start | bytes 1179656 | tf_op jit(solution)/shard_map/ppermute | solution.py:62
  442.8 154.0 %collective-permute-start.19 = (bf16[1536,768]{1,0:T(8,128)(2,1)}, bf16[1536,768]{1,0:T(8,128)(2,1)}, u32[]{:S(2)}, u32[]{:S(2)}) collective-permute-start(bf16[1536,768]{1,0:T(8,128)(2,1)} %pad_maximum_fusion.1), channel_id=1, source_target_pairs={{0,1},{1,0},{2,3},{3,2},{4,5},{5,4},{6,7},{7,6},{8,9},{9,8},{10,11... | collective-permute-start | bytes 7077896 | tf_op jit(solution)/shard_map/ppermute | solution.py:62
  444.7 54.5 %collective-permute-start.56 = (bf16[192,1472]{1,0:T(8,128)(2,1)}, bf16[192,1472]{1,0:T(8,128)(2,1)}, u32[]{:S(2)}, u32[]{:S(2)}) collective-permute-start(bf16[192,1472]{1,0:T(8,128)(2,1)} %add_convert_fusion), channel_id=1, source_target_pairs={{0,16},{4,20},{8,24},{12,28},{16,0},{20,4},{24,8},{28,12},{1,17},{... | collective-permute-start | bytes 1695752 | tf_op jit(solution)/shard_map/ppermute | solution.py:62
  451.6 45.8 %collective-permute-start.33 = (bf16[192,384]{1,0:T(8,128)(2,1)S(1)}, bf16[192,384]{1,0:T(8,128)(2,1)}, u32[]{:S(2)}, u32[]{:S(2)}) collective-permute-start(bf16[192,384]{1,0:T(8,128)(2,1)S(1)} %add_convert_fusion.11), channel_id=1, source_target_pairs={{0,16},{4,20},{8,24},{12,28},{16,0},{20,4},{24,8},{28,12},{1,17},{... | collective-permute-start | bytes 442376 | tf_op jit(solution)/shard_map/ppermute | solution.py:62
  457.6 81.2 %collective-permute-start.20 = (bf16[8,512,128]{2,1,0:T(8,128)(2,1)}, bf16[8,512,128]{2,1,0:T(8,128)(2,1)}, u32[]{:S(2)}, u32[]{:S(2)}) collective-permute-start(bf16[8,512,128]{2,1,0:T(8,128)(2,1)} %get-tuple-element.72), channel_id=1, source_target_pairs={{0,1},{1,0},{2,3},{3,2},{4,5},{5,4},{6,7},{7,6},{8,9},{9,8},{10,11... | collective-permute-start | bytes 3145736 | tf_op jit(solution)/shard_map/ppermute | solution.py:62
  457.9 78.6 %collective-permute-start.53 = (bf16[192,1536]{1,0:T(8,128)(2,1)}, bf16[192,1536]{1,0:T(8,128)(2,1)}, u32[]{:S(2)}, u32[]{:S(2)}) collective-permute-start(bf16[192,1536]{1,0:T(8,128)(2,1)} %add_convert_fusion.1), channel_id=1, source_target_pairs={{0,16},{4,20},{8,24},{12,28},{16,0},{20,4},{24,8},{28,12},{1,17},{... | collective-permute-start | bytes 1769480 | tf_op jit(solution)/shard_map/ppermute | solution.py:62
  497.4 37.6 %collective-permute-start.50 = (bf16[192,1536]{1,0:T(8,128)(2,1)}, bf16[192,1536]{1,0:T(8,128)(2,1)S(1)}, u32[]{:S(2)}, u32[]{:S(2)}) collective-permute-start(bf16[192,1536]{1,0:T(8,128)(2,1)} %add_convert_fusion.2), channel_id=1, source_target_pairs={{0,16},{4,20},{8,24},{12,28},{16,0},{20,4},{24,8},{28,12},{1,17},{... | collective-permute-start | bytes 1769480 | tf_op jit(solution)/shard_map/ppermute | solution.py:62
  499.2 97.6 %collective-permute-start.17 = (bf16[512,768]{1,0:T(8,128)(2,1)}, bf16[512,768]{1,0:T(8,128)(2,1)}, u32[]{:S(2)}, u32[]{:S(2)}) collective-permute-start(bf16[512,768]{1,0:T(8,128)(2,1)} %pad_maximum_fusion.12), channel_id=1, source_target_pairs={{0,1},{1,0},{2,3},{3,2},{4,5},{5,4},{6,7},{7,6},{8,9},{9,8},{10,11... | collective-permute-start | bytes 2359304 | tf_op jit(solution)/shard_map/ppermute | solution.py:62
  (114 other events, 1394.2 us)

commit v2 on v1

--- a/solution.py
+++ b/solution.py
@@ -357,10 +357,10 @@
             jax.ShapeDtypeStruct((tok_rows, heads * HD), jnp.bfloat16),
             jax.ShapeDtypeStruct((heads, tok_rows, HD), jnp.float32),
             jax.ShapeDtypeStruct((heads, tok_rows, HD), jnp.float32),
+            jax.ShapeDtypeStruct((2,) + mine.shape, jnp.bfloat16),
         ),
         in_specs=[SMEM, VMEM, VMEM, VMEM],
-        out_specs=(VMEM, VMEM, VMEM),
-        scratch_shapes=[pltpu.VMEM((2,) + mine.shape, jnp.bfloat16)],
+        out_specs=(VMEM, VMEM, VMEM, VMEM),
         compiler_params=params(),
         cost_estimate=pl.CostEstimate(
             flops=6 * pairs * HD, bytes_accessed=4 * mine.size, transcendentals=pairs
@@ -369,12 +369,10 @@
 
 
 def attend_back_kernel(
-    shards, place_ref, q_ref, mine_ref, other_ref, low_ref, full_ref, log_ref, cos_ref, sin_ref,
-    query_ref, keep_ref, send_ref, pair, grads,
+    shards, place_ref, q_ref, pair, low_ref, full_ref, log_ref, cos_ref, sin_ref,
+    query_ref, keep_ref, send_ref, grads,
 ):
     core = place_ref[1]
-    pair[core] = mine_ref[...]
-    pair[1 - core] = other_ref[...]
     grads[...] = jnp.zeros_like(grads)
     heads, tok_rows = q_ref.shape[0], q_ref.shape[1]
     scale = HD**-0.5
@@ -416,28 +414,25 @@
     send_ref[...] = (grads[1 - core] * jnp.where(is_key, 1.0, scale)).astype(jnp.bfloat16)
 
 
-def attend_back(place, query, mine, other, low, full, log_total, cosine, sine):
+def attend_back(place, query, pair, low, full, log_total, cosine, sine):
     heads, tok_rows, _ = query.shape
-    shards = mine.shape[0]
+    shards = pair.shape[1]
     pairs = heads * tok_rows * tok_rows * shards // 4
     return pl.pallas_call(
         functools.partial(attend_back_kernel, shards),
         out_shape=(
             jax.ShapeDtypeStruct((tok_rows, heads * HD), jnp.bfloat16),
-            jax.ShapeDtypeStruct(mine.shape, jnp.bfloat16),
-            jax.ShapeDtypeStruct(mine.shape, jnp.bfloat16),
+            jax.ShapeDtypeStruct(pair.shape[1:], jnp.bfloat16),
+            jax.ShapeDtypeStruct(pair.shape[1:], jnp.bfloat16),
         ),
-        in_specs=[SMEM] + [VMEM] * 8,
+        in_specs=[SMEM] + [VMEM] * 7,
         out_specs=(VMEM, VMEM, VMEM),
-        scratch_shapes=[
-            pltpu.VMEM((2,) + mine.shape, jnp.bfloat16),
-            pltpu.VMEM((2,) + mine.shape, jnp.float32),
-        ],
+        scratch_shapes=[pltpu.VMEM(pair.shape, jnp.float32)],
         compiler_params=params(),
         cost_estimate=pl.CostEstimate(
-            flops=10 * pairs * HD, bytes_accessed=8 * mine.size, transcendentals=pairs
+            flops=10 * pairs * HD, bytes_accessed=4 * pair.size, transcendentals=pairs
         ),
-    )(place, query, mine, other, low, full, log_total, cosine, sine)
+    )(place, query, pair, low, full, log_total, cosine, sine)
 
 
 def gather_tp(value, axis):
@@ -468,6 +463,810 @@
         ],
         0,
     )
+
+
+UNITS = 256
+TOK = 512
+
+
+def back_kernel(width, units, *refs):
+    (
+        docs_ref, gain_ref, attn_hbm, full_hbm, log_hbm, q_hbm, pair_hbm, x_hbm, cot_hbm,
+        cot_turned_hbm, n1_turned_hbm, cos_hbm, sin_hbm, wo_hbm, wg_hbm, wu_hbm, wd_hbm,
+        tiles_out, wo_out, wq_out, wp_out, gain_out, output_out, middle_out, query_out, pair_out,
+        own_hbm, far_hbm, near1_hbm, near2_hbm,
+        attn_all, attn_far, query_far, pair_far, middle, acc, turned,
+        own_a, far_a, stage, far_stage, part_s, part_k, part_f, near1, part_s2, near2, final,
+        rel, core_in, lane_send, lane_in, grad_full, out_core_in, out_lane_in,
+        kv_send, kv_in, grad_query, grad_pair, small_s, small_in, small_s2, small_in2,
+        send_sem, recv_sem, local_sem, weight_sem,
+    ) = refs
+    me = lax.axis_index("cp")
+    lane = lax.axis_index("tp")
+    b0, b1, b2 = me % 2, (me // 2) % 2, me // 4
+    core, high = lane % 2, lane // 2
+    x_to = {"cp": me + 1 - 2 * b0}
+    z1_to = {"cp": me + 2 - 4 * b1}
+    z2_to = {"cp": me + 4 - 8 * b2}
+    c_to = {"tp": lane + 1 - 2 * core}
+    y_to = {"tp": lane + 2 - 4 * high}
+    lane_c, lane_y = lane + 1 - 2 * core, lane + 2 - 4 * high
+    lane_cy = 3 - lane
+    tiles = pl.cdiv(units, UNITS)
+    rest = units - (tiles - 1) * UNITS
+    block = width // 8
+    half = width // 4
+    quarter = TOK // 4
+    scale = HD**-0.5
+    factor = scale * LOG2E
+    used = {"remote": 0, "local": 0}
+
+    def remote(src, dst, to, count=1):
+        index = used["remote"]
+        used["remote"] += 1
+        return pltpu.make_async_remote_copy(
+            src_ref=src, dst_ref=dst, send_sem=send_sem.at[index], recv_sem=recv_sem.at[index],
+            device_id=to, device_id_type=pl.DeviceIdType.MESH,
+        )
+
+    def local(src, dst):
+        index = used["local"]
+        used["local"] += 1
+        return pltpu.make_async_copy(src, dst, local_sem.at[index])
+
+    def started(*copies):
+        for copy in copies:
+            copy.start()
+        return copies[0] if len(copies) == 1 else copies
+
+    def row_block(side, h, i):
+        mine = (b0 + side) % 2 + 2 * ((b1 + h) % 2) + 4 * ((b2 + i) % 2)
+        return pl.ds(pl.multiple_of(mine * block, 16), block)
+
+    def rows_of(index):
+        return pl.ds(pl.multiple_of(index * quarter, quarter), quarter)
+
+    base = used["remote"]
+    used["remote"] += 3 * tiles
+
+    def tile_copy(kind, src, dst, t, to):
+        index = base + kind * tiles + t
+        return pltpu.make_async_remote_copy(
+            src_ref=src, dst_ref=dst, send_sem=send_sem.at[index], recv_sem=recv_sem.at[index],
+            device_id=to, device_id_type=pl.DeviceIdType.MESH,
+        )
+
+    def x_tile(t):
+        return tile_copy(0, own_hbm.at[t], far_hbm.at[t], t, x_to)
+
+    def z1_tile(t):
+        return tile_copy(1, part_s.at[t % 2], near1_hbm.at[t], t, z1_to)
+
+    def z2_tile(t):
+        return tile_copy(2, part_s2.at[t % 2], near2_hbm.at[t], t, z2_to)
+
+    barrier = pltpu.get_barrier_semaphore()
+    for to in (x_to, z1_to, z2_to, c_to, y_to):
+        pl.semaphore_signal(barrier, inc=1, device_id=to, device_id_type=pl.DeviceIdType.MESH)
+    pl.semaphore_wait(barrier, 5)
+
+    def share(source, index):
+        return [
+            remote(
+                source.at[row_block(1, core, i)],
+                far_a.at[index, core, pl.ds(i * block, block)],
+                x_to,
+            )
+            for i in range(2)
+        ]
+
+    def forward(index):
+        return remote(far_a.at[index, core], far_a.at[index, core], c_to)
+
+    COT, N2, GB, N1 = range(4)
+    attn_y = remote(attn_hbm, attn_all.at[1], y_to)
+    attn_c = remote(attn_hbm, attn_all.at[2], c_to)
+    attn_cy = remote(attn_all.at[1], attn_all.at[3], c_to)
+    attn_x = remote(attn_hbm, attn_far, x_to)
+    attn_own = local(attn_hbm, attn_all.at[0])
+    started(attn_y, attn_c, attn_own)
+    cot_x = share(cot_turned_hbm, COT)
+    started(*cot_x)
+    started(attn_x)
+    n1_x = share(n1_turned_hbm, N1)
+    started(*n1_x)
+    own_loads = []
+    for index, source in ((COT, cot_turned_hbm), (N1, n1_turned_hbm)):
+        for p in range(4):
+            own_loads.append(
+                local(
+                    source.at[row_block(0, p // 2, p % 2)],
+                    own_a.at[index, pl.ds(p * block, block)],
+                )
+            )
+    started(*own_loads)
+
+    def norm_scale(rows):
+        return lax.rsqrt(jnp.mean(rows * rows, axis=-1, keepdims=True) + EPSILON)
+
+    gain = gain_ref[...]
+    n2_x = share(turned, N2)
+
+    def front(weights, cot_turned, ring, wo, x_rows):
+        def fetch(t, slot, rows):
+            return [
+                pltpu.make_async_copy(
+                    source.at[pl.ds(t * UNITS, rows)],
+                    weights.at[slot, k, pl.ds(0, rows)],
+                    weight_sem.at[slot, k],
+                )
+                for k, source in enumerate((wg_hbm, wu_hbm, wd_hbm))
+            ]
+
+        loads = [local(wo_hbm, wo), local(x_hbm, x_rows), local(cot_turned_hbm, cot_turned)]
+        started(*loads)
+        started(*fetch(0, 0, UNITS))
+        loads[0].wait()
+        loads[1].wait()
+
+        def add_part(p, first=False):
+            def body(n, carry):
+                cols = pl.ds(pl.multiple_of(n * 512, 512), 512)
+                held = x_rows[:, cols].astype(jnp.float32) if first else middle[:, cols]
+                middle[:, cols] = held + matmul(attn_all[p], wo[p, :, cols])
+                return carry
+
+            lax.fori_loop(0, width // 512, body, 0)
+
+        attn_own.wait()
+        add_part(0, True)
+        attn_c.wait_recv()
+        add_part(2)
+        attn_y.wait_recv()
+        started(attn_cy)
+        add_part(1)
+        attn_cy.wait_recv()
+        add_part(3)
+
+        def norm(a, carry):
+            rows = middle[rows_of(a), :]
+            turned[:, rows_of(a)] = (rows * norm_scale(rows) * gain).astype(jnp.bfloat16).T
+            return carry
+
+        lax.fori_loop(0, 4, norm, 0)
+        started(*n2_x)
+        for p in range(4):
+            own_a[N2, p * block : (p + 1) * block, :] = turned[row_block(0, p // 2, p % 2), :]
+        loads[2].wait()
+        acc[...] = jnp.zeros_like(acc)
+
+        def keep_tile(t):
+            return pltpu.make_async_copy(ring.at[t % 2], own_hbm.at[t], weight_sem.at[2, t % 2])
+
+        def tile(t, carry):
+            slot = t % 2
+
+            @pl.when(t < tiles - 1)
+            def _():
+                for copy in fetch(t, slot, UNITS):
+                    copy.wait()
+
+            @pl.when(t == tiles - 1)
+            def _():
+                for copy in fetch(t, slot, rest):
+                    copy.wait()
+
+            @pl.when(t + 1 < tiles - 1)
+            def _():
+                started(*fetch(t + 1, 1 - slot, UNITS))
+
+            @pl.when(t + 1 == tiles - 1)
+            def _():
+                weights[1 - slot, :, rest:, :] = jnp.zeros(
+                    (3, UNITS - rest, width), weights.dtype
+                )
+                started(*fetch(t + 1, 1 - slot, rest))
+
+            gate = matmul(weights[slot, 0], turned[...])
+            up_part = matmul(weights[slot, 1], turned[...])
+            grad_hidden = matmul(weights[slot, 2], cot_turned[...])
+            sigma = jax.nn.sigmoid(gate)
+            swish = gate * sigma
+            ring[slot, :, :UNITS] = (swish * up_part).astype(jnp.bfloat16).T
+            ring[slot, :, UNITS : 2 * UNITS] = (
+                (grad_hidden * up_part * sigma * (1.0 + gate * (1.0 - sigma)))
+                .astype(jnp.bfloat16)
+                .T
+            )
+            ring[slot, :, 2 * UNITS :] = (grad_hidden * swish).astype(jnp.bfloat16).T
+
+            def body(n, carry):
+                cols = pl.ds(pl.multiple_of(n * 512, 512), 512)
+                acc[:, cols] += matmul(
+                    ring[slot, :, UNITS : 2 * UNITS], weights[slot, 0, :, cols]
+                ) + matmul(ring[slot, :, 2 * UNITS :], weights[slot, 1, :, cols])
+                return carry
+
+            lax.fori_loop(0, width // 512, body, 0)
+
+            @pl.when(t > 0)
+            def _():
+                keep_tile(t - 1).wait()
+
+            @pl.when((t > 0) & (t <= AHEAD))
+            def _():
+                x_tile(t - 1).start()
+
+            keep_tile(t).start()
+            return carry
+
+        lax.fori_loop(0, tiles, tile, 0)
+        keep_tile(tiles - 1).wait()
+        for copy in n2_x:
+            copy.wait_send()
+
+    pl.run_scoped(
+        front,
+        pltpu.VMEM((2, 3, UNITS, width), jnp.bfloat16),
+        pltpu.VMEM((width, TOK), jnp.bfloat16),
+        pltpu.VMEM((2, TOK, 3 * UNITS), jnp.bfloat16),
+        pltpu.VMEM((4, width // 4, width), jnp.bfloat16),
+        pltpu.VMEM((TOK, width), jnp.bfloat16),
+    )
+
+    def reduce_start(total, sent, core_to):
+        sent[...] = total[...].astype(jnp.bfloat16)
+        copies = [
+            remote(sent.at[rows_of(lane_c)], core_to.at[0], c_to),
+            remote(sent.at[rows_of(lane_cy)], core_to.at[1], c_to),
+        ]
+        started(*copies)
+        return copies
+
+    def reduce_middle(total, copies, core_to, lane_to):
+        for copy in copies:
+            copy.wait()
+        lane_send[...] = (
+            total[rows_of(lane_y), :] + core_to[1].astype(jnp.float32)
+        ).astype(jnp.bfloat16)
+        copy = remote(lane_send, lane_to, y_to)
+        copy.start()
+        return copy
+
+    def reduce_end(total, copy, core_to, lane_to):
+        copy.wait()
+        return (
+            total[rows_of(lane), :]
+            + core_to[0].astype(jnp.float32)
+            + lane_to[...].astype(jnp.float32)
+        )
+
+    def spread_start(full):
+        mine, theirs = full.at[rows_of(lane)], full.at[rows_of(lane_y)]
+        copies = [
+            remote(mine, mine, y_to),
+            remote(mine, mine, c_to),
+            remote(theirs, theirs, c_to),
+        ]
+        started(*copies[:2])
+        return copies
+
+    def spread_end(copies):
+        copies[0].wait_recv()
+        copies[2].start()
+        copies[0].wait_send()
+        copies[1].wait()
+        copies[2].wait()
+
+    def first_product(a, b_own, b_far, h, index):
+        return matmul(own_a[index, h * half : (h + 1) * half, :], b_own) + matmul(
+            far_a[index, h], b_far
+        )
+
+    tile_loads = {}
+
+    def load_own(t):
+        tile_loads[t] = started(local(own_hbm.at[t], stage.at[t % 2]))
+
+    def first_step(t):
+        slot = t % 2
+        if t not in tile_loads:
+            load_own(t)
+        x_tile(t).wait_recv()
+        far_load = started(local(far_hbm.at[t], far_stage))
+        if t + AHEAD < tiles:
+            x_tile(t + AHEAD).start()
+        tile_loads[t].wait()
+        far_load.wait()
+        if t >= 2:
+            z1_tile(t - 2).wait_send()
+
+        def body(n, h):
+            cols = pl.ds(pl.multiple_of(n * UNITS, UNITS), UNITS)
+            index = (n + 1) // 2
+            return cols, matmul(
+                own_a[index, h * half : (h + 1) * half, :], stage[slot, :, cols]
+            ) + matmul(far_a[index, h], far_stage[:, cols])
+
+        def sent(n, carry):
+            cols, value = body(n, 1)
+            part_s[slot, :, cols] = value.astype(jnp.bfloat16)
+            return carry
+
+        def kept(n, carry):
+            cols, value = body(n, 0)
+            part_k[slot, :, cols] = value.astype(jnp.bfloat16)
+            return carry
+
+        lax.fori_loop(0, 3, sent, 0)
+        z1_tile(t).start()
+        lax.fori_loop(0, 3, kept, 0)
+        if t + 1 < tiles:
+            load_own(t + 1)
+
+    def second_step(t):
+        slot = t % 2
+        z1_tile(t).wait_recv()
+        load = started(local(near1_hbm.at[t], near1))
+        load.wait()
+        if t >= 2:
+            z2_tile(t - 2).wait_send()
+        part_s2[slot] = (
+            part_k[slot, block:, :].astype(jnp.float32) + near1[block:, :].astype(jnp.float32)
+        ).astype(jnp.bfloat16)
+        z2_tile(t).start()
+        part_f[slot] = part_k[slot, :block, :].astype(jnp.float32) + near1[:block, :].astype(
+            jnp.float32
+        )
+
+    final_copies = {}
+
+    def third_step(t):
+        slot = t % 2
+        z2_tile(t).wait_recv()
+        load = started(local(near2_hbm.at[t], near2))
+        load.wait()
+        if t >= 2:
+            final_copies[t - 2].wait()
+        final[slot] = part_f[slot] + near2[...].astype(jnp.float32)
+        final_copies[t] = started(local(final.at[slot], tiles_out.at[t]))
+
+    def step(t):
+        if t < tiles:
+            first_step(t)
+        if 0 <= t - 1 < tiles:
+            second_step(t - 1)
+        if 0 <= t - 2 < tiles:
+            third_step(t - 2)
+
+    SMALL = {"out": (0, 384, GB), "query": (384, 384, N1), "pair": (768, 128, N1)}
+    small_copies = {}
+
+    def small_first(name, b_own, b_far):
+        begin, wide, index = SMALL[name]
+        cols = slice(begin, begin + wide)
+        small_s[half:, cols] = (
+            matmul(own_a[index, half:, :], b_own) + matmul(far_a[index, 1], b_far)
+        ).astype(jnp.bfloat16)
+        copy = remote(small_s.at[pl.ds(half, half), pl.ds(begin, wide)], small_in.at[:, pl.ds(begin, wide)], z1_to)
+        copy.start()
+        small_copies[name] = copy
+        small_s[:half, cols] = (
+            matmul(own_a[index, :half, :], b_own) + matmul(far_a[index, 0], b_far)
+        ).astype(jnp.bfloat16)
+
+    def small_second(name):
+        begin, wide, _ = SMALL[name]
+        cols = slice(begin, begin + wide)
+        small_copies[name].wait_recv()
+        small_s2[:, cols] = (
+            small_s[block:half, cols].astype(jnp.float32)
+            + small_in[block:, cols].astype(jnp.float32)
+        ).astype(jnp.bfloat16)
+        copy = remote(small_s2.at[:, pl.ds(begin, wide)], small_in2.at[:, pl.ds(begin, wide)], z2_to)
+        copy.start()
+        small_copies[name].wait_send()
+        small_copies[name] = copy
+
+    def small_third(name, out_ref):
+        begin, wide, _ = SMALL[name]
+        cols = slice(begin, begin + wide)
+        small_copies[name].wait()
+        out_ref[...] = (
+            small_s[:block, cols].astype(jnp.float32)
+            + small_in[:block, cols].astype(jnp.float32)
+            + small_in2[:, cols].astype(jnp.float32)
+        )
+
+    def rest_of(cot, query, pair, full, log_total, cosine, sine, grads, incoming, wo_own):
+        loads = [
+            local(cot_hbm, cot),
+            local(q_hbm, query),
+            local(pair_hbm, pair),
+            local(full_hbm, full),
+            local(log_hbm, log_total),
+            local(cos_hbm, cosine),
+            local(sin_hbm, sine),
+            local(wo_hbm.at[0], wo_own),
+        ]
+        started(*loads)
+        copies = reduce_start(acc, rel, core_in)
+        forwards = []
+        for index, parts in ((COT, cot_x), (N1, n1_x), (N2, n2_x)):
+            for copy in parts:
+                copy.wait_recv()
+            forwards.append(started(forward(index)))
+        lane_copy = reduce_middle(acc, copies, core_in, lane_in)
+        for load in own_loads:
+            load.wait()
+        for copy in forwards:
+            copy.wait()
+        step(0)
+        grad_full[rows_of(lane), :] = reduce_end(acc, lane_copy, core_in, lane_in).astype(
+            jnp.bfloat16
+        )
+        spread = spread_start(grad_full)
+        for copy in cot_x + n1_x:
+            copy.wait_send()
+        grads[...] = jnp.zeros_like(grads)
+        spread_end(spread)
+        for load in loads:
+            load.wait()
+
+        def middle_back(a, total):
+            grad = grad_full[rows_of(a), :].astype(jnp.float32)
+            rows = middle[rows_of(a), :]
+            factor2 = norm_scale(rows)
+            weighted = grad * gain
+            result = (
+                cot[rows_of(a), :].astype(jnp.float32)
+                + factor2 * weighted
+                - rows * factor2**3 * jnp.mean(weighted * rows, axis=-1, keepdims=True)
+            )
+            acc[rows_of(a), :] = result
+            turned[:, rows_of(a)] = result.astype(jnp.bfloat16).T
+            return total + jnp.sum(grad * rows * factor2, axis=0, keepdims=True)
+
+        gain_out[...] = lax.fori_loop(0, 4, middle_back, jnp.zeros((1, width), jnp.float32))
+        middle_copy = started(local(acc, middle_out))
+        branch_x = share(turned, GB)
+        started(*branch_x)
+        incoming[...] = matmul(wo_own[...], turned[...]).astype(jnp.bfloat16).T
+        for p in range(4):
+            own_a[GB, p * block : (p + 1) * block, :] = turned[row_block(0, p // 2, p % 2), :]
+        step(1)
+
+        sign = jnp.where(lax.broadcasted_iota(jnp.int32, (1, HD), 1) < HD // 2, 1.0, -1.0)
+
+        def of_first(t):
+            late = t // 8
+            device = t * (1 - late) + (15 - t) * late
+            return device, late * (TOK - HALF)
+
+        def of_middle(t):
+            return t, HALF
+
+        def region(begin, count, blocks, locate, shared):
+            heads = query.shape[0]
+            rows = heads * count
+            q_rows = region_rows(query, begin, count)
+            grad_rows = jnp.concatenate(
+                [incoming[begin : begin + count, h * HD : (h + 1) * HD] for h in range(heads)], 0
+            )
+            logs = region_rows(log_total, begin, count)[:, :1]
+            delta = jnp.sum(
+                grad_rows.astype(jnp.float32) * region_rows(full, begin, count),
+                axis=1,
+                keepdims=True,
+            )
+
+            def add(t, carry, diagonal=False):
+                device, offset = locate(t)
+                slot = (
+                    4 * ((device % 2 + b0) % 2)
+                    + 2 * (((device // 2) % 2 + b1) % 2)
+                    + (device // 4 + b2) % 2
+                )
+                place = pl.ds(pl.multiple_of(offset, HALF), count)
+                keys, values = pair[0, slot, place, :], pair[1, slot, place, :]
+                probs = jnp.exp2(contract_cols(q_rows, keys) * factor - logs)
+                if diagonal:
+                    probs = jnp.where(triangle(rows, count), probs, 0.0)
+                elif shared:
+                    same = docs_ref[pl.ds(device, 1), :] == docs_ref[pl.ds(me, 1), :]
+                    probs = jnp.where(same, probs, 0.0)
+                grad_scores = (probs * (contract_cols(grad_rows, values) - delta)).astype(
+                    jnp.bfloat16
+                )
+                grads[0, slot, place, :] += contract_rows(grad_scores, q_rows)
+                grads[1, slot, place, :] += contract_rows(probs.astype(jnp.bfloat16), grad_rows)
+                return carry + matmul(grad_scores, keys)
+
+            total = add(blocks, jnp.zeros((rows, HD), jnp.float32), True)
+            total = lax.fori_loop(0, blocks, add, total) * scale
+            cosines, sines = cosine[begin : begin + count, :], sine[begin : begin + count, :]
+            for h in range(heads):
+                part = total[h * count : (h + 1) * count]
+                grad_query[begin : begin + count, h * HD : (h + 1) * HD] = (
+                    part * cosines + pltpu.roll(part * sines, HD // 2, 1) * sign
+                ).astype(jnp.bfloat16)
+
+        region(0, HALF, me, of_first, False)
+        region(TOK - HALF, HALF, 15 - me, of_first, False)
+        step(2)
+        region(HALF, TOK - 2 * HALF, me, of_middle, True)
+
+        is_key = jnp.where(core == 0, 1.0, 0.0)
+        keep_by = is_key * scale + (1.0 - is_key)
+        send_by = (1.0 - is_key) * scale + is_key
+
+        def to_core(s, carry):
+            kv_send[s] = (grads[1 - core, s] * send_by).astype(jnp.bfloat16)
+            return carry
+
+        lax.fori_loop(0, 8, to_core, 0)
+        kv_c = remote(kv_send.at[pl.ds(0, 8)], kv_in.at[pl.ds(0, 8)], c_to)
+        kv_x = remote(kv_send.at[pl.ds(8, 4)], kv_in.at[pl.ds(8, 4)], x_to)
+        kv_1 = remote(kv_send.at[pl.ds(12, 2)], kv_in.at[pl.ds(12, 2)], z1_to)
+        kv_2 = remote(kv_send.at[pl.ds(14, 1)], kv_in.at[pl.ds(14, 1)], z2_to)
+        kv_c.start()
+        query_x = remote(grad_query, query_far, x_to)
+        query_y = remote(grad_query, query_out.at[1], y_to)
+        query_c = remote(grad_query, query_out.at[2], c_to)
+        query_cy = remote(query_out.at[1], query_out.at[3], c_to)
+        query_own = local(grad_query, query_out.at[0])
+        started(query_x, query_y, query_c, query_own)
+        for copy in branch_x:
+            copy.wait()
+        branch_c = started(forward(GB))
+        kv_c.wait()
+
+        def from_core(s, carry):
+            grads[core, s] = grads[core, s] * keep_by + kv_in[s].astype(jnp.float32)
+            return carry
+
+        lax.fori_loop(0, 8, from_core, 0)
+
+        def pass_on(copy, first, count):
+            def cast(s, carry):
+                kv_send[first + s] = grads[core, count + s].astype(jnp.bfloat16)
+                return carry
+
+            lax.fori_loop(0, count, cast, 0)
+            copy.start()
+
+        def take(copy, first, count):
+            copy.wait()
+
+            def add(s, carry):
+                grads[core, s] += kv_in[first + s].astype(jnp.float32)
+                return carry
+
+            lax.fori_loop(0, count, add, 0)
+
+        pass_on(kv_x, 8, 4)
+        step(3)
+        attn_x.wait()
+        branch_c.wait()
+        small_first("out", attn_all[0], attn_far[...])
+        query_y.wait_recv()
+        query_cy.start()
+        take(kv_x, 8, 4)
+        pass_on(kv_1, 12, 2)
+
+        def down(weights, hidden):
+            def fetch(t, slot, rows):
+                return [
+                    pltpu.make_async_copy(
+                        wd_hbm.at[pl.ds(t * UNITS, rows)],
+                        weights.at[slot, pl.ds(0, rows)],
+                        weight_sem.at[slot, 0],
+                    ),
+                    pltpu.make_async_copy(
+                        own_hbm.at[t, :, pl.ds(0, UNITS)], hidden.at[slot], weight_sem.at[slot, 1]
+                    ),
+                ]
+
+            started(*fetch(0, 0, UNITS))
+
+            def tile(t, carry):
+                slot = t % 2
+
+                @pl.when(t < tiles - 1)
+                def _():
+                    for copy in fetch(t, slot, UNITS):
+                        copy.wait()
+
+                @pl.when(t == tiles - 1)
+                def _():
+                    for copy in fetch(t, slot, rest):
+                        copy.wait()
+
+                @pl.when(t + 1 < tiles - 1)
+                def _():
+                    started(*fetch(t + 1, 1 - slot, UNITS))
+
+                @pl.when(t + 1 == tiles - 1)
+                def _():
+                    weights[1 - slot, rest:, :] = jnp.zeros((UNITS - rest, width), weights.dtype)
+                    started(*fetch(t + 1, 1 - slot, rest))
+
+                def body(n, carry):
+                    cols = pl.ds(pl.multiple_of(n * 512, 512), 512)
+                    product = matmul(hidden[slot], weights[slot, :, cols])
+                    acc[:, cols] = jnp.where(t == 0, product, acc[:, cols] + product)
+                    return carry
+
+                lax.fori_loop(0, width // 512, body, 0)
+                return carry
+
+            lax.fori_loop(0, tiles, tile, 0)
+
+        middle_copy.wait()
+        pl.run_scoped(
+            down,
+            pltpu.VMEM((2, UNITS, width), jnp.bfloat16),
+            pltpu.VMEM((2, TOK, UNITS), jnp.bfloat16),
+        )
+        out_copies = reduce_start(acc, rel, out_core_in)
+        step(4)
+        small_second("out")
+        take(kv_1, 12, 2)
+        pass_on(kv_2, 14, 1)
+        out_lane = reduce_middle(acc, out_copies, out_core_in, out_lane_in)
+        query_x.wait()
+        small_first("query", grad_query[...], query_far[...])
+        step(5)
+        small_third("out", wo_out)
+        kv_2.wait()
+        f_cos = cosine[...] * is_key + (1.0 - is_key)
+        f_sin = sine[...] * is_key
+        total = grads[core, 0] + kv_in[14].astype(jnp.float32)
+        grad_pair[...] = (total * f_cos + pltpu.roll(total * f_sin, HD // 2, 1) * sign).astype(
+            jnp.bfloat16
+        )
+        pair_x = remote(grad_pair, pair_far, x_to)
+        pair_y = remote(grad_pair, pair_out.at[1], y_to)
+        pair_c = remote(grad_pair, pair_out.at[2], c_to)
+        pair_cy = remote(pair_out.at[1], pair_out.at[3], c_to)
+        pair_own = local(grad_pair, pair_out.at[0])
+        started(pair_x, pair_y, pair_c, pair_own)
+        out_rows = reduce_end(acc, out_lane, out_core_in, out_lane_in) + middle[rows_of(lane), :]
+        grad_full[rows_of(lane), :] = out_rows.astype(jnp.bfloat16)
+        here = output_out.at[rows_of(lane)]
+        there = output_out.at[rows_of(lane_y)]
+        out_spread = [
+            remote(grad_full.at[rows_of(lane)], here, y_to),
+            remote(grad_full.at[rows_of(lane)], here, c_to),
+            remote(there, there, c_to),
+        ]
+        out_own = local(grad_full.at[rows_of(lane)], here)
+        started(out_spread[0], out_spread[1], out_own)
+        small_second("query")
+        step(6)
+        pair_x.wait()
+        small_first("pair", grad_pair[...], pair_far[...])
+        pair_y.wait_recv()
+        pair_cy.start()
+        small_third("query", wq_out)
+        out_spread[0].wait_recv()
+        out_spread[2].start()
+        step(7)
+        small_second("pair")
+        step(8)
+        small_third("pair", wp_out)
+        step(9)
+        step(10)
+        for t in (tiles - 2, tiles - 1):
+            z1_tile(t).wait_send()
+            z2_tile(t).wait_send()
+            final_copies[t].wait()
+        for t in range(tiles):
+            x_tile(t).wait_send()
+        for copy in (attn_y, attn_c, attn_cy, query_y, pair_y, out_spread[0]):
+            copy.wait_send()
+        for copy in (query_c, query_cy, pair_c, pair_cy, out_spread[1], out_spread[2]):
+            copy.wait()
+        for copy in (query_own, pair_own, out_own):
+            copy.wait()
+
+    pl.run_scoped(
+        rest_of,
+        pltpu.VMEM((TOK, width), jnp.bfloat16),
+        pltpu.VMEM((3, TOK, HD), jnp.bfloat16),
+        pltpu.VMEM((2, 8, TOK, HD), jnp.bfloat16),
+        pltpu.VMEM((3, TOK, HD), jnp.float32),
+        pltpu.VMEM((3, TOK, HD), jnp.float32),
+        pltpu.VMEM((TOK, HD), jnp.float32),
+        pltpu.VMEM((TOK, HD), jnp.float32),
+        pltpu.VMEM((2, 8, TOK, HD), jnp.float32),
+        pltpu.VMEM((TOK, 3 * HD), jnp.bfloat16),
+        pltpu.VMEM((width // 4, width), jnp.bfloat16),
+    )
+    assert used["remote"] <= REMOTE and used["local"] <= LOCAL, used
+
+
+AHEAD = 3
+REMOTE = 96
+LOCAL = 96
+
+
+def back(docs, gain, attn, full, log_total, query, pair, x, cot, normed1, cosine, sine, wo, wg, wu, wd):
+    tok_rows, width = x.shape
+    units = wg.shape[0]
+    tiles = pl.cdiv(units, UNITS)
+    half, block, quarter = width // 4, width // 8, tok_rows // 4
+    low, wide = jnp.bfloat16, jnp.float32
+    shape = jax.ShapeDtypeStruct
+    any_ = pl.BlockSpec(memory_space=pl.ANY)
+    outs = (
+        shape((tiles, block, 3 * UNITS), wide),
+        shape((block, 384), wide),
+        shape((block, 384), wide),
+        shape((block, HD), wide),
+        shape((1, width), wide),
+        shape((tok_rows, width), low),
+        shape((tok_rows, width), wide),
+        shape((4, tok_rows, 384), low),
+        shape((4, tok_rows, HD), low),
+        shape((tiles, tok_rows, 3 * UNITS), low),
+        shape((tiles, tok_rows, 3 * UNITS), low),
+        shape((tiles, half, 3 * UNITS), low),
+        shape((tiles, block, 3 * UNITS), low),
+    )
+    vmem = pltpu.VMEM
+    scratch = [
+        vmem((4, tok_rows, 384), low),
+        vmem((tok_rows, 384), low),
+        vmem((tok_rows, 384), low),
+        vmem((tok_rows, HD), low),
+        vmem((tok_rows, width), wide),
+        vmem((tok_rows, width), wide),
+        vmem((width, tok_rows), low),
+        vmem((4, width // 2, tok_rows), low),
+        vmem((4, 2, half, tok_rows), low),
+        vmem((2, tok_rows, 3 * UNITS), low),
+        vmem((tok_rows, 3 * UNITS), low),
+        vmem((2, half, 3 * UNITS), low),
+        vmem((2, half, 3 * UNITS), low),
+        vmem((2, block, 3 * UNITS), wide),
+        vmem((half, 3 * UNITS), low),
+        vmem((2, block, 3 * UNITS), low),
+        vmem((block, 3 * UNITS), low),
+        vmem((2, block, 3 * UNITS), wide),
+        vmem((tok_rows, width), low),
+        vmem((2, quarter, width), low),
+        vmem((quarter, width), low),
+        vmem((quarter, width), low),
+        vmem((tok_rows, width), low),
+        vmem((2, quarter, width), low),
+        vmem((quarter, width), low),
+        vmem((15, tok_rows, HD), low),
+        vmem((15, tok_rows, HD), low),
+        vmem((tok_rows, 384), low),
+        vmem((tok_rows, HD), low),
+        vmem((2 * half, 896), low),
+        vmem((half, 896), low),
+        vmem((block, 896), low),
+        vmem((block, 896), low),
+        pltpu.SemaphoreType.DMA((REMOTE,)),
+        pltpu.SemaphoreType.DMA((REMOTE,)),
+        pltpu.SemaphoreType.DMA((LOCAL,)),
+        pltpu.SemaphoreType.DMA((3, 3)),
+    ]
+    return pl.pallas_call(
+        functools.partial(back_kernel, width, units),
+        out_shape=outs,
+        in_specs=[VMEM, VMEM] + [any_] * 15,
+        out_specs=(any_, VMEM, VMEM, VMEM, VMEM) + (any_,) * 8,
+        scratch_shapes=scratch,
+        compiler_params=pltpu.CompilerParams(
+            vmem_limit_bytes=64 * 1024 * 1024, collective_id=0, has_side_effects=True
+        ),
+        cost_estimate=pl.CostEstimate(
+            flops=20 * tok_rows * width * units, bytes_accessed=10 * width * units, transcendentals=0
+        ),
+    )(docs, gain, attn, full, log_total, query, pair, x, cot, cot.T, normed1.T, cosine, sine, wo, wg, wu, wd)
 
 
 def on_device(
@@ -498,6 +1297,61 @@
     kv_index = lane * heads // (H // kv_heads)
     is_key = core == 0
 
+    def finish(
+        output, grad_middle, grad_normed1, grad_query, grad_pair, gain2_part,
+        grad_w_query, grad_w_pair, grad_w_out, grad_w_gate, grad_w_up, grad_w_down,
+    ):
+        weighted1 = grad_normed1 * norm1_gain
+        gain1_part = jnp.sum(grad_normed1 * inputs * scale1, axis=0)
+        grad_input = (
+            grad_middle
+            + scale1 * weighted1
+            - inputs * scale1**3 * jnp.mean(weighted1 * inputs, axis=-1, keepdims=True)
+        ).astype(jnp.bfloat16)
+
+        small = jnp.concatenate(
+            [
+                gain1_part,
+                gain2_part,
+                jnp.sum(grad_query.astype(jnp.float32), axis=0),
+                jnp.sum(grad_pair.astype(jnp.float32), axis=0),
+            ]
+        ).reshape(-1, HD)
+        bit = 1
+        while bit < shards:
+            small = small + swap(small, "cp", bit)
+            bit *= 2
+        wide = width // HD
+        gain1_sum = small[:wide].reshape(-1)
+        gain2_sum = small[wide : 2 * wide].reshape(-1)
+        bias_query = small[2 * wide : 2 * wide + heads].reshape(-1)
+
+        def assemble(parts, axis):
+            at = lambda index: lax.dynamic_index_in_dim(parts, reverse_bits(lane ^ index, 2), 0, keepdims=False)
+            return (
+                jnp.concatenate([at(0), at(2)], axis),
+                jnp.concatenate([at(1), at(3)], axis),
+            )
+
+        bias_key, bias_value = assemble(gather_tp(small[None, 2 * wide + heads], 0), 0)
+        grad_w_key, grad_w_value = assemble(gather_tp(grad_w_pair[None], 0), 1)
+        return (
+            output,
+            grad_input,
+            gain1_sum,
+            grad_w_query,
+            bias_query,
+            grad_w_key,
+            bias_key,
+            grad_w_value,
+            bias_value,
+            grad_w_out,
+            gain2_sum,
+            grad_w_gate,
+            grad_w_up,
+            grad_w_down,
+        )
+
     middle_docs = doc_ids.reshape(shards, tok_rows)[:, HALF]
     my_doc = middle_docs[me]
     start = jnp.sum((middle_docs < my_doc).astype(jnp.int32))
@@ -531,11 +1385,41 @@
     ).astype(jnp.bfloat16)
     query = query.transpose(1, 0, 2)
 
-    attn, attn_full, log_total = attend(place, query, pair, other)
+    attn, attn_full, log_total, pair = attend(place, query, pair, other)
     w_out_all = gather_tp(w_out, 0)
-    w_query_all = gather_tp(after(w_query, w_out_all), 1)
-    cot_shared = share(place, after(cotangent, other), shards)
-    normed1_shared = share(place, after(normed1, other), shards)
+    w_query_all = gather_tp(w_query, 1)
+    if shards == 8 and tok_rows == TOK:
+        (
+            tiles, grad_w_out, grad_w_query, grad_w_pair, gain2_part, output, grad_middle,
+            queries_all, pairs_all, *_,
+        ) = back(
+            jnp.broadcast_to(middle_docs[:, None], (shards, 2 * HALF)),
+            norm2_gain[None],
+            attn, attn_full, log_total, query, pair, layer_input, cotangent, normed1,
+            cosine, sine, w_out_all.reshape(4, -1, width), w_gate.T, w_up.T, w_down,
+        )
+        grad_w_out = grad_w_out.T
+        gain2_part = gain2_part[0]
+        grad_query, grad_pair = queries_all[0], pairs_all[0]
+        units = w_gate.shape[1]
+
+        def columns(kind):
+            part = tiles[:, :, kind * UNITS : (kind + 1) * UNITS]
+            return part.transpose(1, 0, 2).reshape(part.shape[1], -1)[:, :units]
+
+        grad_w_down, grad_w_gate, grad_w_up = columns(0).T, columns(1), columns(2)
+        grad_normed1 = sum(
+            contract_cols(queries_all[i], w_query_all[:, i * heads * HD : (i + 1) * heads * HD])
+            for i in range(4)
+        )
+        for i, far in enumerate(TP_ORDER):
+            grad_normed1 = grad_normed1 + contract_cols(pairs_all[i], pair_weight(lane ^ far))
+        return finish(
+            output, grad_middle, grad_normed1, grad_query, grad_pair, gain2_part,
+            grad_w_query, grad_w_pair, grad_w_out, grad_w_gate, grad_w_up, grad_w_down,
+        )
+    cot_shared = share(place, cotangent, shards)
+    normed1_shared = share(place, normed1, shards)
 
     middle = inputs + matmul(gather_tp(attn, 1), w_out_all)
     scale2 = lax.rsqrt(jnp.mean(middle * middle, axis=-1, keepdims=True) + EPSILON)
@@ -578,7 +1462,7 @@
     grad_branch = grad_middle.astype(jnp.bfloat16)
     grad_attn = contract_cols(grad_branch, w_out).astype(jnp.bfloat16)
     grad_query, keep, send = attend_back(
-        place, query, pair, other, grad_attn, attn_full, log_total, cosine, sine
+        place, query, pair, grad_attn, attn_full, log_total, cosine, sine
     )
 
     part = tok_rows // 4
@@ -611,55 +1495,9 @@
         grad_normed1 = grad_normed1 + contract_cols(
             pairs_all[:, i * HD : (i + 1) * HD], pair_weight(lane ^ far)
         )
-    weighted1 = grad_normed1 * norm1_gain
-    gain1_part = jnp.sum(grad_normed1 * inputs * scale1, axis=0)
-    grad_input = (
-        grad_middle
-        + scale1 * weighted1
-        - inputs * scale1**3 * jnp.mean(weighted1 * inputs, axis=-1, keepdims=True)
-    ).astype(jnp.bfloat16)
-
-    small = jnp.concatenate(
-        [
-            gain1_part,
-            gain2_part,
-            jnp.sum(grad_query.astype(jnp.float32), axis=0),
-            jnp.sum(grad_pair.astype(jnp.float32), axis=0),
-        ]
-    ).reshape(-1, HD)
-    bit = 1
-    while bit < shards:
-        small = small + swap(small, "cp", bit)
-        bit *= 2
-    wide = width // HD
-    gain1_sum = small[:wide].reshape(-1)
-    gain2_sum = small[wide : 2 * wide].reshape(-1)
-    bias_query = small[2 * wide : 2 * wide + heads].reshape(-1)
-
-    def assemble(parts, axis):
-        at = lambda index: lax.dynamic_index_in_dim(parts, reverse_bits(lane ^ index, 2), 0, keepdims=False)
-        return (
-            jnp.concatenate([at(0), at(2)], axis),
-            jnp.concatenate([at(1), at(3)], axis),
-        )
-
-    bias_key, bias_value = assemble(gather_tp(small[None, 2 * wide + heads], 0), 0)
-    grad_w_key, grad_w_value = assemble(gather_tp(grad_w_pair[None], 0), 1)
-    return (
-        output,
-        grad_input,
-        gain1_sum,
-        grad_w_query,
-        bias_query,
-        grad_w_key,
-        bias_key,
-        grad_w_value,
-        bias_value,
-        grad_w_out,
-        gain2_sum,
-        grad_w_gate,
-        grad_w_up,
-        grad_w_down,
+    return finish(
+        output, grad_middle, grad_normed1, grad_query, grad_pair, gain2_part,
+        grad_w_query, grad_w_pair, grad_w_out, grad_w_gate, grad_w_up, grad_w_down,
     )
 
 

time: 629 us -> 476 us (0.76)
  waiting for transfers between devices: 239 us -> 22 us
  Pallas kernels: 132 us -> 335 us
  starting transfers between devices: 84.7 us -> 14.1 us
  other arithmetic: 69 us -> 32 us
  local copies, waits for them, and re-layouts: 62.2 us -> 44.1 us
  matrix products: 33.3 us -> 19.7 us
    ppermute x68 -> x15, waiting for transfers between devices: 239 us -> 22 us  [swap(): return lax.ppermute(value, axis, [(i, i ^ bit) for i in range(size)])]
    pallas_call x17 -> x1, Pallas kernels: 119 us -> 321 us  [back(): pl.pallas_call(functools.partial(back_kernel, width, units), out_shape=ou...]
    ppermute x68 -> x15, starting transfers between devices: 84.7 us -> 14.1 us  [swap(): return lax.ppermute(value, axis, [(i, i ^ bit) for i in range(size)])]
    convert_element_type x17 -> x1, other arithmetic: 25.9 us -> 3.64 us  [finish(): grad_input = (grad_middle + scale1 * weighted1 - inputs * scale1 ** 3 * j...]
    unnamed x156 -> x93, local copies, waits for them, and re-layouts: 38.5 us -> 18.3 us
    dot_general x6 -> x2, matrix products: 19.9 us -> 4.05 us  [matmul(): return jnp.dot(left, right, preferred_element_type=jnp.float32)]
    transpose x0 -> x5, local copies, waits for them, and re-layouts: none -> 11.3 us  [the longest x4 8.1 us: columns(): return part.transpose(1, 0, 2).reshape(part.shape[1], -1)[:, :units]]
    dot_general x6 -> x8, matrix products: 13.4 us -> 15.7 us  [contract_cols(): lax.dot_general(left, right, (((1,), (1,)), ((), ())), preferred_element_...]
  transfers between devices with their start and end apart: 68 -> 15, of which waited for: 29 -> 6; matrix products, arithmetic and copies ran while one was open for 25% -> 17% of each run, Pallas kernels for 21% -> 71%
where the time goes in v2:
time: 476 us; the launch traced here: 468 us
  Pallas kernels  335 us (70%)
  local copies, waits for them, and re-layouts  44.1 us (9%)
  other arithmetic  32 us (7%)
  waiting for transfers between devices  22 us (5%)
  matrix products  19.7 us (4%)
  starting transfers between devices  14.1 us (3%)
    pallas_call x1, Pallas kernels, back(): pl.pallas_call(functools.partial(back_kernel, width, units), out_shape=ou...  321 us
    ppermute x15, waiting for transfers between devices, swap(): return lax.ppermute(value, axis, [(i, i ^ bit) for i in range(size)])  22 us
    unnamed x93, local copies, waits for them, and re-layouts  18.3 us
    dot_general x8, matrix products, contract_cols(): lax.dot_general(left, right, (((1,), (1,)), ((), ())), preferred_element_...  15.7 us
    ppermute x15, starting transfers between devices, swap(): return lax.ppermute(value, axis, [(i, i ^ bit) for i in range(size)])  14.1 us
    pallas_call x1, Pallas kernels, attend(): pl.pallas_call(functools.partial(attend_kernel, shards), out_shape=(jax.S...  13.6 us
  transfers between devices with their start and end apart: 15, of which 6 were waited for; matrix products, arithmetic and copies ran while one was open for 17% of the time, Pallas kernels for 71%

profile of v2, /device:TPU:0, one launch (start us, length us, event | category | flops | bytes accessed | tf_op | source)
XLA Modules:
  0.0 468.1 jit_solution(4149039586893547796)
XLA Ops:
  0.7 3.0 collective-permute-start.4
  10.5 2.6 collective-permute-start
  13.6 5.6 %collective-permute-done = bf16[1,512,128]{2,1,0:T(8,128)(2,1)S(1)} collective-permute-done((bf16[1,512,128]{2,1,0:T(8,128)(2,1)S(1)}, bf16[1,512,128]{2,1,0:T(8,128)(2,1)S(1)}, u32[]{:S(2)}, u32[]{:S(2)}) %collective-permute-start) | collective-permute-done | bytes 131104 | tf_op jit(solution)/shard_map/ppermute | solution.py:62
  20.0 10.9 %collective-permute-done.4 = bf16[384,1536]{1,0:T(8,128)(2,1)} collective-permute-done((bf16[384,1536]{1,0:T(8,128)(2,1)}, bf16[384,1536]{1,0:T(8,128)(2,1)}, u32[]{:S(2)}, u32[]{:S(2)}) %collective-permute-start.4) | collective-permute-done | bytes 1179680 | tf_op jit(solution)/shard_map/ppermute | solution.py:62
  30.9 2.8 pad_maximum_fusion.1
  33.7 3.1 convolution_add_fusion.5
  43.7 2.6 copy.70
  51.7 2.2 collective-permute-done.2
  57.9 3.3 pad_maximum_fusion.2
  62.6 13.6 %shard_map.263 = (bf16[512,384]{1,0:T(8,128)(2,1)}, f32[3,512,128]{2,1,0:T(8,128)}, f32[3,512,128]{2,1,0:T(8,128)}, bf16[2,8,512,128]{3,2,1,0:T(8,128)(2,1)}) custom-call(s32[4]{0:T(128)} %pad_add_fusion.place_ref, bf16[3,512,128]{2,1,0:T(8,128)(2,1)} %fusion.16.q_ref.refs_5_, bf16[8,512,128]{2,1,0:T(8,128)(2,1)} %copy-done.16, bf16[8,512,128]{2,1,0:T(8,128)(2,1)} %copy-done.38), custom_call_target="tpu_custom_call" | custom-call | flops 1207959552 | bytes 2097152 | tf_op jit(solution)/shard_map/pallas_call | solution.py:354
  76.2 3.7 pad_maximum_fusion
  80.6 321.0 %shard_map.264 = (f32[9,192,768]{2,1,0:T(8,128)}, f32[192,384]{1,0:T(8,128)}, f32[192,384]{1,0:T(8,128)}, f32[192,128]{1,0:T(8,128)}, f32[1,1536]{1,0:T(1,128)},...) custom-call(s32[8,256]{1,0:T(8,128)} %broadcast_in_dim.34.refs_0_, ...), custom_call_target="tpu_custom_call" | custom-call | flops 35232153600 | bytes 34406400 | tf_op jit(solution)/shard_map/pallas_call | solution.py:1257
  406.3 2.3 fusion.23
  408.6 2.3 convolution_add_fusion.4
  410.9 2.3 fusion.11
  413.2 2.5 fusion.1
  417.7 3.4 fusion.10
  421.8 3.1 collective-permute-start.11
  424.9 2.3 slice_bitcast_fusion.1
  429.2 3.2 slice_bitcast_fusion
  433.3 3.6 copy.79
  437.8 3.6 fusion.7
  446.5 2.9 copy.84
  453.0 3.1 copy.85
  (166 shorter events, 57.5 us)
Async XLA Ops:
  0.7 30.1 %collective-permute-start.4 = (bf16[384,1536]{1,0:T(8,128)(2,1)}, bf16[384,1536]{1,0:T(8,128)(2,1)}, u32[]{:S(2)}, u32[]{:S(2)}) collective-permute-start(bf16[384,1536]{1,0:T(8,128)(2,1)} %param.24), channel_id=1, source_target_pairs={{0,2},{1,3},{2,0},{3,1},{4,6},{5,7},{6,4},{7,5},{8,10},{9,11},{10,... | collective-permute-start | bytes 3538952 | tf_op jit(solution)/shard_map/ppermute | solution.py:62
  5.5 50.8 %copy-start = (bf16[512,1536]{0,1:T(8,128)(2,1)}, bf16[512,1536]{0,1:T(8,128)(2,1)S(1)}, u32[]{:S(2)}) copy-start(bf16[512,1536]{0,1:T(8,128)(2,1)S(1)} %copy.65) | copy-start | bytes 4718596
  8.4 47.9 %copy-start.28 = (f32[512]{0:T(512)}, f32[512]{0:T(512)S(1)}, u32[]{:S(2)}) copy-start(f32[512]{0:T(512)S(1)} %get-tuple-element.109) | copy-start | bytes 6148
  9.3 21.5 %copy-start.3 = (bf16[384,1536]{1,0:T(8,128)(2,1)S(1)}, bf16[384,1536]{1,0:T(8,128)(2,1)}, u32[]{:S(2)}) copy-start(bf16[384,1536]{1,0:T(8,128)(2,1)} %param.24) | copy-start | bytes 3538948
  9.5 24.2 %copy-start.39 = (f32[384]{0:T(512)S(1)}, f32[384]{0:T(512)}, u32[]{:S(2)}) copy-start(f32[384]{0:T(512)} %param.19) | copy-start | bytes 4612
  10.5 27.6 %copy-start.9 = (bf16[1,512,128]{2,1,0:T(8,128)(2,1)}, bf16[1,512,128]{2,1,0:T(8,128)(2,1)S(1)}, u32[]{:S(2)}) copy-start(bf16[1,512,128]{2,1,0:T(8,128)(2,1)S(1)} %get-tuple-element.93) | copy-start | bytes 393220
  10.5 8.7 %collective-permute-start = (bf16[1,512,128]{2,1,0:T(8,128)(2,1)S(1)}, bf16[1,512,128]{2,1,0:T(8,128)(2,1)S(1)}, u32[]{:S(2)}, u32[]{:S(2)}) collective-permute-start(bf16[1,512,128]{2,1,0:T(8,128)(2,1)S(1)} %get-tuple-element.93), channel_id=1, source_target_pairs={{0,16},{4,20},{8,24},{12,28},{16,0},{20,4},{24,8},{28,12},{1,17},{... | collective-permute-start | bytes 393224 | tf_op jit(solution)/shard_map/ppermute | solution.py:62
  13.1 44.8 %collective-permute-start.6 = (bf16[1536,384]{1,0:T(8,128)(2,1)}, bf16[1536,384]{1,0:T(8,128)(2,1)}, u32[]{:S(2)}, u32[]{:S(2)}) collective-permute-start(bf16[1536,384]{1,0:T(8,128)(2,1)} %param.18), channel_id=1, source_target_pairs={{0,2},{1,3},{2,0},{3,1},{4,6},{5,7},{6,4},{7,5},{8,10},{9,11},{10,... | collective-permute-start | bytes 3538952 | tf_op jit(solution)/shard_map/ppermute | solution.py:62
  19.2 18.9 %copy-start.12 = (bf16[1,512,128]{2,1,0:T(8,128)(2,1)}, bf16[1,512,128]{2,1,0:T(8,128)(2,1)S(1)}, u32[]{:S(2)}) copy-start(bf16[1,512,128]{2,1,0:T(8,128)(2,1)S(1)} %collective-permute-done) | copy-start | bytes 393220
  19.2 18.9 %collective-permute-start.1 = (bf16[2,512,128]{2,1,0:T(8,128)(2,1)S(1)}, bf16[2,512,128]{2,1,0:T(8,128)(2,1)S(1)}, u32[]{:S(2)}, u32[]{:S(2)}) collective-permute-start(bf16[2,512,128]{2,1,0:T(8,128)(2,1)S(1)} %pad_maximum_fusion.8), channel_id=1, source_target_pairs={{0,8},{4,12},{8,0},{12,4},{16,24},{20,28},{24,16},{28,20},{1,9},{5... | collective-permute-start | bytes 786440 | tf_op jit(solution)/shard_map/ppermute | solution.py:62
  33.7 42.5 %collective-permute-start.5 = (bf16[768,1536]{1,0:T(8,128)(2,1)}, bf16[768,1536]{1,0:T(8,128)(2,1)}, u32[]{:S(2)}, u32[]{:S(2)}) collective-permute-start(bf16[768,1536]{1,0:T(8,128)(2,1)} %pad_maximum_fusion.1), channel_id=1, source_target_pairs={{0,1},{1,0},{2,3},{3,2},{4,5},{5,4},{6,7},{7,6},{8,9},{9,8},{10,11... | collective-permute-start | bytes 7077896 | tf_op jit(solution)/shard_map/ppermute | solution.py:62
  39.0 14.9 %collective-permute-start.2 = (bf16[4,512,128]{2,1,0:T(8,128)(2,1)}, bf16[4,512,128]{2,1,0:T(8,128)(2,1)}, u32[]{:S(2)}, u32[]{:S(2)}) collective-permute-start(bf16[4,512,128]{2,1,0:T(8,128)(2,1)} %pad_maximum_fusion.4), channel_id=1, source_target_pairs={{0,4},{4,0},{8,12},{12,8},{16,20},{20,16},{24,28},{28,24},{1,5},{5... | collective-permute-start | bytes 1572872 | tf_op jit(solution)/shard_map/ppermute | solution.py:62
  55.1 6.5 %collective-permute-start.3 = (bf16[8,512,128]{2,1,0:T(8,128)(2,1)S(1)}, bf16[8,512,128]{2,1,0:T(8,128)(2,1)S(1)}, u32[]{:S(2)}, u32[]{:S(2)}) collective-permute-start(bf16[8,512,128]{2,1,0:T(8,128)(2,1)S(1)} %pad_maximum_fusion.3.mine_ref), channel_id=1, source_target_pairs={{0,1},{1,0},{2,3},{3,2},{4,5},{5,4},{6,7},{7,6},{8,9},{9,8},{10,11... | collective-permute-start | bytes 3145736 | tf_op jit(solution)/shard_map/ppermute | solution.py:62
  61.1 349.8 %collective-permute-start.7 = (bf16[1536,768]{1,0:T(8,128)(2,1)}, bf16[1536,768]{1,0:T(8,128)(2,1)}, u32[]{:S(2)}, u32[]{:S(2)}) collective-permute-start(bf16[1536,768]{1,0:T(8,128)(2,1)} %pad_maximum_fusion.2), channel_id=1, source_target_pairs={{0,1},{1,0},{2,3},{3,2},{4,5},{5,4},{6,7},{7,6},{8,9},{9,8},{10,11... | collective-permute-start | bytes 7077896 | tf_op jit(solution)/shard_map/ppermute | solution.py:62
  403.4 17.7 %copy-start.31 = (f32[128]{0:T(128)}, f32[128]{0:T(128)S(1)}, u32[]{:S(2)}) copy-start(f32[128]{0:T(128)S(1)} %convert_reduce_fusion.1) | copy-start | bytes 1540
  404.5 16.6 %copy-start.26 = (f32[384]{0:T(512)}, f32[384]{0:T(512)S(1)}, u32[]{:S(2)}) copy-start(f32[384]{0:T(512)S(1)} %convert_reduce_fusion) | copy-start | bytes 4612
  416.3 8.6 %slice-start = ((s8[5308416]{0:T(1024)(128)(4,1)}), s8[4194304]{0:T(1024)(128)(4,1)S(1)}, s32[]{:S(2)}) async-start(s8[5308416]{0:T(1024)(128)(4,1)} %bitcast.91), calls=%async_computation | async-start | bytes 8388608
  421.8 10.6 %collective-permute-start.8 = (f32[28,128]{1,0:T(8,128)}, f32[28,128]{1,0:T(8,128)}, u32[]{:S(2)}, u32[]{:S(2)}) collective-permute-start(f32[28,128]{1,0:T(8,128)} %maximum_bitcast_fusion), channel_id=1, source_target_pairs={{0,4},{4,0},{8,12},{12,8},{16,20},{20,16},{24,28},{28,24},{1,5},{5... | collective-permute-start | bytes 43016 | tf_op jit(solution)/shard_map/ppermute | solution.py:62
  421.8 41.0 %collective-permute-start.11 = (f32[1,192,128]{2,1,0:T(8,128)S(1)}, f32[1,192,128]{2,1,0:T(8,128)S(1)}, u32[]{:S(2)}, u32[]{:S(2)}) collective-permute-start(f32[1,192,128]{2,1,0:T(8,128)S(1)} %bitcast.96), channel_id=1, source_target_pairs={{0,2},{1,3},{2,0},{3,1},{4,6},{5,7},{6,4},{7,5},{8,10},{9,11},{10,... | collective-permute-start | bytes 294920 | tf_op jit(solution)/shard_map/ppermute | solution.py:62
  433.1 3.8 collective-permute-start.9
  437.6 20.3 %collective-permute-start.10 = (f32[28,128]{1,0:T(8,128)S(1)}, f32[28,128]{1,0:T(8,128)S(1)}, u32[]{:S(2)}, u32[]{:S(2)}) collective-permute-start(f32[28,128]{1,0:T(8,128)S(1)} %fusion.62), channel_id=1, source_target_pairs={{0,16},{4,20},{8,24},{12,28},{16,0},{20,4},{24,8},{28,12},{1,17},{... | collective-permute-start | bytes 43016 | tf_op jit(solution)/shard_map/ppermute | solution.py:62
  458.0 3.6 collective-permute-start.13
  461.6 1.1 collective-permute-start.14
  462.8 1.5 collective-permute-start.12
  (33 other events, 151.5 us)

commit v3 on v2

--- a/solution.py
+++ b/solution.py
@@ -471,13 +471,14 @@
 
 def back_kernel(width, units, *refs):
     (
-        docs_ref, gain_ref, attn_hbm, full_hbm, log_hbm, q_hbm, pair_hbm, x_hbm, cot_hbm,
-        cot_turned_hbm, n1_turned_hbm, cos_hbm, sin_hbm, wo_hbm, wg_hbm, wu_hbm, wd_hbm,
-        tiles_out, wo_out, wq_out, wp_out, gain_out, output_out, middle_out, query_out, pair_out,
-        own_hbm, far_hbm, near1_hbm, near2_hbm,
+        docs_ref, gain_ref, bias_ref, cosine, sine, x_hbm, cot_hbm, wq_hbm, wk_hbm, wv_hbm, wo_hbm,
+        wg_hbm, wu_hbm, wd_hbm,
+        tiles_out, wo_out, wq_out, wp_out, sums_out, output_out, input_out,
+        middle_hbm, query_hbm, pair_hbm, own_hbm, far_hbm, near_hbm, wo_all, wq_all, all_hbm, n1_hbm,
+        query, pair, full, log_total, sums, sums_in,
         attn_all, attn_far, query_far, pair_far, middle, acc, turned,
-        own_a, far_a, stage, far_stage, part_s, part_k, part_f, near1, part_s2, near2, final,
-        rel, core_in, lane_send, lane_in, grad_full, out_core_in, out_lane_in,
+        own_a, far_a, part_s, part_k, near1, part_s2, near2, near_stage, final, sent_tile,
+        rel, core_in, lane_send, lane_in, grad_full,
         kv_send, kv_in, grad_query, grad_pair, small_s, small_in, small_s2, small_in2,
         send_sem, recv_sem, local_sem, weight_sem,
     ) = refs
@@ -488,6 +489,12 @@
     x_to = {"cp": me + 1 - 2 * b0}
     z1_to = {"cp": me + 2 - 4 * b1}
     z2_to = {"cp": me + 4 - 8 * b2}
+    z3_to = {"cp": me + 6 - 4 * b1 - 8 * b2}
+    inner = (b1 + b2) % 2
+    peers = [
+        me + (r % 2) * (1 - 2 * b0) + (r // 2 % 2) * (2 - 4 * b1) + (r // 4) * (4 - 8 * b2)
+        for r in range(8)
+    ]
     c_to = {"tp": lane + 1 - 2 * core}
     y_to = {"tp": lane + 2 - 4 * high}
     lane_c, lane_y = lane + 1 - 2 * core, lane + 2 - 4 * high
@@ -523,32 +530,107 @@
         mine = (b0 + side) % 2 + 2 * ((b1 + h) % 2) + 4 * ((b2 + i) % 2)
         return pl.ds(pl.multiple_of(mine * block, 16), block)
 
+    def rows_of_block(index):
+        return pl.ds(pl.multiple_of(index * block, 16), block)
+
     def rows_of(index):
         return pl.ds(pl.multiple_of(index * quarter, quarter), quarter)
 
-    base = used["remote"]
-    used["remote"] += 3 * tiles
-
-    def tile_copy(kind, src, dst, t, to):
-        index = base + kind * tiles + t
+    x_tile = remote(own_hbm.at[tiles - 1], far_hbm, x_to)
+    z1_tile = remote(part_s, near1, z1_to)
+    z2_tile = remote(part_s2, near2, z2_to)
+
+    spread_base = used["remote"]
+    used["remote"] += 2 * 20
+    wide_half, wide_quarter = width // 2, width // 4
+
+    def block_of(j, side):
+        z = (b1 + 2 * b2, 1 - b1 + 2 * b2, 2 - b2, 3 - 3 * b2)[j]
+        return 2 * z + (b0 + side) % 2
+
+    def spread_part(k, j, side, c, y=None):
+        if y is None:
+            rows = pl.ds(pl.multiple_of(c * wide_half, wide_half), wide_half)
+        else:
+            rows = pl.ds(
+                pl.multiple_of(c * wide_half + y * wide_quarter, wide_quarter), wide_quarter
+            )
+        return all_hbm.at[k, block_of(j, side), rows]
+
+    def spread_copy(k, part, send, recv, to):
+        index = spread_base + 20 * k
         return pltpu.make_async_remote_copy(
-            src_ref=src, dst_ref=dst, send_sem=send_sem.at[index], recv_sem=recv_sem.at[index],
-            device_id=to, device_id_type=pl.DeviceIdType.MESH,
-        )
-
-    def x_tile(t):
-        return tile_copy(0, own_hbm.at[t], far_hbm.at[t], t, x_to)
-
-    def z1_tile(t):
-        return tile_copy(1, part_s.at[t % 2], near1_hbm.at[t], t, z1_to)
-
-    def z2_tile(t):
-        return tile_copy(2, part_s2.at[t % 2], near2_hbm.at[t], t, z2_to)
+            src_ref=part, dst_ref=part, send_sem=send_sem.at[index + send],
+            recv_sem=recv_sem.at[index + recv], device_id=to, device_id_type=pl.DeviceIdType.MESH,
+        )
+
+    def z_copy(k, m):
+        j, recv, to = ((0, 1, z1_to), (0, 2, z3_to), (1, 3, z3_to), (2, 2, z1_to), (3, 3, z1_to))[m]
+        return spread_copy(k, spread_part(k, j, 0, core), m, recv, to)
+
+    def z_arrival(k, j):
+        return spread_copy(k, spread_part(k, j, 0, core), 0, j, z1_to)
+
+    def c_copy(k, j, c=None):
+        return spread_copy(k, spread_part(k, j, 0, core if c is None else c), 4 + j, 4 + j, c_to)
+
+    def x_copy(k, j, side=0):
+        part = spread_part(k, j, side, core, None if (k, j) in WHOLE_HALVES else high)
+        return spread_copy(k, part, 8 + j, 8 + j, x_to)
+
+    def y_copy(k, j, y=None):
+        return spread_copy(
+            k, spread_part(k, j, 1, core, high if y is None else y), 12 + j, 12 + j, y_to
+        )
+
+    def d_copy(k, j, c=None):
+        return spread_copy(k, spread_part(k, j, 1, core if c is None else c), 16 + j, 16 + j, c_to)
+
+    def when(condition):
+        return pl.when(condition == 1)
+
+    def begin_spread(k):
+        z_copy(k, 0).start()
+
+        @when(inner)
+        def _():
+            z_copy(k, 1).start()
+
+    def arrive(k, j):
+        z_arrival(k, j).wait_recv()
+
+        @when(inner)
+        def _():
+            z_copy(k, j + 1).start()
+
+        started(c_copy(k, j), x_copy(k, j))
+
+    def arrive_inner(k, j):
+        @when(inner)
+        def _():
+            arrive(k, j)
+
+    def arrive_outer(k, j):
+        @when(1 - inner)
+        def _():
+            arrive(k, j)
+
+    def pass_y(k, j):
+        assert (k, j) not in WHOLE_HALVES
+        x_copy(k, j, 1).wait_recv()
+        y_copy(k, j).start()
+
+    def pass_core(k, j):
+        if (k, j) in WHOLE_HALVES:
+            x_copy(k, j, 1).wait_recv()
+        else:
+            y_copy(k, j, 1 - high).wait_recv()
+        d_copy(k, j).start()
 
     barrier = pltpu.get_barrier_semaphore()
-    for to in (x_to, z1_to, z2_to, c_to, y_to):
+    for to in (*({"cp": peers[r]} for r in (1, 2, 3, 4, 6)), c_to, y_to):
         pl.semaphore_signal(barrier, inc=1, device_id=to, device_id_type=pl.DeviceIdType.MESH)
-    pl.semaphore_wait(barrier, 5)
+    pl.semaphore_wait(barrier, 7)
 
     def share(source, index):
         return [
@@ -564,35 +646,180 @@
         return remote(far_a.at[index, core], far_a.at[index, core], c_to)
 
     COT, N2, GB, N1 = range(4)
-    attn_y = remote(attn_hbm, attn_all.at[1], y_to)
-    attn_c = remote(attn_hbm, attn_all.at[2], c_to)
+    own_blocks = [local(turned, all_hbm.at[k, me]) for k in range(2)]
+    wo_y = remote(wo_hbm, wo_all.at[1], y_to)
+    wo_c = remote(wo_hbm, wo_all.at[2], c_to)
+    wo_cy = remote(wo_all.at[1], wo_all.at[3], c_to)
+    wq_y = remote(wq_hbm, wq_all.at[1], y_to)
+    wq_c = remote(wq_hbm, wq_all.at[2], c_to)
+    wq_cy = remote(wq_all.at[1], wq_all.at[3], c_to)
+    attn_y = remote(attn_all.at[0], attn_all.at[1], y_to)
+    attn_c = remote(attn_all.at[0], attn_all.at[2], c_to)
     attn_cy = remote(attn_all.at[1], attn_all.at[3], c_to)
-    attn_x = remote(attn_hbm, attn_far, x_to)
-    attn_own = local(attn_hbm, attn_all.at[0])
-    started(attn_y, attn_c, attn_own)
-    cot_x = share(cot_turned_hbm, COT)
-    started(*cot_x)
-    started(attn_x)
-    n1_x = share(n1_turned_hbm, N1)
-    started(*n1_x)
-    own_loads = []
-    for index, source in ((COT, cot_turned_hbm), (N1, n1_turned_hbm)):
-        for p in range(4):
-            own_loads.append(
-                local(
-                    source.at[row_block(0, p // 2, p % 2)],
-                    own_a.at[index, pl.ds(p * block, block)],
-                )
-            )
-    started(*own_loads)
+    attn_x = remote(attn_all.at[0], attn_far, x_to)
+    n1_x = share(n1_hbm, N1)
+    n1_keep = local(turned, n1_hbm)
+    pair_1 = remote(pair.at[core, 0], pair.at[core, 2], z1_to)
+    pair_2 = remote(pair.at[core, 0], pair.at[core, 1], z2_to)
+    pair_3 = remote(pair.at[core, 0], pair.at[core, 3], z3_to)
+    pair_near = [remote(pair.at[core, i], pair.at[core, 4 + i], x_to) for i in range(4)]
+    pair_core = [remote(pair.at[core, i], pair.at[core, i], c_to) for i in range(8)]
+    started(wo_y, wo_c)
 
     def norm_scale(rows):
         return lax.rsqrt(jnp.mean(rows * rows, axis=-1, keepdims=True) + EPSILON)
 
-    gain = gain_ref[...]
-    n2_x = share(turned, N2)
-
-    def front(weights, cot_turned, ring, wo, x_rows):
+    gain1, gain2 = gain_ref[0:1, :], gain_ref[1:2, :]
+    sign = jnp.where(lax.broadcasted_iota(jnp.int32, (1, HD), 1) < HD // 2, 1.0, -1.0)
+    is_key = jnp.where(core == 0, 1.0, 0.0)
+
+    def turn(rows, cosines, sines):
+        return rows * cosines + pltpu.roll(rows * sign, HD // 2, 1) * sines
+
+    def turn_back(rows, cosines, sines):
+        return rows * cosines + pltpu.roll(rows * sines, HD // 2, 1) * sign
+
+    def opening(x_rows, cot_rows, normed, w_query, w_pair):
+        loads = [
+            local(x_hbm, x_rows),
+            local(wq_hbm, w_query),
+            local(cot_hbm, cot_rows),
+        ]
+        started(*loads)
+        index = used["local"]
+        used["local"] += 1
+        columns = pl.ds(pl.multiple_of(high * HD, HD), HD)
+        key_load = pltpu.make_async_copy(wk_hbm.at[:, columns], w_pair, local_sem.at[index])
+        value_load = pltpu.make_async_copy(wv_hbm.at[:, columns], w_pair, local_sem.at[index])
+
+        @pl.when(core == 0)
+        def _():
+            key_load.start()
+
+        @pl.when(core == 1)
+        def _():
+            value_load.start()
+
+        loads[0].wait()
+
+        def norm(a, carry):
+            rows = x_rows[rows_of(a), :].astype(jnp.float32)
+            normed[rows_of(a), :] = (rows * norm_scale(rows) * gain1).astype(jnp.bfloat16)
+            return carry
+
+        lax.fori_loop(0, 4, norm, 0)
+        key_load.wait()
+        rows = matmul(normed[...], w_pair[...]) + bias_ref[0:1, 3 * HD :]
+        pair[core, 0] = turn(
+            rows, cosine[...] * is_key + (1.0 - is_key), sine[...] * is_key
+        ).astype(jnp.bfloat16)
+        started(pair_1, pair_2, pair_3, pair_near[0], pair_core[0])
+        loads[2].wait()
+
+        def flip_cot(a, carry):
+            turned[:, rows_of(a)] = cot_rows[rows_of(a), :].T
+            return carry
+
+        lax.fori_loop(0, 4, flip_cot, 0)
+        own_blocks[0].start()
+        loads[1].wait()
+        rows = matmul(normed[...], w_query[...]) + bias_ref[0:1, : 3 * HD]
+        for h in range(3):
+            query[h] = turn(rows[:, h * HD : (h + 1) * HD], cosine[...], sine[...]).astype(
+                jnp.bfloat16
+            )
+        own_blocks[0].wait()
+        begin_spread(0)
+        for copy, i in ((pair_1, 2), (pair_2, 1), (pair_3, 3)):
+            copy.wait_recv()
+            started(pair_near[i], pair_core[i])
+
+        def flip(a, carry):
+            turned[:, rows_of(a)] = normed[rows_of(a), :].T
+            return carry
+
+        lax.fori_loop(0, 4, flip, 0)
+        for p in range(4):
+            own_a[N1, p * block : (p + 1) * block, :] = turned[row_block(0, p // 2, p % 2), :]
+        for i in (0, 2, 1, 3):
+            pair_near[i].wait_recv()
+            pair_core[4 + i].start()
+        x_copy(0, 0).start()
+        n1_keep.start()
+        n1_keep.wait()
+        started(*n1_x)
+        for copy in pair_core:
+            copy.wait_recv()
+
+    pl.run_scoped(
+        opening,
+        pltpu.VMEM((TOK, width), jnp.bfloat16),
+        pltpu.VMEM((TOK, width), jnp.bfloat16),
+        pltpu.VMEM((TOK, width), jnp.bfloat16),
+        pltpu.VMEM((width, 3 * HD), jnp.bfloat16),
+        pltpu.VMEM((width, HD), jnp.bfloat16),
+    )
+
+    def of_first(t):
+        late = t // 8
+        device = t * (1 - late) + (15 - t) * late
+        return device, late * (TOK - HALF)
+
+    def of_middle(t):
+        return t, HALF
+
+    def rows_at(t, locate, count):
+        device, offset = locate(t)
+        slot = (
+            4 * ((device % 2 + b0) % 2)
+            + 2 * (((device // 2) % 2 + b1) % 2)
+            + (device // 4 + b2) % 2
+        )
+        return device, slot, pl.ds(pl.multiple_of(offset, HALF), count)
+
+    def same_document(device):
+        return docs_ref[pl.ds(device, 1), :] == docs_ref[pl.ds(me, 1), :]
+
+    def attend_region(begin, count, blocks, locate, shared):
+        rows = 3 * count
+        q_rows = region_rows(query, begin, count)
+
+        def score(t, diagonal=False):
+            device, slot, place = rows_at(t, locate, count)
+            scores = contract_cols(q_rows, pair[0, slot, place, :])
+            if diagonal:
+                return jnp.where(triangle(rows, count), scores, MASKED)
+            if shared:
+                return jnp.where(same_document(device), scores, MASKED)
+            return scores
+
+        def add(t, carry, scores):
+            _, slot, place = rows_at(t, locate, count)
+            total, accum = carry
+            weights = jnp.exp2(scores * factor - peak)
+            return total + weights, accum + matmul(
+                weights.astype(jnp.bfloat16), pair[1, slot, place, :]
+            )
+
+        last = score(blocks, True)
+        peak = lax.fori_loop(0, blocks, lambda t, top: jnp.maximum(top, score(t)), last)
+        peak = jnp.max(peak, axis=1, keepdims=True) * factor
+        carry = add(
+            blocks, (jnp.zeros((rows, count), jnp.float32), jnp.zeros((rows, HD), jnp.float32)), last
+        )
+        total, accum = lax.fori_loop(0, blocks, lambda t, held: add(t, held, score(t)), carry)
+        total = jnp.sum(total, axis=1, keepdims=True)
+        result = accum / total
+        logs = jnp.broadcast_to(peak + jnp.log2(total), (rows, HD))
+        for h in range(3):
+            part = slice(h * count, (h + 1) * count)
+            attn_all[0, begin : begin + count, h * HD : (h + 1) * HD] = result[part].astype(
+                jnp.bfloat16
+            )
+            full[h, begin : begin + count, :] = result[part]
+            log_total[h, begin : begin + count, :] = logs[part]
+
+    def front(weights, ring, wo, x_rows, cot_turned):
         def fetch(t, slot, rows):
             return [
                 pltpu.make_async_copy(
@@ -603,12 +830,34 @@
                 for k, source in enumerate((wg_hbm, wu_hbm, wd_hbm))
             ]
 
-        loads = [local(wo_hbm, wo), local(x_hbm, x_rows), local(cot_turned_hbm, cot_turned)]
-        started(*loads)
+        loads = [
+            local(wo_hbm, wo.at[0]),
+            local(x_hbm, x_rows),
+            local(wo_all.at[2], wo.at[2]),
+            local(wo_all.at[1], wo.at[1]),
+            local(wo_all.at[3], wo.at[3]),
+            local(all_hbm.at[0, me], cot_turned),
+        ]
+        wo_c.wait_recv()
+        started(*loads[:3], loads[5])
         started(*fetch(0, 0, UNITS))
-        loads[0].wait()
-        loads[1].wait()
-
+        attend_region(0, HALF, me, of_first, False)
+        attend_region(TOK - HALF, HALF, 15 - me, of_first, False)
+        wo_y.wait_recv()
+        wo_cy.start()
+        loads[3].start()
+        attend_region(HALF, TOK - 2 * HALF, me, of_middle, True)
+        started(attn_y, attn_c)
+        wo_cy.wait_recv()
+        loads[4].start()
+        arrive(0, 1)
+        arrive_inner(0, 2)
+        started(attn_x)
+        pass_y(0, 0)
+        for load in loads[:4]:
+            load.wait()
+        for copy in (pair_1, pair_2, pair_3, *pair_near, *pair_core):
+            copy.wait_send()
         def add_part(p, first=False):
             def body(n, carry):
                 cols = pl.ds(pl.multiple_of(n * 512, 512), 512)
@@ -618,7 +867,6 @@
 
             lax.fori_loop(0, width // 512, body, 0)
 
-        attn_own.wait()
         add_part(0, True)
         attn_c.wait_recv()
         add_part(2)
@@ -626,18 +874,20 @@
         started(attn_cy)
         add_part(1)
         attn_cy.wait_recv()
+        loads[4].wait()
         add_part(3)
 
         def norm(a, carry):
             rows = middle[rows_of(a), :]
-            turned[:, rows_of(a)] = (rows * norm_scale(rows) * gain).astype(jnp.bfloat16).T
+            turned[:, rows_of(a)] = (rows * norm_scale(rows) * gain2).astype(jnp.bfloat16).T
             return carry
 
         lax.fori_loop(0, 4, norm, 0)
-        started(*n2_x)
-        for p in range(4):
-            own_a[N2, p * block : (p + 1) * block, :] = turned[row_block(0, p // 2, p % 2), :]
-        loads[2].wait()
+        own_blocks[1].start()
+        own_blocks[1].wait()
+        begin_spread(1)
+        x_copy(1, 0).start()
+        loads[5].wait()
         acc[...] = jnp.zeros_like(acc)
 
         def keep_tile(t):
@@ -693,25 +943,34 @@
             def _():
                 keep_tile(t - 1).wait()
 
-            @pl.when((t > 0) & (t <= AHEAD))
+            @pl.when(t == 3)
             def _():
-                x_tile(t - 1).start()
+                arrive_outer(0, 2)
+                arrive_inner(0, 3)
+                pass_core(0, 0)
+                pass_y(0, 1)
+
+            @pl.when(t == 7)
+            def _():
+                arrive(1, 1)
+                arrive_inner(1, 2)
+                pass_y(1, 0)
+                pass_core(0, 1)
 
             keep_tile(t).start()
             return carry
 
         lax.fori_loop(0, tiles, tile, 0)
         keep_tile(tiles - 1).wait()
-        for copy in n2_x:
-            copy.wait_send()
+        x_tile.start()
 
     pl.run_scoped(
         front,
         pltpu.VMEM((2, 3, UNITS, width), jnp.bfloat16),
-        pltpu.VMEM((width, TOK), jnp.bfloat16),
         pltpu.VMEM((2, TOK, 3 * UNITS), jnp.bfloat16),
         pltpu.VMEM((4, width // 4, width), jnp.bfloat16),
         pltpu.VMEM((TOK, width), jnp.bfloat16),
+        pltpu.VMEM((width, TOK), jnp.bfloat16),
     )
 
     def reduce_start(total, sent, core_to):
@@ -758,89 +1017,53 @@
         copies[1].wait()
         copies[2].wait()
 
-    def first_product(a, b_own, b_far, h, index):
-        return matmul(own_a[index, h * half : (h + 1) * half, :], b_own) + matmul(
-            far_a[index, h], b_far
-        )
-
-    tile_loads = {}
-
-    def load_own(t):
-        tile_loads[t] = started(local(own_hbm.at[t], stage.at[t % 2]))
-
-    def first_step(t):
-        slot = t % 2
-        if t not in tile_loads:
-            load_own(t)
-        x_tile(t).wait_recv()
-        far_load = started(local(far_hbm.at[t], far_stage))
-        if t + AHEAD < tiles:
-            x_tile(t + AHEAD).start()
-        tile_loads[t].wait()
-        far_load.wait()
-        if t >= 2:
-            z1_tile(t - 2).wait_send()
-
-        def body(n, h):
-            cols = pl.ds(pl.multiple_of(n * UNITS, UNITS), UNITS)
-            index = (n + 1) // 2
-            return cols, matmul(
-                own_a[index, h * half : (h + 1) * half, :], stage[slot, :, cols]
-            ) + matmul(far_a[index, h], far_stage[:, cols])
-
-        def sent(n, carry):
-            cols, value = body(n, 1)
-            part_s[slot, :, cols] = value.astype(jnp.bfloat16)
-            return carry
-
-        def kept(n, carry):
-            cols, value = body(n, 0)
-            part_k[slot, :, cols] = value.astype(jnp.bfloat16)
-            return carry
-
-        lax.fori_loop(0, 3, sent, 0)
-        z1_tile(t).start()
-        lax.fori_loop(0, 3, kept, 0)
-        if t + 1 < tiles:
-            load_own(t + 1)
-
-    def second_step(t):
-        slot = t % 2
-        z1_tile(t).wait_recv()
-        load = started(local(near1_hbm.at[t], near1))
-        load.wait()
-        if t >= 2:
-            z2_tile(t - 2).wait_send()
-        part_s2[slot] = (
-            part_k[slot, block:, :].astype(jnp.float32) + near1[block:, :].astype(jnp.float32)
-        ).astype(jnp.bfloat16)
-        z2_tile(t).start()
-        part_f[slot] = part_k[slot, :block, :].astype(jnp.float32) + near1[:block, :].astype(
-            jnp.float32
-        )
-
-    final_copies = {}
-
-    def third_step(t):
-        slot = t % 2
-        z2_tile(t).wait_recv()
-        load = started(local(near2_hbm.at[t], near2))
-        load.wait()
-        if t >= 2:
-            final_copies[t - 2].wait()
-        final[slot] = part_f[slot] + near2[...].astype(jnp.float32)
-        final_copies[t] = started(local(final.at[slot], tiles_out.at[t]))
-
-    def step(t):
-        if t < tiles:
-            first_step(t)
-        if 0 <= t - 1 < tiles:
-            second_step(t - 1)
-        if 0 <= t - 2 < tiles:
-            third_step(t - 2)
+    near_base = used["remote"]
+    used["remote"] += 4
+    near_loads = [local(near_hbm.at[r], near_stage) for r in range(4)]
+
+    def near_copy(r):
+        index = near_base + r
+        return pltpu.make_async_remote_copy(
+            src_ref=sent_tile.at[rows_of_block(peers[r] - 4 * b2)], dst_ref=near_hbm.at[r],
+            send_sem=send_sem.at[index], recv_sem=recv_sem.at[index],
+            device_id={"cp": peers[r]}, device_id_type=pl.DeviceIdType.MESH,
+        )
+
+    final_base = used["local"]
+    used["local"] += 3
+
+    def final_copies(t):
+        return [
+            pltpu.make_async_copy(
+                final.at[:, pl.ds(k * UNITS, UNITS)],
+                tiles_out.at[k, :, pl.ds(pl.multiple_of(t * UNITS, UNITS), UNITS)],
+                local_sem.at[final_base + k],
+            )
+            for k in range(3)
+        ]
+
+    def finish_tile(t, value):
+        final[...] = value
+        started(*final_copies(t))
+        for copy in final_copies(t):
+            copy.wait()
 
     SMALL = {"out": (0, 384, GB), "query": (384, 384, N1), "pair": (768, 128, N1)}
-    small_copies = {}
+    small_base = used["remote"]
+    used["remote"] += 6
+
+    def small_copy(name, second):
+        begin, wide, _ = SMALL[name]
+        index = small_base + 2 * list(SMALL).index(name) + second
+        cols = pl.ds(begin, wide)
+        if second:
+            src, dst, to = small_s2.at[:, cols], small_in2.at[:, cols], z2_to
+        else:
+            src, dst, to = small_s.at[pl.ds(half, half), cols], small_in.at[:, cols], z1_to
+        return pltpu.make_async_remote_copy(
+            src_ref=src, dst_ref=dst, send_sem=send_sem.at[index], recv_sem=recv_sem.at[index],
+            device_id=to, device_id_type=pl.DeviceIdType.MESH,
+        )
 
     def small_first(name, b_own, b_far):
         begin, wide, index = SMALL[name]
@@ -848,9 +1071,7 @@
         small_s[half:, cols] = (
             matmul(own_a[index, half:, :], b_own) + matmul(far_a[index, 1], b_far)
         ).astype(jnp.bfloat16)
-        copy = remote(small_s.at[pl.ds(half, half), pl.ds(begin, wide)], small_in.at[:, pl.ds(begin, wide)], z1_to)
-        copy.start()
-        small_copies[name] = copy
+        small_copy(name, 0).start()
         small_s[:half, cols] = (
             matmul(own_a[index, :half, :], b_own) + matmul(far_a[index, 0], b_far)
         ).astype(jnp.bfloat16)
@@ -858,68 +1079,180 @@
     def small_second(name):
         begin, wide, _ = SMALL[name]
         cols = slice(begin, begin + wide)
-        small_copies[name].wait_recv()
+        small_copy(name, 0).wait_recv()
         small_s2[:, cols] = (
             small_s[block:half, cols].astype(jnp.float32)
             + small_in[block:, cols].astype(jnp.float32)
         ).astype(jnp.bfloat16)
-        copy = remote(small_s2.at[:, pl.ds(begin, wide)], small_in2.at[:, pl.ds(begin, wide)], z2_to)
-        copy.start()
-        small_copies[name].wait_send()
-        small_copies[name] = copy
+        small_copy(name, 1).start()
+        small_copy(name, 0).wait_send()
 
     def small_third(name, out_ref):
         begin, wide, _ = SMALL[name]
         cols = slice(begin, begin + wide)
-        small_copies[name].wait()
+        small_copy(name, 1).wait()
         out_ref[...] = (
             small_s[:block, cols].astype(jnp.float32)
             + small_in[:block, cols].astype(jnp.float32)
             + small_in2[:, cols].astype(jnp.float32)
         )
 
-    def rest_of(cot, query, pair, full, log_total, cosine, sine, grads, incoming, wo_own):
-        loads = [
-            local(cot_hbm, cot),
-            local(q_hbm, query),
-            local(pair_hbm, pair),
-            local(full_hbm, full),
-            local(log_hbm, log_total),
-            local(cos_hbm, cosine),
-            local(sin_hbm, sine),
-            local(wo_hbm.at[0], wo_own),
+    query_x = remote(grad_query, query_far, x_to)
+    query_y = remote(grad_query, query_hbm.at[1], y_to)
+    query_c = remote(grad_query, query_hbm.at[2], c_to)
+    query_cy = remote(query_hbm.at[1], query_hbm.at[3], c_to)
+    query_own = local(grad_query, query_hbm.at[0])
+    pair_x = remote(grad_pair, pair_far, x_to)
+    pair_y = remote(grad_pair, pair_hbm.at[1], y_to)
+    pair_c = remote(grad_pair, pair_hbm.at[2], c_to)
+    pair_cy = remote(pair_hbm.at[1], pair_hbm.at[3], c_to)
+    pair_own = local(grad_pair, pair_hbm.at[0])
+    here = output_out.at[rows_of(lane)]
+    there = output_out.at[rows_of(lane_y)]
+    out_spread = [
+        remote(grad_full.at[rows_of(lane)], here, y_to),
+        remote(grad_full.at[rows_of(lane)], here, c_to),
+        remote(there, there, c_to),
+    ]
+    out_own = local(grad_full.at[rows_of(lane)], here)
+
+    def rest_of(grads, wo_own, second, cots, weights, ring, total_tile):
+        mine = [b0 + 2 * b1 + 4 * i for i in range(2)]
+        weight_loads = [
+            local(source.at[pl.ds(pl.multiple_of(tile * UNITS, UNITS), UNITS)], weights.at[i, k])
+            for i, tile in enumerate(mine)
+            for k, source in enumerate((wg_hbm, wu_hbm, wd_hbm))
         ]
-        started(*loads)
+        wo_load = local(wo_hbm, wo_own)
+        started(*weight_loads, wo_load)
+        block_base = used["local"]
+        used["local"] += 4
+        own_tiles = [local(own_hbm.at[tile], ring) for tile in mine]
+        own_rows = pl.ds(pl.multiple_of(b2 * wide_half, wide_half), wide_half)
+
+        def block_loads(j, side):
+            slot = (2 * j + side) % 2
+            return [
+                pltpu.make_async_copy(
+                    all_hbm.at[k, block_of(j, side)], ref.at[slot], local_sem.at[block_base + 2 * slot + k]
+                )
+                for k, ref in ((0, cots), (1, second))
+            ]
+
+        def prefetch(j, side):
+            if side:
+                d_copy(0, j, 1 - core).wait_recv()
+                d_copy(1, j, 1 - core).wait_recv()
+            elif j:
+                c_copy(0, j, 1 - core).wait_recv()
+                c_copy(1, j, 1 - core).wait_recv()
+            started(*block_loads(j, side))
+
+        def product(j, side):
+            slot = (2 * j + side) % 2
+            loads = block_loads(j, side)
+            first = j == 0 and side == 0
+            loads[1].wait()
+            for i in range(2):
+                if first:
+                    own_tiles[i].start()
+                    own_tiles[i].wait()
+                    if i == 0:
+                        loads[0].wait()
+                else:
+                    gate = matmul(weights[i, 0], second[slot])
+                    up_part = matmul(weights[i, 1], second[slot])
+                    sigma = jax.nn.sigmoid(gate)
+                    swish = gate * sigma
+                    ring[:, :UNITS] = (swish * up_part).astype(jnp.bfloat16).T
+                    if i == 0:
+                        loads[0].wait()
+                    grad_hidden = matmul(weights[i, 2], cots[slot])
+                    ring[:, UNITS : 2 * UNITS] = (
+                        (grad_hidden * up_part * sigma * (1.0 + gate * (1.0 - sigma)))
+                        .astype(jnp.bfloat16)
+                        .T
+                    )
+                    ring[:, 2 * UNITS :] = (grad_hidden * swish).astype(jnp.bfloat16).T
+                for n, rows in enumerate((cots, second, second)):
+                    cols = slice(n * UNITS, (n + 1) * UNITS)
+                    total_cols = slice((3 * i + n) * UNITS, (3 * i + n + 1) * UNITS)
+                    value = matmul(rows[slot, own_rows, :], ring[:, cols])
+                    if first:
+                        total_tile[:, total_cols] = value
+                    else:
+                        total_tile[:, total_cols] += value
+
+        far_loads = [
+            local(
+                all_hbm.at[k, block_of(0, side), row_block(0, p // 2, p % 2)],
+                (far_a.at[k, p // 2, pl.ds((p % 2) * block, block)] if side else own_a.at[k, pl.ds(p * block, block)]),
+            )
+            for k in range(2)
+            for side in range(2)
+            for p in range(4)
+        ]
+        stage, far_stage = sent_tile.at[:TOK, : 3 * UNITS], sent_tile.at[:TOK, 3 * UNITS :]
+        last_loads = [local(own_hbm.at[tiles - 1], stage), local(far_hbm, far_stage)]
+
+        def last_first():
+            x_tile.wait_recv()
+            started(*far_loads, *last_loads)
+            for load in (*far_loads, *last_loads):
+                load.wait()
+
+            def body(n, h):
+                cols = pl.ds(pl.multiple_of(n * UNITS, UNITS), UNITS)
+                far_cols = pl.ds(pl.multiple_of((3 + n) * UNITS, UNITS), UNITS)
+                index = (n + 1) // 2
+                return cols, matmul(
+                    own_a[index, h * half : (h + 1) * half, :], sent_tile[:TOK, cols]
+                ) + matmul(far_a[index, h], sent_tile[:TOK, far_cols])
+
+            def sent(n, carry):
+                cols, value = body(n, 1)
+                part_s[:, cols] = value.astype(jnp.bfloat16)
+                return carry
+
+            def kept(n, carry):
+                cols, value = body(n, 0)
+                part_k[:, cols] = value
+                return carry
+
+            lax.fori_loop(0, 3, sent, 0)
+            z1_tile.start()
+            lax.fori_loop(0, 3, kept, 0)
+
         copies = reduce_start(acc, rel, core_in)
-        forwards = []
-        for index, parts in ((COT, cot_x), (N1, n1_x), (N2, n2_x)):
-            for copy in parts:
-                copy.wait_recv()
-            forwards.append(started(forward(index)))
+        prefetch(0, 0)
+        for load in weight_loads:
+            load.wait()
         lane_copy = reduce_middle(acc, copies, core_in, lane_in)
-        for load in own_loads:
-            load.wait()
-        for copy in forwards:
-            copy.wait()
-        step(0)
+        product(0, 0)
+        pass_core(1, 0)
+        arrive_outer(0, 3)
         grad_full[rows_of(lane), :] = reduce_end(acc, lane_copy, core_in, lane_in).astype(
             jnp.bfloat16
         )
         spread = spread_start(grad_full)
-        for copy in cot_x + n1_x:
-            copy.wait_send()
+        cot_load = started(local(cot_hbm, rel))
+        prefetch(0, 1)
+        pass_y(0, 2)
+        pass_y(1, 1)
+        product(0, 1)
+        arrive_inner(1, 3)
         grads[...] = jnp.zeros_like(grads)
         spread_end(spread)
-        for load in loads:
-            load.wait()
+        cot_load.wait()
+        wo_load.wait()
 
         def middle_back(a, total):
             grad = grad_full[rows_of(a), :].astype(jnp.float32)
             rows = middle[rows_of(a), :]
             factor2 = norm_scale(rows)
-            weighted = grad * gain
+            weighted = grad * gain2
             result = (
-                cot[rows_of(a), :].astype(jnp.float32)
+                rel[rows_of(a), :].astype(jnp.float32)
                 + factor2 * weighted
                 - rows * factor2**3 * jnp.mean(weighted * rows, axis=-1, keepdims=True)
             )
@@ -927,31 +1260,30 @@
             turned[:, rows_of(a)] = result.astype(jnp.bfloat16).T
             return total + jnp.sum(grad * rows * factor2, axis=0, keepdims=True)
 
-        gain_out[...] = lax.fori_loop(0, 4, middle_back, jnp.zeros((1, width), jnp.float32))
-        middle_copy = started(local(acc, middle_out))
+        sums[...] = jnp.zeros_like(sums)
+        sums[0, 1:2, :] = lax.fori_loop(
+            0, 4, middle_back, jnp.zeros((1, width), jnp.float32)
+        )
+        middle_copy = started(local(acc, middle_hbm))
         branch_x = share(turned, GB)
-        started(*branch_x)
-        incoming[...] = matmul(wo_own[...], turned[...]).astype(jnp.bfloat16).T
+        pass_core(0, 2)
+        attn_cy.wait_send()
+        attn_all[1] = matmul(wo_own[...], turned[...]).astype(jnp.bfloat16).T
         for p in range(4):
             own_a[GB, p * block : (p + 1) * block, :] = turned[row_block(0, p // 2, p % 2), :]
-        step(1)
-
-        sign = jnp.where(lax.broadcasted_iota(jnp.int32, (1, HD), 1) < HD // 2, 1.0, -1.0)
-
-        def of_first(t):
-            late = t // 8
-            device = t * (1 - late) + (15 - t) * late
-            return device, late * (TOK - HALF)
-
-        def of_middle(t):
-            return t, HALF
+        arrive_outer(1, 2)
+        prefetch(1, 0)
+        product(1, 0)
+        pass_core(1, 1)
+        pass_core(0, 3)
+        last_first()
 
         def region(begin, count, blocks, locate, shared):
             heads = query.shape[0]
             rows = heads * count
             q_rows = region_rows(query, begin, count)
             grad_rows = jnp.concatenate(
-                [incoming[begin : begin + count, h * HD : (h + 1) * HD] for h in range(heads)], 0
+                [attn_all[1, begin : begin + count, h * HD : (h + 1) * HD] for h in range(heads)], 0
             )
             logs = region_rows(log_total, begin, count)[:, :1]
             delta = jnp.sum(
@@ -961,20 +1293,13 @@
             )
 
             def add(t, carry, diagonal=False):
-                device, offset = locate(t)
-                slot = (
-                    4 * ((device % 2 + b0) % 2)
-                    + 2 * (((device // 2) % 2 + b1) % 2)
-                    + (device // 4 + b2) % 2
-                )
-                place = pl.ds(pl.multiple_of(offset, HALF), count)
+                device, slot, place = rows_at(t, locate, count)
                 keys, values = pair[0, slot, place, :], pair[1, slot, place, :]
                 probs = jnp.exp2(contract_cols(q_rows, keys) * factor - logs)
                 if diagonal:
                     probs = jnp.where(triangle(rows, count), probs, 0.0)
                 elif shared:
-                    same = docs_ref[pl.ds(device, 1), :] == docs_ref[pl.ds(me, 1), :]
-                    probs = jnp.where(same, probs, 0.0)
+                    probs = jnp.where(same_document(device), probs, 0.0)
                 grad_scores = (probs * (contract_cols(grad_rows, values) - delta)).astype(
                     jnp.bfloat16
                 )
@@ -988,15 +1313,18 @@
             for h in range(heads):
                 part = total[h * count : (h + 1) * count]
                 grad_query[begin : begin + count, h * HD : (h + 1) * HD] = (
-                    part * cosines + pltpu.roll(part * sines, HD // 2, 1) * sign
+                    turn_back(part, cosines, sines)
                 ).astype(jnp.bfloat16)
 
         region(0, HALF, me, of_first, False)
         region(TOK - HALF, HALF, 15 - me, of_first, False)
-        step(2)
+        prefetch(1, 1)
+        product(1, 1)
+        prefetch(2, 0)
+        arrive_outer(1, 3)
+        pass_core(1, 2)
         region(HALF, TOK - 2 * HALF, me, of_middle, True)
 
-        is_key = jnp.where(core == 0, 1.0, 0.0)
         keep_by = is_key * scale + (1.0 - is_key)
         send_by = (1.0 - is_key) * scale + is_key
 
@@ -1006,53 +1334,88 @@
 
         lax.fori_loop(0, 8, to_core, 0)
         kv_c = remote(kv_send.at[pl.ds(0, 8)], kv_in.at[pl.ds(0, 8)], c_to)
-        kv_x = remote(kv_send.at[pl.ds(8, 4)], kv_in.at[pl.ds(8, 4)], x_to)
-        kv_1 = remote(kv_send.at[pl.ds(12, 2)], kv_in.at[pl.ds(12, 2)], z1_to)
-        kv_2 = remote(kv_send.at[pl.ds(14, 1)], kv_in.at[pl.ds(14, 1)], z2_to)
+        kv_x = remote(kv_send.at[pl.ds(0, 4)], kv_in.at[pl.ds(8, 4)], x_to)
+        kv_1 = remote(kv_send.at[pl.ds(4, 2)], kv_in.at[pl.ds(12, 2)], z1_to)
+        kv_2 = remote(kv_send.at[pl.ds(6, 1)], kv_in.at[pl.ds(14, 1)], z2_to)
         kv_c.start()
-        query_x = remote(grad_query, query_far, x_to)
-        query_y = remote(grad_query, query_out.at[1], y_to)
-        query_c = remote(grad_query, query_out.at[2], c_to)
-        query_cy = remote(query_out.at[1], query_out.at[3], c_to)
-        query_own = local(grad_query, query_out.at[0])
-        started(query_x, query_y, query_c, query_own)
+        started(query_y, query_c, query_own)
+        product(2, 0)
+        prefetch(2, 1)
+        kv_c.wait()
+
+        def from_core(s, carry):
+            grads[core, s] = grads[core, s] * keep_by + kv_in[s].astype(jnp.float32)
+            return carry
+
+        lax.fori_loop(0, 8, from_core, 0)
+
+        def pass_on(copy, first, count):
+            def cast(s, carry):
+                kv_send[first - 8 + s] = grads[core, count + s].astype(jnp.bfloat16)
+                return carry
+
+            lax.fori_loop(0, count, cast, 0)
+            copy.start()
+
+        def take(copy, first, count):
+            copy.wait()
+
+            def add(s, carry):
+                grads[core, s] += kv_in[first + s].astype(jnp.float32)
+                return carry
+
+            lax.fori_loop(0, count, add, 0)
+
+        pass_on(kv_x, 8, 4)
+        started(query_x, *branch_x, wq_y, wq_c)
+        product(2, 1)
+        prefetch(3, 0)
+        z1_tile.wait_recv()
+        part_s2[...] = (
+            part_k[block:, :] + near1[block:, :].astype(jnp.float32)
+        ).astype(jnp.bfloat16)
+        z2_tile.start()
+        product(3, 0)
+        take(kv_x, 8, 4)
+        pass_on(kv_1, 12, 2)
+        pass_core(1, 3)
+        prefetch(3, 1)
+        n1_forward = forward(N1)
+        for copy in n1_x:
+            copy.wait()
+        n1_forward.start()
+        product(3, 1)
+        sent_tile[...] = total_tile[...].astype(jnp.bfloat16)
+        take(kv_1, 12, 2)
+        pass_on(kv_2, 14, 1)
+        for r in (3, 1, 2):
+            near_copy(r).start()
+        query_y.wait_recv()
+        query_cy.start()
         for copy in branch_x:
             copy.wait()
         branch_c = started(forward(GB))
-        kv_c.wait()
-
-        def from_core(s, carry):
-            grads[core, s] = grads[core, s] * keep_by + kv_in[s].astype(jnp.float32)
-            return carry
-
-        lax.fori_loop(0, 8, from_core, 0)
-
-        def pass_on(copy, first, count):
-            def cast(s, carry):
-                kv_send[first + s] = grads[core, count + s].astype(jnp.bfloat16)
-                return carry
-
-            lax.fori_loop(0, count, cast, 0)
-            copy.start()
-
-        def take(copy, first, count):
-            copy.wait()
-
-            def add(s, carry):
-                grads[core, s] += kv_in[first + s].astype(jnp.float32)
-                return carry
-
-            lax.fori_loop(0, count, add, 0)
-
-        pass_on(kv_x, 8, 4)
-        step(3)
+        for i, tile in enumerate(mine):
+            finish_tile(
+                tile,
+                total_tile[
+                    rows_of_block(me - 4 * b2), i * 3 * UNITS : (i + 1) * 3 * UNITS
+                ],
+            )
         attn_x.wait()
         branch_c.wait()
         small_first("out", attn_all[0], attn_far[...])
-        query_y.wait_recv()
-        query_cy.start()
-        take(kv_x, 8, 4)
-        pass_on(kv_1, 12, 2)
+        query_x.wait()
+        n1_forward.wait()
+        small_first("query", grad_query[...], query_far[...])
+        kv_2.wait()
+        f_cos = cosine[...] * is_key + (1.0 - is_key)
+        f_sin = sine[...] * is_key
+        total = grads[core, 0] + kv_in[14].astype(jnp.float32)
+        grad_pair[...] = turn_back(total, f_cos, f_sin).astype(jnp.bfloat16)
+        started(pair_x, pair_y, pair_c, pair_own)
+        wq_y.wait_recv()
+        wq_cy.start()
 
         def down(weights, hidden):
             def fetch(t, slot, rows):
@@ -1108,114 +1471,209 @@
             pltpu.VMEM((2, UNITS, width), jnp.bfloat16),
             pltpu.VMEM((2, TOK, UNITS), jnp.bfloat16),
         )
-        out_copies = reduce_start(acc, rel, out_core_in)
-        step(4)
+        out_copies = reduce_start(acc, rel, core_in)
         small_second("out")
-        take(kv_1, 12, 2)
-        pass_on(kv_2, 14, 1)
-        out_lane = reduce_middle(acc, out_copies, out_core_in, out_lane_in)
-        query_x.wait()
-        small_first("query", grad_query[...], query_far[...])
-        step(5)
-        small_third("out", wo_out)
-        kv_2.wait()
-        f_cos = cosine[...] * is_key + (1.0 - is_key)
-        f_sin = sine[...] * is_key
-        total = grads[core, 0] + kv_in[14].astype(jnp.float32)
-        grad_pair[...] = (total * f_cos + pltpu.roll(total * f_sin, HD // 2, 1) * sign).astype(
-            jnp.bfloat16
-        )
-        pair_x = remote(grad_pair, pair_far, x_to)
-        pair_y = remote(grad_pair, pair_out.at[1], y_to)
-        pair_c = remote(grad_pair, pair_out.at[2], c_to)
-        pair_cy = remote(pair_out.at[1], pair_out.at[3], c_to)
-        pair_own = local(grad_pair, pair_out.at[0])
-        started(pair_x, pair_y, pair_c, pair_own)
-        out_rows = reduce_end(acc, out_lane, out_core_in, out_lane_in) + middle[rows_of(lane), :]
+        out_lane = reduce_middle(acc, out_copies, core_in, lane_in)
+        small_second("query")
+        z2_tile.wait_recv()
+        finish_tile(
+            tiles - 1,
+            part_k[:block, :]
+            + near1[:block, :].astype(jnp.float32)
+            + near2[...].astype(jnp.float32),
+        )
+        out_rows = reduce_end(acc, out_lane, core_in, lane_in) + middle[rows_of(lane), :]
         grad_full[rows_of(lane), :] = out_rows.astype(jnp.bfloat16)
-        here = output_out.at[rows_of(lane)]
-        there = output_out.at[rows_of(lane_y)]
-        out_spread = [
-            remote(grad_full.at[rows_of(lane)], here, y_to),
-            remote(grad_full.at[rows_of(lane)], here, c_to),
-            remote(there, there, c_to),
-        ]
-        out_own = local(grad_full.at[rows_of(lane)], here)
         started(out_spread[0], out_spread[1], out_own)
-        small_second("query")
-        step(6)
-        pair_x.wait()
-        small_first("pair", grad_pair[...], pair_far[...])
-        pair_y.wait_recv()
-        pair_cy.start()
-        small_third("query", wq_out)
-        out_spread[0].wait_recv()
-        out_spread[2].start()
-        step(7)
-        small_second("pair")
-        step(8)
-        small_third("pair", wp_out)
-        step(9)
-        step(10)
-        for t in (tiles - 2, tiles - 1):
-            z1_tile(t).wait_send()
-            z2_tile(t).wait_send()
-            final_copies[t].wait()
-        for t in range(tiles):
-            x_tile(t).wait_send()
-        for copy in (attn_y, attn_c, attn_cy, query_y, pair_y, out_spread[0]):
-            copy.wait_send()
-        for copy in (query_c, query_cy, pair_c, pair_cy, out_spread[1], out_spread[2]):
-            copy.wait()
-        for copy in (query_own, pair_own, out_own):
-            copy.wait()
 
     pl.run_scoped(
         rest_of,
+        pltpu.VMEM((2, 8, TOK, HD), jnp.float32),
+        pltpu.VMEM((width // 4, width), jnp.bfloat16),
+        pltpu.VMEM((2, width, TOK), jnp.bfloat16),
+        pltpu.VMEM((2, width, TOK), jnp.bfloat16),
+        pltpu.VMEM((2, 3, UNITS, width), jnp.bfloat16),
+        pltpu.VMEM((TOK, 3 * UNITS), jnp.bfloat16),
+        pltpu.VMEM((width // 2, 6 * UNITS), jnp.float32),
+    )
+    pair_x.wait()
+    small_first("pair", grad_pair[...], pair_far[...])
+    pair_y.wait_recv()
+    pair_cy.start()
+    out_spread[0].wait_recv()
+    out_spread[2].start()
+    small_third("out", wo_out)
+    pair_cy.wait_recv()
+    pair_c.wait_recv()
+    query_own.wait()
+    pair_own.wait()
+    query_c.wait_recv()
+    query_cy.wait_recv()
+    wq_c.wait_recv()
+    wq_cy.wait_recv()
+
+    def closing(x_rows, queries, pairs, w_queries, w_pairs):
+        loads = [
+            local(query_hbm, queries),
+            local(wq_all.at[pl.ds(1, 3)], w_queries.at[pl.ds(1, 3)]),
+            local(wq_hbm, w_queries.at[0]),
+            local(pair_hbm, pairs),
+            local(wk_hbm, w_pairs.at[0]),
+            local(wv_hbm, w_pairs.at[1]),
+            local(x_hbm, x_rows),
+            local(middle_hbm, middle),
+        ]
+        started(*loads)
+        for load in loads:
+            load.wait()
+
+        def part_of(n, carry):
+            cols = pl.ds(pl.multiple_of(n * 512, 512), 512)
+            total = jnp.zeros((TOK, 512), jnp.float32)
+            for p, far in enumerate(TP_ORDER):
+                kind = (core + far % 2) % 2
+                head = (high + far // 2) % 2
+                lanes = pl.ds(pl.multiple_of(head * HD, HD), HD)
+                total += contract_cols(queries[p], w_queries[p, cols, :])
+                total += contract_cols(pairs[p], w_pairs[kind, cols, lanes])
+            acc[:, cols] = total
+            return carry
+
+        lax.fori_loop(0, width // 512, part_of, 0)
+
+        def last(a, total):
+            grad = acc[rows_of(a), :]
+            rows = x_rows[rows_of(a), :].astype(jnp.float32)
+            scale1 = norm_scale(rows)
+            weighted = grad * gain1
+            rel[rows_of(a), :] = (
+                middle[rows_of(a), :]
+                + scale1 * weighted
+                - rows * scale1**3 * jnp.mean(weighted * rows, axis=-1, keepdims=True)
+            ).astype(jnp.bfloat16)
+            return total + jnp.sum(grad * rows * scale1, axis=0, keepdims=True)
+
+        gain1_part = lax.fori_loop(0, 4, last, jnp.zeros((1, width), jnp.float32))
+        copy = started(local(rel, input_out))
+        sums[0, 0:1, :] = gain1_part
+        sums[0, 2:3, : 3 * HD] = jnp.sum(
+            grad_query[...].astype(jnp.float32), axis=0, keepdims=True
+        )
+        sums[0, 2:3, 3 * HD : 4 * HD] = jnp.sum(
+            grad_pair[...].astype(jnp.float32), axis=0, keepdims=True
+        )
+        sums_copies[0].start()
+        copy.wait()
+
+    sums_copies = [
+        remote(sums.at[i], sums_in.at[i], to) for i, to in enumerate((x_to, z1_to, z2_to))
+    ]
+    pl.run_scoped(
+        closing,
         pltpu.VMEM((TOK, width), jnp.bfloat16),
-        pltpu.VMEM((3, TOK, HD), jnp.bfloat16),
-        pltpu.VMEM((2, 8, TOK, HD), jnp.bfloat16),
-        pltpu.VMEM((3, TOK, HD), jnp.float32),
-        pltpu.VMEM((3, TOK, HD), jnp.float32),
-        pltpu.VMEM((TOK, HD), jnp.float32),
-        pltpu.VMEM((TOK, HD), jnp.float32),
-        pltpu.VMEM((2, 8, TOK, HD), jnp.float32),
-        pltpu.VMEM((TOK, 3 * HD), jnp.bfloat16),
-        pltpu.VMEM((width // 4, width), jnp.bfloat16),
+        pltpu.VMEM((4, TOK, 3 * HD), jnp.bfloat16),
+        pltpu.VMEM((4, TOK, HD), jnp.bfloat16),
+        pltpu.VMEM((4, width, 3 * HD), jnp.bfloat16),
+        pltpu.VMEM((2, width, 2 * HD), jnp.bfloat16),
     )
+    sums_copies[0].wait()
+    sums[1] = sums[0] + sums_in[0]
+    sums_copies[1].start()
+    small_second("pair")
+    small_third("query", wq_out)
+
+    def take_near(r):
+        near_copy(r).wait_recv()
+        near_loads[r].start()
+        near_loads[r].wait()
+        for i in range(2):
+            finish_tile(
+                peers[r] - 4 * b2 + 4 * i,
+                near_stage[:, i * 3 * UNITS : (i + 1) * 3 * UNITS].astype(jnp.float32),
+            )
+
+    take_near(1)
+    take_near(2)
+    sums_copies[1].wait()
+    sums[2] = sums[1] + sums_in[1]
+    sums_copies[2].start()
+    take_near(3)
+    small_third("pair", wp_out)
+    sums_copies[2].wait()
+    sums_out[...] = sums[2] + sums_in[2]
+    x_tile.wait_send()
+    z1_tile.wait_send()
+    z2_tile.wait_send()
+    for r in (1, 2, 3):
+        near_copy(r).wait_send()
+    for k in range(2):
+        z_copy(k, 0).wait_send()
+
+        @when(inner)
+        def _():
+            for m in (1, 2, 3, 4):
+                z_copy(k, m).wait_send()
+
+        for j in range(4):
+            if j:
+                c_copy(k, j).wait_send()
+            x_copy(k, j).wait_send()
+            if (k, j) not in WHOLE_HALVES:
+                y_copy(k, j).wait_send()
+            d_copy(k, j).wait_send()
+    for copy in (
+        attn_y, attn_c, query_y, query_c, query_cy, pair_y, pair_c, pair_cy,
+        out_spread[0], wo_y, wo_c, wo_cy, wq_y, wq_c, wq_cy,
+    ):
+        copy.wait_send()
+    for copy in (out_spread[1], out_spread[2]):
+        copy.wait()
+    out_own.wait()
     assert used["remote"] <= REMOTE and used["local"] <= LOCAL, used
 
 
-AHEAD = 3
-REMOTE = 96
-LOCAL = 96
-
-
-def back(docs, gain, attn, full, log_total, query, pair, x, cot, normed1, cosine, sine, wo, wg, wu, wd):
+WHOLE_HALVES = ((0, 3), (1, 2), (1, 3))
+REMOTE = 134
+LOCAL = 130
+
+
+def whole_layer(
+    docs, gains, biases, cosine, sine, x, cot, w_query, w_key, w_value, w_out, w_gate, w_up, w_down
+):
     tok_rows, width = x.shape
-    units = wg.shape[0]
+    units = w_gate.shape[0]
     tiles = pl.cdiv(units, UNITS)
     half, block, quarter = width // 4, width // 8, tok_rows // 4
     low, wide = jnp.bfloat16, jnp.float32
     shape = jax.ShapeDtypeStruct
     any_ = pl.BlockSpec(memory_space=pl.ANY)
     outs = (
-        shape((tiles, block, 3 * UNITS), wide),
+        shape((3, block, tiles * UNITS), wide),
         shape((block, 384), wide),
         shape((block, 384), wide),
         shape((block, HD), wide),
-        shape((1, width), wide),
+        shape((8, width), wide),
+        shape((tok_rows, width), low),
         shape((tok_rows, width), low),
         shape((tok_rows, width), wide),
         shape((4, tok_rows, 384), low),
         shape((4, tok_rows, HD), low),
         shape((tiles, tok_rows, 3 * UNITS), low),
-        shape((tiles, tok_rows, 3 * UNITS), low),
-        shape((tiles, half, 3 * UNITS), low),
-        shape((tiles, block, 3 * UNITS), low),
+        shape((tok_rows, 3 * UNITS), low),
+        shape((4, block, 6 * UNITS), low),
+        shape((4,) + w_out.shape, low),
+        shape((4,) + w_query.shape, low),
+        shape((2, 8, width, tok_rows), low),
+        shape((width, tok_rows), low),
     )
     vmem = pltpu.VMEM
     scratch = [
+        vmem((3, tok_rows, HD), low),
+        vmem((2, 8, tok_rows, HD), low),
+        vmem((3, tok_rows, HD), wide),
+        vmem((3, tok_rows, HD), wide),
+        vmem((3, 8, width), wide),
+        vmem((3, 8, width), wide),
         vmem((4, tok_rows, 384), low),
         vmem((tok_rows, 384), low),
         vmem((tok_rows, 384), low),
@@ -1225,23 +1683,20 @@
         vmem((width, tok_rows), low),
         vmem((4, width // 2, tok_rows), low),
         vmem((4, 2, half, tok_rows), low),
-        vmem((2, tok_rows, 3 * UNITS), low),
-        vmem((tok_rows, 3 * UNITS), low),
-        vmem((2, half, 3 * UNITS), low),
-        vmem((2, half, 3 * UNITS), low),
-        vmem((2, block, 3 * UNITS), wide),
         vmem((half, 3 * UNITS), low),
-        vmem((2, block, 3 * UNITS), low),
+        vmem((half, 3 * UNITS), wide),
+        vmem((half, 3 * UNITS), low),
         vmem((block, 3 * UNITS), low),
-        vmem((2, block, 3 * UNITS), wide),
+        vmem((block, 3 * UNITS), low),
+        vmem((block, 6 * UNITS), low),
+        vmem((block, 3 * UNITS), wide),
+        vmem((width // 2, 6 * UNITS), low),
         vmem((tok_rows, width), low),
         vmem((2, quarter, width), low),
         vmem((quarter, width), low),
         vmem((quarter, width), low),
         vmem((tok_rows, width), low),
-        vmem((2, quarter, width), low),
-        vmem((quarter, width), low),
-        vmem((15, tok_rows, HD), low),
+        vmem((8, tok_rows, HD), low),
         vmem((15, tok_rows, HD), low),
         vmem((tok_rows, 384), low),
         vmem((tok_rows, HD), low),
@@ -1257,8 +1712,8 @@
     return pl.pallas_call(
         functools.partial(back_kernel, width, units),
         out_shape=outs,
-        in_specs=[VMEM, VMEM] + [any_] * 15,
-        out_specs=(any_, VMEM, VMEM, VMEM, VMEM) + (any_,) * 8,
+        in_specs=[VMEM] * 5 + [any_] * 9,
+        out_specs=(any_, VMEM, VMEM, VMEM, VMEM) + (any_,) * 12,
         scratch_shapes=scratch,
         compiler_params=pltpu.CompilerParams(
             vmem_limit_bytes=64 * 1024 * 1024, collective_id=0, has_side_effects=True
@@ -1266,7 +1721,7 @@
         cost_estimate=pl.CostEstimate(
             flops=20 * tok_rows * width * units, bytes_accessed=10 * width * units, transcendentals=0
         ),
-    )(docs, gain, attn, full, log_total, query, pair, x, cot, cot.T, normed1.T, cosine, sine, wo, wg, wu, wd)
+    )(docs, gains, biases, cosine, sine, x, cot, w_query, w_key, w_value, w_out, w_gate, w_up, w_down)
 
 
 def on_device(
@@ -1297,6 +1752,13 @@
     kv_index = lane * heads // (H // kv_heads)
     is_key = core == 0
 
+    def assemble(parts, axis):
+        at = lambda index: lax.dynamic_index_in_dim(parts, reverse_bits(lane ^ index, 2), 0, keepdims=False)
+        return (
+            jnp.concatenate([at(0), at(2)], axis),
+            jnp.concatenate([at(1), at(3)], axis),
+        )
+
     def finish(
         output, grad_middle, grad_normed1, grad_query, grad_pair, gain2_part,
         grad_w_query, grad_w_pair, grad_w_out, grad_w_gate, grad_w_up, grad_w_down,
@@ -1325,13 +1787,6 @@
         gain1_sum = small[:wide].reshape(-1)
         gain2_sum = small[wide : 2 * wide].reshape(-1)
         bias_query = small[2 * wide : 2 * wide + heads].reshape(-1)
-
-        def assemble(parts, axis):
-            at = lambda index: lax.dynamic_index_in_dim(parts, reverse_bits(lane ^ index, 2), 0, keepdims=False)
-            return (
-                jnp.concatenate([at(0), at(2)], axis),
-                jnp.concatenate([at(1), at(3)], axis),
-            )
 
         bias_key, bias_value = assemble(gather_tp(small[None, 2 * wide + heads], 0), 0)
         grad_w_key, grad_w_value = assemble(gather_tp(grad_w_pair[None], 0), 1)
@@ -1359,6 +1814,37 @@
     my_pos = lax.dynamic_slice_in_dim(positions, me * tok_rows, tok_rows)
     cosine, sine = rope_tables(my_pos, HD)
 
+    pair_bias = lax.dynamic_slice_in_dim(jnp.where(is_key, b_key, b_value), kv_index * HD, HD)
+
+    if shards == 8 and tok_rows == TOK:
+        tiles, grad_w_out, grad_w_query, grad_w_pair, sums, output, grad_input, *_ = whole_layer(
+            jnp.broadcast_to(middle_docs[:, None], (shards, 2 * HALF)),
+            jnp.stack([norm1_gain, norm2_gain]),
+            jnp.concatenate([b_query, pair_bias])[None],
+            cosine, sine, layer_input, cotangent, w_query, w_key, w_value, w_out,
+            w_gate.T, w_up.T, w_down,
+        )
+        units = w_gate.shape[1]
+        bias_query, bias_pair = sums[2, : heads * HD], sums[2, heads * HD : (heads + 1) * HD]
+        bias_key, bias_value = assemble(gather_tp(bias_pair[None], 0), 0)
+        grad_w_key, grad_w_value = assemble(gather_tp(grad_w_pair[None], 0), 1)
+        return (
+            output,
+            grad_input,
+            sums[0],
+            grad_w_query,
+            bias_query,
+            grad_w_key,
+            bias_key,
+            grad_w_value,
+            bias_value,
+            grad_w_out.T,
+            sums[1],
+            tiles[1, :, :units],
+            tiles[2, :, :units],
+            tiles[0, :, :units].T,
+        )
+
     inputs = layer_input.astype(jnp.float32)
     scale1 = lax.rsqrt(jnp.mean(inputs * inputs, axis=-1, keepdims=True) + EPSILON)
     normed1 = (inputs * scale1 * norm1_gain).astype(jnp.bfloat16)
@@ -1368,7 +1854,6 @@
         source = jnp.where(index % 2 == 0, w_key, w_value)
         return lax.dynamic_slice_in_dim(source, head * HD, HD, 1)
 
-    pair_bias = lax.dynamic_slice_in_dim(jnp.where(is_key, b_key, b_value), kv_index * HD, HD)
     pair_cos = jnp.where(is_key, cosine, 1.0)
     pair_sin = jnp.where(is_key, sine, 0.0)
     pair_pre = matmul(normed1, pair_weight(lane)) + pair_bias
@@ -1388,36 +1873,6 @@
     attn, attn_full, log_total, pair = attend(place, query, pair, other)
     w_out_all = gather_tp(w_out, 0)
     w_query_all = gather_tp(w_query, 1)
-    if shards == 8 and tok_rows == TOK:
-        (
-            tiles, grad_w_out, grad_w_query, grad_w_pair, gain2_part, output, grad_middle,
-            queries_all, pairs_all, *_,
-        ) = back(
-            jnp.broadcast_to(middle_docs[:, None], (shards, 2 * HALF)),
-            norm2_gain[None],
-            attn, attn_full, log_total, query, pair, layer_input, cotangent, normed1,
-            cosine, sine, w_out_all.reshape(4, -1, width), w_gate.T, w_up.T, w_down,
-        )
-        grad_w_out = grad_w_out.T
-        gain2_part = gain2_part[0]
-        grad_query, grad_pair = queries_all[0], pairs_all[0]
-        units = w_gate.shape[1]
-
-        def columns(kind):
-            part = tiles[:, :, kind * UNITS : (kind + 1) * UNITS]
-            return part.transpose(1, 0, 2).reshape(part.shape[1], -1)[:, :units]
-
-        grad_w_down, grad_w_gate, grad_w_up = columns(0).T, columns(1), columns(2)
-        grad_normed1 = sum(
-            contract_cols(queries_all[i], w_query_all[:, i * heads * HD : (i + 1) * heads * HD])
-            for i in range(4)
-        )
-        for i, far in enumerate(TP_ORDER):
-            grad_normed1 = grad_normed1 + contract_cols(pairs_all[i], pair_weight(lane ^ far))
-        return finish(
-            output, grad_middle, grad_normed1, grad_query, grad_pair, gain2_part,
-            grad_w_query, grad_w_pair, grad_w_out, grad_w_gate, grad_w_up, grad_w_down,
-        )
     cot_shared = share(place, cotangent, shards)
     normed1_shared = share(place, normed1, shards)
 

time: 476 us -> 316 us (0.66)
  Pallas kernels: 335 us -> 282 us
  local copies, waits for them, and re-layouts: 44.1 us -> 15.3 us
  other arithmetic: 32 us -> 7.89 us
  waiting for transfers between devices: 22 us -> 1.23 us
  matrix products: 19.7 us -> 0 us
  starting transfers between devices: 14.1 us -> 2.34 us
    pallas_call x2 -> x1, Pallas kernels: 335 us -> 282 us  [whole_layer(): pl.pallas_call(functools.partial(back_kernel, width, units), out_shape=ou...]
    ppermute x15 -> x4, waiting for transfers between devices: 22 us -> 1.23 us  [swap(): return lax.ppermute(value, axis, [(i, i ^ bit) for i in range(size)])]
    dot_general x10 -> x0, matrix products: 19.7 us -> none  [the longest x8 15.7 us: contract_cols(): lax.dot_general(left, right, (((1,), (1,)), ((), ())), preferred_element_...]
    unnamed x93 -> x14, local copies, waits for them, and re-layouts: 18.3 us -> 3.73 us
    ppermute x15 -> x4, starting transfers between devices: 14.1 us -> 2.34 us  [swap(): return lax.ppermute(value, axis, [(i, i ^ bit) for i in range(size)])]
    transpose x5 -> x1, local copies, waits for them, and re-layouts: 11.3 us -> 5.06 us  [on_device(): tiles[0, :, :units]]
    concatenate x4 -> x2, other arithmetic: 6.09 us -> 0.02 us  [gather_tp(): value = jnp.concatenate([value, swap(value, 'tp', 2)], axis)]
  transfers between devices with their start and end apart: 15 -> 4, of which waited for: 6 -> 2; matrix products, arithmetic and copies ran while one was open for 17% -> 3% of each run, Pallas kernels for 71% -> 0%
where the time goes in v3:
time: 316 us; the launch traced here: 310 us
  Pallas kernels  282 us (89%)
  local copies, waits for them, and re-layouts  15.3 us (5%)
  other arithmetic  7.89 us (2%)
    pallas_call x1, Pallas kernels, whole_layer(): pl.pallas_call(functools.partial(back_kernel, width, units), out_shape=ou...  282 us
  transfers between devices with their start and end apart: 4, of which 2 were waited for; matrix products, arithmetic and copies ran while one was open for 3% of the time, Pallas kernels for 0%

profile of v3, /device:TPU:0, one launch (start us, length us, event | category | flops | bytes accessed | tf_op | source)
XLA Modules:
  0.0 310.2 jit_solution(4084521639730009244)
XLA Ops:
  0.7 0.7 reshape.38
  1.6 0.7 stack.10
  2.3 0.7 stack.9
  3.0 0.7 broadcast_select_fusion
  3.7 1.3 pad_maximum_fusion.7
  5.0 0.8 dynamic-slice_convert_fusion
  5.8 1.0 multiply_sine_fusion
  6.7 1.0 pad_maximum_fusion.1
  7.7 0.6 pad_maximum_fusion.6.refs_1_
  8.4 0.7 broadcast_in_dim.16.refs_0_
  9.0 282.2 %shard_map.263 = (f32[3,192,2304]{2,1,0:T(8,128)}, f32[192,384]{1,0:T(8,128)}, f32[192,384]{1,0:T(8,128)}, f32[192,128]{1,0:T(8,128)}, f32[8,1536]{1,0:T(8,128)}...) custom-call(s32[8,256]{1,0:T(8,128)} %broadcast_in_dim.16.refs_0_, ...), custom_call_target="tpu_custom_call" | custom-call | flops 35232153600 | bytes 34406400 | tf_op jit(solution)/shard_map/pallas_call | solution.py:1712
  291.2 0.7 slice.27
  291.9 1.1 collective-permute-start.2
  293.0 0.9 collective-permute-start
  293.9 1.5 slice_reduce_fusion
  295.4 1.3 slice_reduce_fusion.3
  296.7 5.1 %slice_bitcast_fusion = (f32[2240,192]{0,1:T(8,128)}, f32[192,2240]{1,0:T(8,128)}, f32[192,2240]{1,0:T(8,128)}) fusion(f32[3,192,2304]{2,1,0:T(8,128)} %get-tuple-element.27), kind=kLoop, calls=%fused_computation | loop fusion | bytes 10321920 | tf_op jit(solution)/shard_map/transpose | solution.py:1845
  301.9 1.1 collective-permute-done.3
  304.7 0.7 pad_maximum_fusion.5
  305.4 0.7 pad_maximum_fusion.4
  306.1 1.1 copy.34
  307.2 1.1 copy.35
  308.4 0.7 copy.36
  309.1 0.7 copy.37
  (26 shorter events, 1.9 us)
Async XLA Ops:
  291.9 9.9 %collective-permute-start.2 = (f32[1,128]{1,0:T(1,128)S(1)}, f32[1,128]{1,0:T(1,128)S(1)}, u32[]{:S(2)}, u32[]{:S(2)}) collective-permute-start(f32[1,128]{1,0:T(1,128)S(1)} %slice.27), channel_id=1, source_target_pairs={{0,2},{1,3},{2,0},{3,1},{4,6},{5,7},{6,4},{7,5},{8,10},{9,11},{10,... | collective-permute-start | bytes 1544 | tf_op jit(solution)/shard_map/ppermute | solution.py:62
  293.0 10.0 %collective-permute-start = (f32[1,192,128]{2,1,0:T(8,128)}, f32[1,192,128]{2,1,0:T(8,128)S(1)}, u32[]{:S(2)}, u32[]{:S(2)}) collective-permute-start(f32[1,192,128]{2,1,0:T(8,128)} %bitcast.29), channel_id=1, source_target_pairs={{0,2},{1,3},{2,0},{3,1},{4,6},{5,7},{6,4},{7,5},{8,10},{9,11},{10,... | collective-permute-start | bytes 294920 | tf_op jit(solution)/shard_map/ppermute | solution.py:62
  296.7 6.3 %copy-start.2 = (f32[192,128]{1,0:T(8,128)S(1)}, f32[192,128]{1,0:T(8,128)}, u32[]{:S(2)}) copy-start(f32[192,128]{1,0:T(8,128)} %get-tuple-element.25) | copy-start | bytes 294916
  301.8 4.3 %copy-start.1 = (bf16[512,1536]{1,0:T(8,128)(2,1)S(1)}, bf16[512,1536]{1,0:T(8,128)(2,1)}, u32[]{:S(2)}) copy-start(bf16[512,1536]{1,0:T(8,128)(2,1)} %get-tuple-element.59) | copy-start | bytes 4718596
  301.8 1.2 collective-permute-start.3
  303.1 1.5 collective-permute-start.1
  305.4 1.8 copy-start
  307.2 1.1 copy-start.4
  307.2 1.9 copy-start.3

commit v4 on v3

--- a/solution.py
+++ b/solution.py
@@ -471,15 +471,15 @@
 
 def back_kernel(width, units, *refs):
     (
-        docs_ref, gain_ref, bias_ref, cosine, sine, x_hbm, cot_hbm, wq_hbm, wk_hbm, wv_hbm, wo_hbm,
+        docs_ref, pos_ref, freq_ref, gain1_ref, gain2_ref, bq_ref, bk_ref, bv_ref, x_hbm, cot_hbm, wq_hbm, wk_hbm, wv_hbm, wo_hbm,
         wg_hbm, wu_hbm, wd_hbm,
-        tiles_out, wo_out, wq_out, wp_out, sums_out, output_out, input_out,
-        middle_hbm, query_hbm, pair_hbm, own_hbm, far_hbm, near_hbm, wo_all, wq_all, all_hbm, n1_hbm,
-        query, pair, full, log_total, sums, sums_in,
+        tiles_out, wo_out, wq_out, wkv_out, sums_out, output_out, input_out,
+        middle_hbm, pair_hbm, own_hbm, near_hbm, wo_all, wq_turned_hbm, all_hbm, n1_hbm, via_hbm,
+        cosine, sine, gains, w_pair_grad, query, pair, full, log_total, sums, sums_in,
         attn_all, attn_far, query_far, pair_far, middle, acc, turned,
-        own_a, far_a, part_s, part_k, near1, part_s2, near2, near_stage, final, sent_tile,
+        own_a, far_a, part_s, part_k, near1, part_s2, near2, sent_tile,
         rel, core_in, lane_send, lane_in, grad_full,
-        kv_send, kv_in, grad_query, grad_pair, small_s, small_in, small_s2, small_in2,
+        held_query, kv_send, kv_in, grad_query, grad_pair, small_s, small_in, small_s2, small_in2, pair_terms,
         send_sem, recv_sem, local_sem, weight_sem,
     ) = refs
     me = lax.axis_index("cp")
@@ -499,6 +499,7 @@
     y_to = {"tp": lane + 2 - 4 * high}
     lane_c, lane_y = lane + 1 - 2 * core, lane + 2 - 4 * high
     lane_cy = 3 - lane
+    cy_to = {"tp": lane_cy}
     tiles = pl.cdiv(units, UNITS)
     rest = units - (tiles - 1) * UNITS
     block = width // 8
@@ -536,7 +537,6 @@
     def rows_of(index):
         return pl.ds(pl.multiple_of(index * quarter, quarter), quarter)
 
-    x_tile = remote(own_hbm.at[tiles - 1], far_hbm, x_to)
     z1_tile = remote(part_s, near1, z1_to)
     z2_tile = remote(part_s2, near2, z2_to)
 
@@ -549,24 +549,26 @@
         return 2 * z + (b0 + side) % 2
 
     def spread_part(k, j, side, c, y=None):
+        rows = half_of(c, y)
+        return all_hbm.at[k, block_of(j, side), rows]
+
+    def half_of(c, y=None):
         if y is None:
-            rows = pl.ds(pl.multiple_of(c * wide_half, wide_half), wide_half)
-        else:
-            rows = pl.ds(
-                pl.multiple_of(c * wide_half + y * wide_quarter, wide_quarter), wide_quarter
-            )
-        return all_hbm.at[k, block_of(j, side), rows]
-
-    def spread_copy(k, part, send, recv, to):
+            return pl.ds(pl.multiple_of(c * wide_half, wide_half), wide_half)
+        return pl.ds(pl.multiple_of(c * wide_half + y * wide_quarter, wide_quarter), wide_quarter)
+
+    def spread_copy(k, part, send, recv, to, source=None):
         index = spread_base + 20 * k
         return pltpu.make_async_remote_copy(
-            src_ref=part, dst_ref=part, send_sem=send_sem.at[index + send],
+            src_ref=part if source is None else source, dst_ref=part,
+            send_sem=send_sem.at[index + send],
             recv_sem=recv_sem.at[index + recv], device_id=to, device_id_type=pl.DeviceIdType.MESH,
         )
 
     def z_copy(k, m):
         j, recv, to = ((0, 1, z1_to), (0, 2, z3_to), (1, 3, z3_to), (2, 2, z1_to), (3, 3, z1_to))[m]
-        return spread_copy(k, spread_part(k, j, 0, core), m, recv, to)
+        own = turned.at[half_of(core)] if (k, j) == (1, 0) else None
+        return spread_copy(k, spread_part(k, j, 0, core), m, recv, to, own)
 
     def z_arrival(k, j):
         return spread_copy(k, spread_part(k, j, 0, core), 0, j, z1_to)
@@ -575,8 +577,9 @@
         return spread_copy(k, spread_part(k, j, 0, core if c is None else c), 4 + j, 4 + j, c_to)
 
     def x_copy(k, j, side=0):
-        part = spread_part(k, j, side, core, None if (k, j) in WHOLE_HALVES else high)
-        return spread_copy(k, part, 8 + j, 8 + j, x_to)
+        y = None if (k, j) in WHOLE_HALVES else high
+        own = turned.at[half_of(core, y)] if (k, j, side) == (1, 0, 0) else None
+        return spread_copy(k, spread_part(k, j, side, core, y), 8 + j, 8 + j, x_to, own)
 
     def y_copy(k, j, y=None):
         return spread_copy(
@@ -628,9 +631,8 @@
         d_copy(k, j).start()
 
     barrier = pltpu.get_barrier_semaphore()
-    for to in (*({"cp": peers[r]} for r in (1, 2, 3, 4, 6)), c_to, y_to):
+    for to in (*({"cp": peer} for peer in peers[1:]), c_to, y_to, cy_to):
         pl.semaphore_signal(barrier, inc=1, device_id=to, device_id_type=pl.DeviceIdType.MESH)
-    pl.semaphore_wait(barrier, 7)
 
     def share(source, index):
         return [
@@ -650,12 +652,15 @@
     wo_y = remote(wo_hbm, wo_all.at[1], y_to)
     wo_c = remote(wo_hbm, wo_all.at[2], c_to)
     wo_cy = remote(wo_all.at[1], wo_all.at[3], c_to)
-    wq_y = remote(wq_hbm, wq_all.at[1], y_to)
-    wq_c = remote(wq_hbm, wq_all.at[2], c_to)
-    wq_cy = remote(wq_all.at[1], wq_all.at[3], c_to)
-    attn_y = remote(attn_all.at[0], attn_all.at[1], y_to)
-    attn_c = remote(attn_all.at[0], attn_all.at[2], c_to)
-    attn_cy = remote(attn_all.at[1], attn_all.at[3], c_to)
+    attn_y, attn_c, attn_cy = [
+        [
+            remote(
+                attn_all.at[src, pl.ds(begin, count)], attn_all.at[dst, pl.ds(begin, count)], to
+            )
+            for begin, count in ((0, HALF), (TOK - HALF, HALF), (HALF, TOK - 2 * HALF))
+        ]
+        for src, dst, to in ((0, 1, y_to), (0, 2, c_to), (1, 3, c_to))
+    ]
     attn_x = remote(attn_all.at[0], attn_far, x_to)
     n1_x = share(n1_hbm, N1)
     n1_keep = local(turned, n1_hbm)
@@ -664,12 +669,9 @@
     pair_3 = remote(pair.at[core, 0], pair.at[core, 3], z3_to)
     pair_near = [remote(pair.at[core, i], pair.at[core, 4 + i], x_to) for i in range(4)]
     pair_core = [remote(pair.at[core, i], pair.at[core, i], c_to) for i in range(8)]
-    started(wo_y, wo_c)
-
     def norm_scale(rows):
         return lax.rsqrt(jnp.mean(rows * rows, axis=-1, keepdims=True) + EPSILON)
 
-    gain1, gain2 = gain_ref[0:1, :], gain_ref[1:2, :]
     sign = jnp.where(lax.broadcasted_iota(jnp.int32, (1, HD), 1) < HD // 2, 1.0, -1.0)
     is_key = jnp.where(core == 0, 1.0, 0.0)
 
@@ -679,7 +681,7 @@
     def turn_back(rows, cosines, sines):
         return rows * cosines + pltpu.roll(rows * sines, HD // 2, 1) * sign
 
-    def opening(x_rows, cot_rows, normed, w_query, w_pair):
+    def opening(x_rows, cot_rows, normed, w_query, w_pair, w_turned):
         loads = [
             local(x_hbm, x_rows),
             local(wq_hbm, w_query),
@@ -700,20 +702,37 @@
         def _():
             value_load.start()
 
+        lanes_of = [slice(i * HD, (i + 1) * HD) for i in range(width // HD)]
+        for i, lanes in enumerate(lanes_of):
+            gains[0:1, lanes] = gain1_ref[i : i + 1, :]
+            gains[1:2, lanes] = gain2_ref[i : i + 1, :]
+        places = pos_ref[pl.ds(me * 4, 4), :].astype(jnp.float32)
+        places = jnp.concatenate([places, places], 0).T
+        for i in range(4):
+            angle = places[:, i : i + 1] * freq_ref[...]
+            cosine[i * HD : (i + 1) * HD, :] = jnp.cos(angle)
+            sine[i * HD : (i + 1) * HD, :] = jnp.sin(angle)
         loads[0].wait()
 
         def norm(a, carry):
             rows = x_rows[rows_of(a), :].astype(jnp.float32)
-            normed[rows_of(a), :] = (rows * norm_scale(rows) * gain1).astype(jnp.bfloat16)
+            normed[rows_of(a), :] = (rows * norm_scale(rows) * gains[0:1, :]).astype(
+                jnp.bfloat16
+            )
             return carry
 
         lax.fori_loop(0, 4, norm, 0)
         key_load.wait()
-        rows = matmul(normed[...], w_pair[...]) + bias_ref[0:1, 3 * HD :]
+        rows = (
+            matmul(normed[...], w_pair[...])
+            + bk_ref[pl.ds(high, 1), :] * is_key
+            + bv_ref[pl.ds(high, 1), :] * (1.0 - is_key)
+        )
         pair[core, 0] = turn(
             rows, cosine[...] * is_key + (1.0 - is_key), sine[...] * is_key
         ).astype(jnp.bfloat16)
-        started(pair_1, pair_2, pair_3, pair_near[0], pair_core[0])
+        pl.semaphore_wait(barrier, 10)
+        started(pair_1, pair_2, pair_3, pair_near[0], pair_core[0], wo_y, wo_c)
         loads[2].wait()
 
         def flip_cot(a, carry):
@@ -723,13 +742,15 @@
         lax.fori_loop(0, 4, flip_cot, 0)
         own_blocks[0].start()
         loads[1].wait()
-        rows = matmul(normed[...], w_query[...]) + bias_ref[0:1, : 3 * HD]
+        rows = matmul(normed[...], w_query[...])
         for h in range(3):
-            query[h] = turn(rows[:, h * HD : (h + 1) * HD], cosine[...], sine[...]).astype(
-                jnp.bfloat16
-            )
+            query[h] = turn(
+                rows[:, h * HD : (h + 1) * HD] + bq_ref[h : h + 1, :], cosine[...], sine[...]
+            ).astype(jnp.bfloat16)
         own_blocks[0].wait()
         begin_spread(0)
+        w_turned[...] = w_query[...].T
+        turned_copy = started(local(w_turned, wq_turned_hbm))
         for copy, i in ((pair_1, 2), (pair_2, 1), (pair_3, 3)):
             copy.wait_recv()
             started(pair_near[i], pair_core[i])
@@ -746,10 +767,9 @@
             pair_core[4 + i].start()
         x_copy(0, 0).start()
         n1_keep.start()
-        n1_keep.wait()
-        started(*n1_x)
         for copy in pair_core:
             copy.wait_recv()
+        turned_copy.wait()
 
     pl.run_scoped(
         opening,
@@ -758,56 +778,81 @@
         pltpu.VMEM((TOK, width), jnp.bfloat16),
         pltpu.VMEM((width, 3 * HD), jnp.bfloat16),
         pltpu.VMEM((width, HD), jnp.bfloat16),
+        pltpu.VMEM((3 * HD, width), jnp.bfloat16),
     )
 
     def of_first(t):
+        t = t - t // 16
         late = t // 8
         device = t * (1 - late) + (15 - t) * late
         return device, late * (TOK - HALF)
 
-    def of_middle(t):
-        return t, HALF
-
-    def rows_at(t, locate, count):
-        device, offset = locate(t)
-        slot = (
+    def same_document(device):
+        ids = [docs_ref[pl.ds(4 * at + 1, 1), :] for at in (device, me)]
+        return jnp.concatenate([ids[0], ids[0]], 1) == jnp.concatenate([ids[1], ids[1]], 1)
+
+    def slot_of(device):
+        return (
             4 * ((device % 2 + b0) % 2)
             + 2 * (((device // 2) % 2 + b1) % 2)
             + (device // 4 + b2) % 2
         )
-        return device, slot, pl.ds(pl.multiple_of(offset, HALF), count)
-
-    def same_document(device):
-        return docs_ref[pl.ds(device, 1), :] == docs_ref[pl.ds(me, 1), :]
-
-    def attend_region(begin, count, blocks, locate, shared):
+
+    def places_of(step, wide):
+        if wide:
+            return [(slot_of(step), pl.ds(HALF, TOK - 2 * HALF))]
+        places = []
+        for block in (2 * step, 2 * step + 1):
+            device, offset = of_first(block)
+            places.append((slot_of(device), pl.ds(pl.multiple_of(offset, HALF), HALF)))
+        return places
+
+    def keys_of(which, step, wide):
+        parts = [pair[which, slot, rows, :] for slot, rows in places_of(step, wide)]
+        return parts[0] if wide else jnp.concatenate(parts, 0)
+
+    def seen(begin, count, blocks, wide):
+        shape = (3 * count, 2 * HALF)
+        row = lax.broadcasted_iota(jnp.int32, shape, 0) & (count - 1)
+        if not wide:
+            row = row + blocks % 2 * HALF
+        return row >= lax.broadcasted_iota(jnp.int32, shape, 1)
+
+    def regions():
+        return (
+            (0, HALF, me, False, me // 2),
+            (TOK - HALF, HALF, 15 - me, False, (15 - me) // 2),
+            (HALF, TOK - 2 * HALF, me, True, me),
+        )
+
+    def attend_region(begin, count, blocks, wide, steps):
         rows = 3 * count
         q_rows = region_rows(query, begin, count)
 
-        def score(t, diagonal=False):
-            device, slot, place = rows_at(t, locate, count)
-            scores = contract_cols(q_rows, pair[0, slot, place, :])
-            if diagonal:
-                return jnp.where(triangle(rows, count), scores, MASKED)
-            if shared:
-                return jnp.where(same_document(device), scores, MASKED)
-            return scores
-
-        def add(t, carry, scores):
-            _, slot, place = rows_at(t, locate, count)
+        def score(step):
+            scores = contract_cols(q_rows, keys_of(0, step, wide))
+            return jnp.where(same_document(step), scores, MASKED) if wide else scores
+
+        def add(step, carry, scores):
             total, accum = carry
             weights = jnp.exp2(scores * factor - peak)
             return total + weights, accum + matmul(
-                weights.astype(jnp.bfloat16), pair[1, slot, place, :]
+                weights.astype(jnp.bfloat16), keys_of(1, step, wide)
             )
 
-        last = score(blocks, True)
-        peak = lax.fori_loop(0, blocks, lambda t, top: jnp.maximum(top, score(t)), last)
+        last = jnp.where(
+            seen(begin, count, blocks, wide),
+            contract_cols(q_rows, keys_of(0, steps, wide)),
+            MASKED,
+        )
+        peak = lax.fori_loop(0, steps, lambda t, top: jnp.maximum(top, score(t)), last)
         peak = jnp.max(peak, axis=1, keepdims=True) * factor
         carry = add(
-            blocks, (jnp.zeros((rows, count), jnp.float32), jnp.zeros((rows, HD), jnp.float32)), last
-        )
-        total, accum = lax.fori_loop(0, blocks, lambda t, held: add(t, held, score(t)), carry)
+            steps,
+            (jnp.zeros((rows, 2 * HALF), jnp.float32), jnp.zeros((rows, HD), jnp.float32)),
+            last,
+        )
+        total, accum = lax.fori_loop(0, steps, lambda t, held: add(t, held, score(t)), carry)
         total = jnp.sum(total, axis=1, keepdims=True)
         result = accum / total
         logs = jnp.broadcast_to(peak + jnp.log2(total), (rows, HD))
@@ -841,20 +886,20 @@
         wo_c.wait_recv()
         started(*loads[:3], loads[5])
         started(*fetch(0, 0, UNITS))
-        attend_region(0, HALF, me, of_first, False)
-        attend_region(TOK - HALF, HALF, 15 - me, of_first, False)
+        attend_region(*regions()[0])
+        attend_region(*regions()[1])
+        started(*attn_y[:2], *attn_c[:2])
+        n1_keep.wait()
+        started(*n1_x)
+        arrive(0, 1)
+        arrive_inner(0, 2)
+        attend_region(*regions()[2])
+        started(attn_y[2], attn_c[2])
         wo_y.wait_recv()
         wo_cy.start()
         loads[3].start()
-        attend_region(HALF, TOK - 2 * HALF, me, of_middle, True)
-        started(attn_y, attn_c)
-        wo_cy.wait_recv()
-        loads[4].start()
-        arrive(0, 1)
-        arrive_inner(0, 2)
-        started(attn_x)
         pass_y(0, 0)
-        for load in loads[:4]:
+        for load in loads[:3]:
             load.wait()
         for copy in (pair_1, pair_2, pair_3, *pair_near, *pair_core):
             copy.wait_send()
@@ -868,25 +913,30 @@
             lax.fori_loop(0, width // 512, body, 0)
 
         add_part(0, True)
-        attn_c.wait_recv()
+        for copy in attn_c:
+            copy.wait_recv()
         add_part(2)
-        attn_y.wait_recv()
-        started(attn_cy)
+        for copy, forward_copy in zip(attn_y, attn_cy):
+            copy.wait_recv()
+            forward_copy.start()
+        loads[3].wait()
+        wo_cy.wait_recv()
+        loads[4].start()
         add_part(1)
-        attn_cy.wait_recv()
+        for copy in attn_cy:
+            copy.wait_recv()
         loads[4].wait()
         add_part(3)
 
         def norm(a, carry):
             rows = middle[rows_of(a), :]
-            turned[:, rows_of(a)] = (rows * norm_scale(rows) * gain2).astype(jnp.bfloat16).T
+            turned[:, rows_of(a)] = (rows * norm_scale(rows) * gains[1:2, :]).astype(jnp.bfloat16).T
             return carry
 
         lax.fori_loop(0, 4, norm, 0)
-        own_blocks[1].start()
-        own_blocks[1].wait()
         begin_spread(1)
         x_copy(1, 0).start()
+        own_blocks[1].start()
         loads[5].wait()
         acc[...] = jnp.zeros_like(acc)
 
@@ -917,27 +967,23 @@
                 )
                 started(*fetch(t + 1, 1 - slot, rest))
 
-            gate = matmul(weights[slot, 0], turned[...])
-            up_part = matmul(weights[slot, 1], turned[...])
-            grad_hidden = matmul(weights[slot, 2], cot_turned[...])
-            sigma = jax.nn.sigmoid(gate)
-            swish = gate * sigma
-            ring[slot, :, :UNITS] = (swish * up_part).astype(jnp.bfloat16).T
-            ring[slot, :, UNITS : 2 * UNITS] = (
-                (grad_hidden * up_part * sigma * (1.0 + gate * (1.0 - sigma)))
-                .astype(jnp.bfloat16)
-                .T
-            )
-            ring[slot, :, 2 * UNITS :] = (grad_hidden * swish).astype(jnp.bfloat16).T
-
-            def body(n, carry):
-                cols = pl.ds(pl.multiple_of(n * 512, 512), 512)
-                acc[:, cols] += matmul(
-                    ring[slot, :, UNITS : 2 * UNITS], weights[slot, 0, :, cols]
-                ) + matmul(ring[slot, :, 2 * UNITS :], weights[slot, 1, :, cols])
-                return carry
-
-            lax.fori_loop(0, width // 512, body, 0)
+            for part in (slice(0, TOK // 2), slice(TOK // 2, TOK)):
+                gate = matmul(weights[slot, 0], turned[:, part])
+                up_part = matmul(weights[slot, 1], turned[:, part])
+                grad_hidden = matmul(weights[slot, 2], cot_turned[:, part])
+                sigma = jax.nn.sigmoid(gate)
+                swish = gate * sigma
+                ring[slot, part, :UNITS] = (swish * up_part).astype(jnp.bfloat16).T
+                ring[slot, part, UNITS : 2 * UNITS] = (
+                    (grad_hidden * up_part * sigma * (1.0 + gate * (1.0 - sigma)))
+                    .astype(jnp.bfloat16)
+                    .T
+                )
+                ring[slot, part, 2 * UNITS :] = (grad_hidden * swish).astype(jnp.bfloat16).T
+            for part in (slice(0, TOK // 2), slice(TOK // 2, TOK)):
+                acc[part, :] += matmul(
+                    ring[slot, part, UNITS:], weights[slot, 0:2].reshape(2 * UNITS, width)
+                )
 
             @pl.when(t > 0)
             def _():
@@ -950,19 +996,21 @@
                 pass_core(0, 0)
                 pass_y(0, 1)
 
+            @pl.when(t == 6)
+            def _():
+                pass_y(1, 0)
+
             @pl.when(t == 7)
             def _():
                 arrive(1, 1)
                 arrive_inner(1, 2)
-                pass_y(1, 0)
-                pass_core(0, 1)
 
             keep_tile(t).start()
             return carry
 
         lax.fori_loop(0, tiles, tile, 0)
         keep_tile(tiles - 1).wait()
-        x_tile.start()
+        own_blocks[1].wait()
 
     pl.run_scoped(
         front,
@@ -973,42 +1021,36 @@
         pltpu.VMEM((width, TOK), jnp.bfloat16),
     )
 
-    def reduce_start(total, sent, core_to):
-        sent[...] = total[...].astype(jnp.bfloat16)
-        copies = [
-            remote(sent.at[rows_of(lane_c)], core_to.at[0], c_to),
-            remote(sent.at[rows_of(lane_cy)], core_to.at[1], c_to),
-        ]
-        started(*copies)
-        return copies
-
-    def reduce_middle(total, copies, core_to, lane_to):
-        for copy in copies:
-            copy.wait()
+    def reduce_copies():
+        return (
+            remote(rel.at[rows_of(lane_c)], core_in.at[0], c_to),
+            remote(rel.at[rows_of(lane_cy)], core_in.at[1], c_to),
+            remote(lane_send, lane_in, y_to),
+        )
+
+    def reduce_start(copies):
+        rel[...] = acc[...].astype(jnp.bfloat16)
+        started(*copies[:2])
+
+    def reduce_middle(copies):
+        copies[0].wait()
+        copies[1].wait()
         lane_send[...] = (
-            total[rows_of(lane_y), :] + core_to[1].astype(jnp.float32)
+            acc[rows_of(lane_y), :] + core_in[1].astype(jnp.float32)
         ).astype(jnp.bfloat16)
-        copy = remote(lane_send, lane_to, y_to)
-        copy.start()
-        return copy
-
-    def reduce_end(total, copy, core_to, lane_to):
-        copy.wait()
-        return (
-            total[rows_of(lane), :]
-            + core_to[0].astype(jnp.float32)
-            + lane_to[...].astype(jnp.float32)
-        )
-
-    def spread_start(full):
+        copies[2].start()
+
+    def reduce_end(copies, held):
+        copies[2].wait()
+        return held + core_in[0].astype(jnp.float32) + lane_in[...].astype(jnp.float32)
+
+    def spread_copies(full):
         mine, theirs = full.at[rows_of(lane)], full.at[rows_of(lane_y)]
-        copies = [
+        return [
             remote(mine, mine, y_to),
             remote(mine, mine, c_to),
             remote(theirs, theirs, c_to),
         ]
-        started(*copies[:2])
-        return copies
 
     def spread_end(copies):
         copies[0].wait_recv()
@@ -1019,38 +1061,30 @@
 
     near_base = used["remote"]
     used["remote"] += 4
-    near_loads = [local(near_hbm.at[r], near_stage) for r in range(4)]
 
     def near_copy(r):
         index = near_base + r
         return pltpu.make_async_remote_copy(
-            src_ref=sent_tile.at[rows_of_block(peers[r] - 4 * b2)], dst_ref=near_hbm.at[r],
+            src_ref=sent_tile.at[rows_of_block(peers[r] - 4 * b2)],
+            dst_ref=via_hbm if r == 3 else near_hbm.at[r],
             send_sem=send_sem.at[index], recv_sem=recv_sem.at[index],
-            device_id={"cp": peers[r]}, device_id_type=pl.DeviceIdType.MESH,
-        )
+            device_id={"cp": peers[1 if r == 3 else r]}, device_id_type=pl.DeviceIdType.MESH,
+        )
+
+    via_copy = remote(via_hbm, near_hbm.at[3], z1_to)
 
     final_base = used["local"]
-    used["local"] += 3
-
-    def final_copies(t):
-        return [
-            pltpu.make_async_copy(
-                final.at[:, pl.ds(k * UNITS, UNITS)],
-                tiles_out.at[k, :, pl.ds(pl.multiple_of(t * UNITS, UNITS), UNITS)],
-                local_sem.at[final_base + k],
-            )
-            for k in range(3)
-        ]
-
-    def finish_tile(t, value):
-        final[...] = value
-        started(*final_copies(t))
-        for copy in final_copies(t):
-            copy.wait()
+    used["local"] += 24
 
     SMALL = {"out": (0, 384, GB), "query": (384, 384, N1), "pair": (768, 128, N1)}
     small_base = used["remote"]
     used["remote"] += 6
+    pair_hops = [
+        remote(
+            small_s.at[pl.ds(p * block, block), pl.ds(768, HD)], pair_terms.at[p - 1], to
+        )
+        for p, to in ((1, z2_to), (2, z1_to), (3, z3_to))
+    ]
 
     def small_copy(name, second):
         begin, wide, _ = SMALL[name]
@@ -1071,10 +1105,13 @@
         small_s[half:, cols] = (
             matmul(own_a[index, half:, :], b_own) + matmul(far_a[index, 1], b_far)
         ).astype(jnp.bfloat16)
-        small_copy(name, 0).start()
+        if name != "pair":
+            small_copy(name, 0).start()
         small_s[:half, cols] = (
             matmul(own_a[index, :half, :], b_own) + matmul(far_a[index, 0], b_far)
         ).astype(jnp.bfloat16)
+        if name == "pair":
+            started(*pair_hops)
 
     def small_second(name):
         begin, wide, _ = SMALL[name]
@@ -1098,10 +1135,6 @@
         )
 
     query_x = remote(grad_query, query_far, x_to)
-    query_y = remote(grad_query, query_hbm.at[1], y_to)
-    query_c = remote(grad_query, query_hbm.at[2], c_to)
-    query_cy = remote(query_hbm.at[1], query_hbm.at[3], c_to)
-    query_own = local(grad_query, query_hbm.at[0])
     pair_x = remote(grad_pair, pair_far, x_to)
     pair_y = remote(grad_pair, pair_hbm.at[1], y_to)
     pair_c = remote(grad_pair, pair_hbm.at[2], c_to)
@@ -1110,34 +1143,48 @@
     here = output_out.at[rows_of(lane)]
     there = output_out.at[rows_of(lane_y)]
     out_spread = [
-        remote(grad_full.at[rows_of(lane)], here, y_to),
-        remote(grad_full.at[rows_of(lane)], here, c_to),
+        remote(lane_send, here, y_to),
+        remote(lane_send, here, c_to),
         remote(there, there, c_to),
     ]
-    out_own = local(grad_full.at[rows_of(lane)], here)
-
-    def rest_of(grads, wo_own, second, cots, weights, ring, total_tile):
+    out_own = local(lane_send, here)
+
+    query_reduction = reduce_copies()
+
+    def rest_of(grads, wo_own, second, cots, weights, w_last, ring, total_tile):
         mine = [b0 + 2 * b1 + 4 * i for i in range(2)]
         weight_loads = [
-            local(source.at[pl.ds(pl.multiple_of(tile * UNITS, UNITS), UNITS)], weights.at[i, k])
+            local(
+                source.at[pl.ds(pl.multiple_of(tile * UNITS, UNITS), UNITS)],
+                weights.at[k, pl.ds(i * UNITS, UNITS)],
+            )
             for i, tile in enumerate(mine)
             for k, source in enumerate((wg_hbm, wu_hbm, wd_hbm))
         ]
         wo_load = local(wo_hbm, wo_own)
-        started(*weight_loads, wo_load)
+        own_tiles = [
+            local(
+                own_hbm.at[tile, :, pl.ds(k * UNITS, UNITS)],
+                ring.at[:, pl.ds((2 * k + i) * UNITS, UNITS)],
+            )
+            for i, tile in enumerate(mine)
+            for k in range(3)
+        ]
         block_base = used["local"]
-        used["local"] += 4
-        own_tiles = [local(own_hbm.at[tile], ring) for tile in mine]
+        used["local"] += 3
         own_rows = pl.ds(pl.multiple_of(b2 * wide_half, wide_half), wide_half)
-
-        def block_loads(j, side):
-            slot = (2 * j + side) % 2
-            return [
-                pltpu.make_async_copy(
-                    all_hbm.at[k, block_of(j, side)], ref.at[slot], local_sem.at[block_base + 2 * slot + k]
-                )
-                for k, ref in ((0, cots), (1, second))
-            ]
+        order = ((0, 0), (1, 0), (0, 1), (1, 1), (2, 0), (3, 0), (2, 1), (3, 1))
+
+        def load_second(j, side):
+            slot = order.index((j, side)) % 2
+            return pltpu.make_async_copy(
+                all_hbm.at[1, block_of(j, side)], second.at[slot], local_sem.at[block_base + slot]
+            )
+
+        def load_cots(j, side):
+            return pltpu.make_async_copy(
+                all_hbm.at[0, block_of(j, side)], cots, local_sem.at[block_base + 2]
+            )
 
         def prefetch(j, side):
             if side:
@@ -1146,58 +1193,87 @@
             elif j:
                 c_copy(0, j, 1 - core).wait_recv()
                 c_copy(1, j, 1 - core).wait_recv()
-            started(*block_loads(j, side))
-
-        def product(j, side):
-            slot = (2 * j + side) % 2
-            loads = block_loads(j, side)
-            first = j == 0 and side == 0
-            loads[1].wait()
-            for i in range(2):
-                if first:
-                    own_tiles[i].start()
-                    own_tiles[i].wait()
-                    if i == 0:
-                        loads[0].wait()
-                else:
-                    gate = matmul(weights[i, 0], second[slot])
-                    up_part = matmul(weights[i, 1], second[slot])
+            load_second(j, side).start()
+
+        def product(q):
+            slot = q % 2
+            pltpu.make_async_copy(
+                all_hbm.at[1, 0], second.at[slot], local_sem.at[block_base + slot]
+            ).wait()
+            cots_load = pltpu.make_async_copy(
+                all_hbm.at[0, 0], cots, local_sem.at[block_base + 2]
+            )
+
+            @pl.when(q == 0)
+            def _():
+                for load in own_tiles:
+                    load.wait()
+                cots_load.wait()
+
+            @pl.when(q > 0)
+            def _():
+                for part in (slice(0, TOK // 2), slice(TOK // 2, TOK)):
+                    gate = matmul(weights[0], second[slot, :, part])
+                    up_part = matmul(weights[1], second[slot, :, part])
                     sigma = jax.nn.sigmoid(gate)
                     swish = gate * sigma
-                    ring[:, :UNITS] = (swish * up_part).astype(jnp.bfloat16).T
-                    if i == 0:
-                        loads[0].wait()
-                    grad_hidden = matmul(weights[i, 2], cots[slot])
-                    ring[:, UNITS : 2 * UNITS] = (
+                    ring[part, : 2 * UNITS] = (swish * up_part).astype(jnp.bfloat16).T
+                    if part.start == 0:
+                        cots_load.wait()
+                    grad_hidden = matmul(weights[2], cots[:, part])
+                    ring[part, 2 * UNITS : 4 * UNITS] = (
                         (grad_hidden * up_part * sigma * (1.0 + gate * (1.0 - sigma)))
                         .astype(jnp.bfloat16)
                         .T
                     )
-                    ring[:, 2 * UNITS :] = (grad_hidden * swish).astype(jnp.bfloat16).T
-                for n, rows in enumerate((cots, second, second)):
-                    cols = slice(n * UNITS, (n + 1) * UNITS)
-                    total_cols = slice((3 * i + n) * UNITS, (3 * i + n + 1) * UNITS)
-                    value = matmul(rows[slot, own_rows, :], ring[:, cols])
-                    if first:
-                        total_tile[:, total_cols] = value
-                    else:
-                        total_tile[:, total_cols] += value
+                    ring[part, 4 * UNITS :] = (grad_hidden * swish).astype(jnp.bfloat16).T
+
+            for n in range(3):
+                cols = slice(2 * n * UNITS, 2 * (n + 1) * UNITS)
+                rows = second[slot, own_rows, :] if n else cots[own_rows, :]
+                total_tile[:, cols] += matmul(rows, ring[:, cols])
 
         far_loads = [
             local(
                 all_hbm.at[k, block_of(0, side), row_block(0, p // 2, p % 2)],
-                (far_a.at[k, p // 2, pl.ds((p % 2) * block, block)] if side else own_a.at[k, pl.ds(p * block, block)]),
+                (
+                    far_a.at[k, p // 2, pl.ds((p % 2) * block, block)]
+                    if side
+                    else own_a.at[k, pl.ds(p * block, block)]
+                ),
             )
             for k in range(2)
             for side in range(2)
             for p in range(4)
         ]
-        stage, far_stage = sent_tile.at[:TOK, : 3 * UNITS], sent_tile.at[:TOK, 3 * UNITS :]
-        last_loads = [local(own_hbm.at[tiles - 1], stage), local(far_hbm, far_stage)]
+        last_loads = [local(own_hbm.at[tiles - 1], sent_tile.at[:TOK, : 3 * UNITS])]
+        last_weights = [
+            local(source.at[pl.ds((tiles - 1) * UNITS, rest)], w_last.at[k])
+            for k, source in enumerate((wg_hbm, wu_hbm, wd_hbm))
+        ]
+
+        def last_far():
+            slot = order.index((0, 1)) % 2
+            for load in last_weights:
+                load.wait()
+            padding = jnp.zeros((TOK, UNITS - rest), jnp.bfloat16)
+            gate = matmul(w_last[0], second[slot])
+            up_part = matmul(w_last[1], second[slot])
+            grad_hidden = matmul(w_last[2], cots[...])
+            sigma = jax.nn.sigmoid(gate)
+            swish = gate * sigma
+            parts = (
+                swish * up_part,
+                grad_hidden * up_part * sigma * (1.0 + gate * (1.0 - sigma)),
+                grad_hidden * swish,
+            )
+            for k, part in enumerate(parts):
+                begin = (3 + k) * UNITS
+                sent_tile[:TOK, begin : begin + UNITS] = jnp.concatenate(
+                    [part.astype(jnp.bfloat16).T, padding], 1
+                )
 
         def last_first():
-            x_tile.wait_recv()
-            started(*far_loads, *last_loads)
             for load in (*far_loads, *last_loads):
                 load.wait()
 
@@ -1216,41 +1292,29 @@
 
             def kept(n, carry):
                 cols, value = body(n, 0)
-                part_k[:, cols] = value
+                part_k[:, cols] = value.astype(jnp.bfloat16)
                 return carry
 
             lax.fori_loop(0, 3, sent, 0)
             z1_tile.start()
             lax.fori_loop(0, 3, kept, 0)
 
-        copies = reduce_start(acc, rel, core_in)
-        prefetch(0, 0)
-        for load in weight_loads:
-            load.wait()
-        lane_copy = reduce_middle(acc, copies, core_in, lane_in)
-        product(0, 0)
-        pass_core(1, 0)
-        arrive_outer(0, 3)
-        grad_full[rows_of(lane), :] = reduce_end(acc, lane_copy, core_in, lane_in).astype(
-            jnp.bfloat16
-        )
-        spread = spread_start(grad_full)
-        cot_load = started(local(cot_hbm, rel))
-        prefetch(0, 1)
-        pass_y(0, 2)
-        pass_y(1, 1)
-        product(0, 1)
-        arrive_inner(1, 3)
-        grads[...] = jnp.zeros_like(grads)
-        spread_end(spread)
-        cot_load.wait()
-        wo_load.wait()
+        reduction = reduce_copies()
+        wq_load = local(wq_turned_hbm, wo_own)
+        spread = spread_copies(grad_full)
+        cot_load = local(cot_hbm, rel)
+        kv_c = remote(kv_send.at[pl.ds(0, 8)], kv_in.at[pl.ds(0, 8)], c_to)
+        kv_x = remote(kv_send.at[pl.ds(0, 4)], kv_in.at[pl.ds(8, 4)], x_to)
+        kv_1 = remote(kv_send.at[pl.ds(4, 2)], kv_in.at[pl.ds(12, 2)], z1_to)
+        kv_2 = remote(kv_send.at[pl.ds(6, 1)], kv_in.at[pl.ds(14, 1)], z2_to)
+        keep_by = is_key * scale + (1.0 - is_key)
+        send_by = (1.0 - is_key) * scale + is_key
 
         def middle_back(a, total):
             grad = grad_full[rows_of(a), :].astype(jnp.float32)
             rows = middle[rows_of(a), :]
             factor2 = norm_scale(rows)
-            weighted = grad * gain2
+            weighted = grad * gains[1:2, :]
             result = (
                 rel[rows_of(a), :].astype(jnp.float32)
                 + factor2 * weighted
@@ -1260,25 +1324,7 @@
             turned[:, rows_of(a)] = result.astype(jnp.bfloat16).T
             return total + jnp.sum(grad * rows * factor2, axis=0, keepdims=True)
 
-        sums[...] = jnp.zeros_like(sums)
-        sums[0, 1:2, :] = lax.fori_loop(
-            0, 4, middle_back, jnp.zeros((1, width), jnp.float32)
-        )
-        middle_copy = started(local(acc, middle_hbm))
-        branch_x = share(turned, GB)
-        pass_core(0, 2)
-        attn_cy.wait_send()
-        attn_all[1] = matmul(wo_own[...], turned[...]).astype(jnp.bfloat16).T
-        for p in range(4):
-            own_a[GB, p * block : (p + 1) * block, :] = turned[row_block(0, p // 2, p % 2), :]
-        arrive_outer(1, 2)
-        prefetch(1, 0)
-        product(1, 0)
-        pass_core(1, 1)
-        pass_core(0, 3)
-        last_first()
-
-        def region(begin, count, blocks, locate, shared):
+        def region(begin, count, blocks, wide, steps):
             heads = query.shape[0]
             rows = heads * count
             q_rows = region_rows(query, begin, count)
@@ -1292,23 +1338,26 @@
                 keepdims=True,
             )
 
-            def add(t, carry, diagonal=False):
-                device, slot, place = rows_at(t, locate, count)
-                keys, values = pair[0, slot, place, :], pair[1, slot, place, :]
+            def add(step, carry, last=False):
+                keys, values = keys_of(0, step, wide), keys_of(1, step, wide)
                 probs = jnp.exp2(contract_cols(q_rows, keys) * factor - logs)
-                if diagonal:
-                    probs = jnp.where(triangle(rows, count), probs, 0.0)
-                elif shared:
-                    probs = jnp.where(same_document(device), probs, 0.0)
+                if last:
+                    probs = jnp.where(seen(begin, count, blocks, wide), probs, 0.0)
+                elif wide:
+                    probs = jnp.where(same_document(step), probs, 0.0)
                 grad_scores = (probs * (contract_cols(grad_rows, values) - delta)).astype(
                     jnp.bfloat16
                 )
-                grads[0, slot, place, :] += contract_rows(grad_scores, q_rows)
-                grads[1, slot, place, :] += contract_rows(probs.astype(jnp.bfloat16), grad_rows)
+                key_part = contract_rows(grad_scores, q_rows)
+                value_part = contract_rows(probs.astype(jnp.bfloat16), grad_rows)
+                for i, (slot, place) in enumerate(places_of(step, wide)):
+                    part = slice(None) if wide else slice(i * HALF, (i + 1) * HALF)
+                    grads[0, slot, place, :] += key_part[part]
+                    grads[1, slot, place, :] += value_part[part]
                 return carry + matmul(grad_scores, keys)
 
-            total = add(blocks, jnp.zeros((rows, HD), jnp.float32), True)
-            total = lax.fori_loop(0, blocks, add, total) * scale
+            total = add(steps, jnp.zeros((rows, HD), jnp.float32), True)
+            total = lax.fori_loop(0, steps, add, total) * scale
             cosines, sines = cosine[begin : begin + count, :], sine[begin : begin + count, :]
             for h in range(heads):
                 part = total[h * count : (h + 1) * count]
@@ -1316,38 +1365,13 @@
                     turn_back(part, cosines, sines)
                 ).astype(jnp.bfloat16)
 
-        region(0, HALF, me, of_first, False)
-        region(TOK - HALF, HALF, 15 - me, of_first, False)
-        prefetch(1, 1)
-        product(1, 1)
-        prefetch(2, 0)
-        arrive_outer(1, 3)
-        pass_core(1, 2)
-        region(HALF, TOK - 2 * HALF, me, of_middle, True)
-
-        keep_by = is_key * scale + (1.0 - is_key)
-        send_by = (1.0 - is_key) * scale + is_key
-
         def to_core(s, carry):
             kv_send[s] = (grads[1 - core, s] * send_by).astype(jnp.bfloat16)
             return carry
 
-        lax.fori_loop(0, 8, to_core, 0)
-        kv_c = remote(kv_send.at[pl.ds(0, 8)], kv_in.at[pl.ds(0, 8)], c_to)
-        kv_x = remote(kv_send.at[pl.ds(0, 4)], kv_in.at[pl.ds(8, 4)], x_to)
-        kv_1 = remote(kv_send.at[pl.ds(4, 2)], kv_in.at[pl.ds(12, 2)], z1_to)
-        kv_2 = remote(kv_send.at[pl.ds(6, 1)], kv_in.at[pl.ds(14, 1)], z2_to)
-        kv_c.start()
-        started(query_y, query_c, query_own)
-        product(2, 0)
-        prefetch(2, 1)
-        kv_c.wait()
-
         def from_core(s, carry):
             grads[core, s] = grads[core, s] * keep_by + kv_in[s].astype(jnp.float32)
             return carry
-
-        lax.fori_loop(0, 8, from_core, 0)
 
         def pass_on(copy, first, count):
             def cast(s, carry):
@@ -1366,47 +1390,137 @@
 
             lax.fori_loop(0, count, add, 0)
 
-        pass_on(kv_x, 8, 4)
-        started(query_x, *branch_x, wq_y, wq_c)
-        product(2, 1)
-        prefetch(3, 0)
-        z1_tile.wait_recv()
-        part_s2[...] = (
-            part_k[block:, :] + near1[block:, :].astype(jnp.float32)
-        ).astype(jnp.bfloat16)
-        z2_tile.start()
-        product(3, 0)
-        take(kv_x, 8, 4)
-        pass_on(kv_1, 12, 2)
-        pass_core(1, 3)
-        prefetch(3, 1)
-        n1_forward = forward(N1)
-        for copy in n1_x:
-            copy.wait()
-        n1_forward.start()
-        product(3, 1)
+        def stage_0():
+            reduce_start(reduction)
+            total_tile[...] = jnp.zeros_like(total_tile)
+            reduce_middle(reduction)
+            prefetch(1, 0)
+            started(*weight_loads, wo_load)
+            pass_core(1, 0)
+
+        def stage_1():
+            started(*last_weights, attn_x)
+            for load in weight_loads:
+                load.wait()
+
+        def stage_2():
+            arrive_inner(1, 3)
+            prefetch(0, 1)
+            grads[...] = jnp.zeros_like(grads)
+            grad_full[rows_of(lane), :] = reduce_end(reduction, acc[rows_of(lane), :]).astype(
+                jnp.bfloat16
+            )
+            started(*spread[:2])
+            cot_load.start()
+            pass_core(0, 1)
+
+        def stage_3():
+            last_far()
+            spread_end(spread)
+            pass_y(1, 1)
+            cot_load.wait()
+            wo_load.wait()
+            z_copy(1, 0).wait_send()
+            x_copy(1, 0).wait_send()
+
+            @when(inner)
+            def _():
+                z_copy(1, 1).wait_send()
+
+            sums[...] = jnp.zeros_like(sums)
+            gain2_part = lax.fori_loop(0, 4, middle_back, jnp.zeros((1, width), jnp.float32))
+            for i in range(width // HD):
+                sums[12 + i : 13 + i, :] = gain2_part[:, i * HD : (i + 1) * HD]
+            middle_copy.start()
+            for copy in attn_cy:
+                copy.wait_send()
+            attn_all[1] = matmul(wo_own[...], turned[...]).astype(jnp.bfloat16).T
+            wq_load.start()
+            arrive_outer(1, 2)
+            arrive_outer(0, 3)
+            region(*regions()[0])
+            pass_y(0, 2)
+            region(*regions()[1])
+            pass_core(1, 1)
+            region(*regions()[2])
+            lax.fori_loop(0, 8, to_core, 0)
+            kv_c.start()
+            arrive_outer(1, 3)
+            prefetch(1, 1)
+            prefetch(2, 0)
+
+        def stage_4():
+            started(*far_loads, *last_loads)
+            kv_c.wait()
+            lax.fori_loop(0, 8, from_core, 0)
+            pass_on(kv_x, 8, 4)
+            pass_y(1, 2)
+            pass_y(0, 3)
+            pass_core(0, 2)
+            wq_load.wait()
+            middle_copy.wait()
+            acc[...] = matmul(grad_query[...], wo_own[...])
+            reduce_start(query_reduction)
+
+        def stage_5():
+            prefetch(3, 0)
+            last_first()
+            started(*branch_x)
+            pass_core(1, 2)
+
+        def stage_6():
+            prefetch(2, 1)
+            take(kv_x, 8, 4)
+            pass_on(kv_1, 12, 2)
+            started(query_x)
+            pass_y(1, 3)
+            pass_core(0, 3)
+            for p in range(4):
+                own_a[GB, p * block : (p + 1) * block, :] = turned[
+                    row_block(0, p // 2, p % 2), :
+                ]
+            for copy in n1_x:
+                copy.wait()
+            n1_forward.start()
+
+        def stage_7():
+            z1_tile.wait_recv()
+            part_s2[...] = (
+                part_k[block:, :].astype(jnp.float32) + near1[block:, :].astype(jnp.float32)
+            ).astype(jnp.bfloat16)
+            z2_tile.start()
+            reduce_middle(query_reduction)
+            held_query[...] = acc[rows_of(lane), :].astype(jnp.bfloat16)
+            take(kv_1, 12, 2)
+            pass_on(kv_2, 14, 1)
+            pass_core(1, 3)
+            n1_forward.wait()
+            prefetch(3, 1)
+
+        stages = (stage_0, stage_1, stage_2, stage_3, stage_4, stage_5, stage_6, stage_7)
+
+        def body(q, carry):
+            for at, (stage, of) in enumerate(zip(stages, order)):
+
+                @pl.when(q == at)
+                def _(stage=stage, of=of):
+                    stage()
+                    if of != order[0]:
+                        load_cots(*of).start()
+
+            product(q)
+            return carry
+
+        prefetch(0, 0)
+        load_cots(0, 0).start()
+        started(*own_tiles)
+        lax.fori_loop(0, len(order), body, 0)
         sent_tile[...] = total_tile[...].astype(jnp.bfloat16)
-        take(kv_1, 12, 2)
-        pass_on(kv_2, 14, 1)
-        for r in (3, 1, 2):
-            near_copy(r).start()
-        query_y.wait_recv()
-        query_cy.start()
+        near_copy(2).start()
         for copy in branch_x:
             copy.wait()
-        branch_c = started(forward(GB))
-        for i, tile in enumerate(mine):
-            finish_tile(
-                tile,
-                total_tile[
-                    rows_of_block(me - 4 * b2), i * 3 * UNITS : (i + 1) * 3 * UNITS
-                ],
-            )
-        attn_x.wait()
-        branch_c.wait()
-        small_first("out", attn_all[0], attn_far[...])
+        branch_forward.start()
         query_x.wait()
-        n1_forward.wait()
         small_first("query", grad_query[...], query_far[...])
         kv_2.wait()
         f_cos = cosine[...] * is_key + (1.0 - is_key)
@@ -1414,138 +1528,137 @@
         total = grads[core, 0] + kv_in[14].astype(jnp.float32)
         grad_pair[...] = turn_back(total, f_cos, f_sin).astype(jnp.bfloat16)
         started(pair_x, pair_y, pair_c, pair_own)
-        wq_y.wait_recv()
-        wq_cy.start()
-
-        def down(weights, hidden):
-            def fetch(t, slot, rows):
-                return [
-                    pltpu.make_async_copy(
-                        wd_hbm.at[pl.ds(t * UNITS, rows)],
-                        weights.at[slot, pl.ds(0, rows)],
-                        weight_sem.at[slot, 0],
-                    ),
-                    pltpu.make_async_copy(
-                        own_hbm.at[t, :, pl.ds(0, UNITS)], hidden.at[slot], weight_sem.at[slot, 1]
-                    ),
-                ]
-
-            started(*fetch(0, 0, UNITS))
-
-            def tile(t, carry):
-                slot = t % 2
-
-                @pl.when(t < tiles - 1)
-                def _():
-                    for copy in fetch(t, slot, UNITS):
-                        copy.wait()
-
-                @pl.when(t == tiles - 1)
-                def _():
-                    for copy in fetch(t, slot, rest):
-                        copy.wait()
-
-                @pl.when(t + 1 < tiles - 1)
-                def _():
-                    started(*fetch(t + 1, 1 - slot, UNITS))
-
-                @pl.when(t + 1 == tiles - 1)
-                def _():
-                    weights[1 - slot, rest:, :] = jnp.zeros((UNITS - rest, width), weights.dtype)
-                    started(*fetch(t + 1, 1 - slot, rest))
-
-                def body(n, carry):
-                    cols = pl.ds(pl.multiple_of(n * 512, 512), 512)
-                    product = matmul(hidden[slot], weights[slot, :, cols])
-                    acc[:, cols] = jnp.where(t == 0, product, acc[:, cols] + product)
-                    return carry
-
-                lax.fori_loop(0, width // 512, body, 0)
-                return carry
-
-            lax.fori_loop(0, tiles, tile, 0)
-
-        middle_copy.wait()
-        pl.run_scoped(
-            down,
-            pltpu.VMEM((2, UNITS, width), jnp.bfloat16),
-            pltpu.VMEM((2, TOK, UNITS), jnp.bfloat16),
-        )
-        out_copies = reduce_start(acc, rel, core_in)
-        small_second("out")
-        out_lane = reduce_middle(acc, out_copies, core_in, lane_in)
-        small_second("query")
-        z2_tile.wait_recv()
-        finish_tile(
-            tiles - 1,
-            part_k[:block, :]
-            + near1[:block, :].astype(jnp.float32)
-            + near2[...].astype(jnp.float32),
-        )
-        out_rows = reduce_end(acc, out_lane, core_in, lane_in) + middle[rows_of(lane), :]
-        grad_full[rows_of(lane), :] = out_rows.astype(jnp.bfloat16)
-        started(out_spread[0], out_spread[1], out_own)
-
+        near_copy(3).start()
+        branch_forward.wait()
+        attn_x.wait()
+        small_first("out", attn_all[0], attn_far[...])
+
+    n1_forward = forward(N1)
+    branch_x = share(turned, GB)
+    branch_forward = forward(GB)
+    middle_copy = local(acc, middle_hbm)
     pl.run_scoped(
         rest_of,
         pltpu.VMEM((2, 8, TOK, HD), jnp.float32),
         pltpu.VMEM((width // 4, width), jnp.bfloat16),
         pltpu.VMEM((2, width, TOK), jnp.bfloat16),
-        pltpu.VMEM((2, width, TOK), jnp.bfloat16),
-        pltpu.VMEM((2, 3, UNITS, width), jnp.bfloat16),
-        pltpu.VMEM((TOK, 3 * UNITS), jnp.bfloat16),
+        pltpu.VMEM((width, TOK), jnp.bfloat16),
+        pltpu.VMEM((3, 2 * UNITS, width), jnp.bfloat16),
+        pltpu.VMEM((3, rest, width), jnp.bfloat16),
+        pltpu.VMEM((TOK, 6 * UNITS), jnp.bfloat16),
         pltpu.VMEM((width // 2, 6 * UNITS), jnp.float32),
     )
-    pair_x.wait()
-    small_first("pair", grad_pair[...], pair_far[...])
-    pair_y.wait_recv()
-    pair_cy.start()
-    out_spread[0].wait_recv()
-    out_spread[2].start()
-    small_third("out", wo_out)
-    pair_cy.wait_recv()
-    pair_c.wait_recv()
-    query_own.wait()
-    pair_own.wait()
-    query_c.wait_recv()
-    query_cy.wait_recv()
-    wq_c.wait_recv()
-    wq_cy.wait_recv()
-
-    def closing(x_rows, queries, pairs, w_queries, w_pairs):
-        loads = [
-            local(query_hbm, queries),
-            local(wq_all.at[pl.ds(1, 3)], w_queries.at[pl.ds(1, 3)]),
-            local(wq_hbm, w_queries.at[0]),
-            local(pair_hbm, pairs),
-            local(wk_hbm, w_pairs.at[0]),
-            local(wv_hbm, w_pairs.at[1]),
-            local(x_hbm, x_rows),
-            local(middle_hbm, middle),
+
+    def closing(
+        x_rows, pres, w_pres, w_down, hidden, near_low, final, held
+    ):
+        gathered_pair = []
+        loads = [local(x_hbm, x_rows)]
+        pairs_load = [
+            local(pair_hbm.at[p], pres.at[:, pl.ds(p * HD, HD)]) for p in range(4)
         ]
-        started(*loads)
-        for load in loads:
+        for p, far in enumerate(TP_ORDER):
+            head = (high + far // 2) % 2
+            lanes = pl.ds(pl.multiple_of(head * HD, HD), HD)
+            index = used["local"]
+            used["local"] += 1
+            key_load, value_load = [
+                pltpu.make_async_copy(
+                    source.at[:, lanes],
+                    w_pres.at[:, pl.ds(p * HD, HD)],
+                    local_sem.at[index],
+                )
+                for source in (wk_hbm, wv_hbm)
+            ]
+            kind = (core + far % 2) % 2
+
+            @pl.when(kind == 0)
+            def _(key_load=key_load):
+                key_load.start()
+
+            @pl.when(kind == 1)
+            def _(value_load=value_load):
+                value_load.start()
+
+            gathered_pair.append(key_load)
+        middle_load = local(middle_hbm, middle)
+        wide_unit = 2 * UNITS
+        steps = [
+            (t, min(wide_unit, units - t * wide_unit)) for t in range(pl.cdiv(units, wide_unit))
+        ]
+
+        def fetch(t, rows):
+            slot = t % 2
+            copies = [
+                pltpu.make_async_copy(
+                    wd_hbm.at[pl.ds(t * wide_unit, rows)],
+                    w_down.at[slot, pl.ds(0, rows)],
+                    weight_sem.at[slot, 0],
+                )
+            ]
+            for i in range(pl.cdiv(rows, UNITS)):
+                copies.append(
+                    pltpu.make_async_copy(
+                        own_hbm.at[2 * t + i, :, pl.ds(0, UNITS)],
+                        hidden.at[slot, :, pl.ds(i * UNITS, UNITS)],
+                        weight_sem.at[slot, 1 + i],
+                    )
+                )
+            return copies
+
+        started(*fetch(*steps[0]), *loads)
+        for t, rows in steps:
+            slot = t % 2
+            if t + 1 < len(steps):
+                more = steps[t + 1][1]
+                if more < wide_unit:
+                    end = pl.cdiv(more, UNITS) * UNITS
+                    w_down[1 - slot, more:end, :] = jnp.zeros((end - more, width), w_down.dtype)
+                started(*fetch(*steps[t + 1]))
+            for copy in fetch(t, rows):
+                copy.wait()
+            depth = pl.cdiv(rows, UNITS) * UNITS
+
+            for part in (slice(0, TOK // 2), slice(TOK // 2, TOK)):
+                value = matmul(hidden[slot, part, :depth], w_down[slot, :depth, :])
+                if t == 0:
+                    acc[part, :] = value
+                else:
+                    acc[part, :] += value
+            if t == 0:
+                pair_y.wait_recv()
+                pair_cy.start()
+                pair_c.wait_recv()
+                pair_own.wait()
+            if t == 1:
+                pair_cy.wait_recv()
+                started(*pairs_load)
+                pair_x.wait()
+                small_first("pair", grad_pair[...], pair_far[...])
+                for load in (*pairs_load, *gathered_pair):
+                    load.wait()
+                grad_full[rows_of(lane), :] = (
+                    reduce_end(query_reduction, held_query[...].astype(jnp.float32))
+                    + contract_cols(pres[rows_of(lane), :], w_pres[...])
+                ).astype(jnp.bfloat16)
+                started(*normed_spread[:2])
+        acc[rows_of(lane), :] += middle[rows_of(lane), :]
+        middle_load.start()
+        near_copy(3).wait_recv()
+        via_copy.start()
+        near_copy(1).start()
+        spread_end(normed_spread)
+        reduce_start(out_reduction)
+        reduce_middle(out_reduction)
+        held[...] = acc[rows_of(lane), :]
+        for load in (*loads, middle_load):
             load.wait()
 
-        def part_of(n, carry):
-            cols = pl.ds(pl.multiple_of(n * 512, 512), 512)
-            total = jnp.zeros((TOK, 512), jnp.float32)
-            for p, far in enumerate(TP_ORDER):
-                kind = (core + far % 2) % 2
-                head = (high + far // 2) % 2
-                lanes = pl.ds(pl.multiple_of(head * HD, HD), HD)
-                total += contract_cols(queries[p], w_queries[p, cols, :])
-                total += contract_cols(pairs[p], w_pairs[kind, cols, lanes])
-            acc[:, cols] = total
-            return carry
-
-        lax.fori_loop(0, width // 512, part_of, 0)
-
         def last(a, total):
-            grad = acc[rows_of(a), :]
+            grad = grad_full[rows_of(a), :].astype(jnp.float32)
             rows = x_rows[rows_of(a), :].astype(jnp.float32)
             scale1 = norm_scale(rows)
-            weighted = grad * gain1
+            weighted = grad * gains[0:1, :]
             rel[rows_of(a), :] = (
                 middle[rows_of(a), :]
                 + scale1 * weighted
@@ -1554,76 +1667,133 @@
             return total + jnp.sum(grad * rows * scale1, axis=0, keepdims=True)
 
         gain1_part = lax.fori_loop(0, 4, last, jnp.zeros((1, width), jnp.float32))
-        copy = started(local(rel, input_out))
-        sums[0, 0:1, :] = gain1_part
-        sums[0, 2:3, : 3 * HD] = jnp.sum(
-            grad_query[...].astype(jnp.float32), axis=0, keepdims=True
-        )
-        sums[0, 2:3, 3 * HD : 4 * HD] = jnp.sum(
-            grad_pair[...].astype(jnp.float32), axis=0, keepdims=True
-        )
-        sums_copies[0].start()
-        copy.wait()
-
+        input_copy = started(local(rel, input_out))
+        for i in range(width // HD):
+            sums[i : i + 1, :] = gain1_part[:, i * HD : (i + 1) * HD]
+        bias_part = jnp.sum(grad_query[...].astype(jnp.float32), axis=0, keepdims=True)
+        for h in range(3):
+            sums[24 + h : 25 + h, :] = bias_part[:, h * HD : (h + 1) * HD]
+        for p, far in enumerate(TP_ORDER):
+            row = 27 + 2 * ((core + far % 2) % 2) + (high + far // 2) % 2
+            lanes = slice(p * HD, (p + 1) * HD)
+            sums[pl.ds(row, 1), :] = jnp.sum(
+                pres[:, lanes].astype(jnp.float32), axis=0, keepdims=True
+            )
+        started(*sums_copies)
+        small_second("query")
+        lane_send[...] = reduce_end(out_reduction, held[...]).astype(jnp.bfloat16)
+        started(out_spread[0], out_spread[1], out_own)
+        for copy in pair_hops:
+            copy.wait()
+        w_pair_grad[...] = small_s[:block, 768 : 768 + HD].astype(jnp.float32) + sum(
+            pair_terms[i].astype(jnp.float32) for i in range(3)
+        )
+        started(*w_pair_copies)
+
+        mine_rows = rows_of_block(me - 4 * b2)
+
+        def tile_copies(r):
+            tile = peers[r] - 4 * b2
+            return [
+                pltpu.make_async_copy(
+                    (near_low.at[r - 1] if r else sent_tile.at[mine_rows]).at[
+                        :, pl.ds((2 * k + i) * UNITS, UNITS)
+                    ],
+                    tiles_out.at[
+                        k, :, pl.ds(pl.multiple_of((tile + 4 * i) * UNITS, UNITS), UNITS)
+                    ],
+                    local_sem.at[final_base + 6 * r + 2 * k + i],
+                )
+                for k in range(3)
+                for i in range(2)
+            ]
+
+        started(*tile_copies(0))
+        near_loads = [None] + [local(near_hbm.at[r], near_low.at[r - 1]) for r in (1, 2, 3)]
+        for r in (2, 1, 3):
+            if r == 3:
+                via_copy.wait_recv()
+            else:
+                near_copy(r).wait_recv()
+            near_loads[r].start()
+            if r == 1:
+                small_second("out")
+                out_spread[0].wait_recv()
+                out_spread[2].start()
+            near_loads[r].wait()
+            started(*tile_copies(r))
+        z2_tile.wait_recv()
+        final[...] = (
+            part_k[:block, :].astype(jnp.float32)
+            + near1[:block, :].astype(jnp.float32)
+            + near2[...].astype(jnp.float32)
+        ).astype(jnp.bfloat16)
+        last_copies = [
+            local(
+                final.at[:, pl.ds(k * UNITS, UNITS)],
+                tiles_out.at[k, :, pl.ds((tiles - 1) * UNITS, UNITS)],
+            )
+            for k in range(3)
+        ]
+        started(*last_copies)
+        small_third("out", wo_out)
+        small_third("query", wq_out)
+        input_copy.wait()
+        for r in range(4):
+            for copy in tile_copies(r):
+                copy.wait()
+        for copy in last_copies:
+            copy.wait()
+
+    out_reduction = reduce_copies()
+    normed_spread = spread_copies(grad_full)
     sums_copies = [
-        remote(sums.at[i], sums_in.at[i], to) for i, to in enumerate((x_to, z1_to, z2_to))
+        remote(sums, sums_in.at[r], {"cp": peers[r]}) for r in range(1, 8)
     ]
+    w_pair_place = wkv_out.at[core, :, pl.ds(pl.multiple_of(high * HD, HD), HD)]
+    w_pair_copies = [remote(w_pair_grad, w_pair_place, to) for to in (y_to, c_to, cy_to)]
+    w_pair_copies.append(local(w_pair_grad, w_pair_place))
     pl.run_scoped(
         closing,
         pltpu.VMEM((TOK, width), jnp.bfloat16),
-        pltpu.VMEM((4, TOK, 3 * HD), jnp.bfloat16),
-        pltpu.VMEM((4, TOK, HD), jnp.bfloat16),
-        pltpu.VMEM((4, width, 3 * HD), jnp.bfloat16),
-        pltpu.VMEM((2, width, 2 * HD), jnp.bfloat16),
+        pltpu.VMEM((TOK, 4 * HD), jnp.bfloat16),
+        pltpu.VMEM((width, 4 * HD), jnp.bfloat16),
+        pltpu.VMEM((2, 2 * UNITS, width), jnp.bfloat16),
+        pltpu.VMEM((2, TOK, 2 * UNITS), jnp.bfloat16),
+        pltpu.VMEM((3, block, 6 * UNITS), jnp.bfloat16),
+        pltpu.VMEM((block, 3 * UNITS), jnp.bfloat16),
+        pltpu.VMEM((quarter, width), jnp.float32),
     )
-    sums_copies[0].wait()
-    sums[1] = sums[0] + sums_in[0]
-    sums_copies[1].start()
-    small_second("pair")
-    small_third("query", wq_out)
-
-    def take_near(r):
-        near_copy(r).wait_recv()
-        near_loads[r].start()
-        near_loads[r].wait()
-        for i in range(2):
-            finish_tile(
-                peers[r] - 4 * b2 + 4 * i,
-                near_stage[:, i * 3 * UNITS : (i + 1) * 3 * UNITS].astype(jnp.float32),
-            )
-
-    take_near(1)
-    take_near(2)
-    sums_copies[1].wait()
-    sums[2] = sums[1] + sums_in[1]
-    sums_copies[2].start()
-    take_near(3)
-    small_third("pair", wp_out)
-    sums_copies[2].wait()
-    sums_out[...] = sums[2] + sums_in[2]
-    x_tile.wait_send()
+    for copy in sums_copies:
+        copy.wait()
+    sums_out[...] = sums[...] + sum(sums_in[r] for r in range(1, 8))
+    for copy in w_pair_copies:
+        copy.wait()
     z1_tile.wait_send()
     z2_tile.wait_send()
     for r in (1, 2, 3):
         near_copy(r).wait_send()
+    via_copy.wait_send()
+    z_copy(0, 0).wait_send()
+    x_copy(0, 0).wait_send()
+
+    @when(inner)
+    def _():
+        z_copy(0, 1).wait_send()
+        for k in range(2):
+            for m in (2, 3, 4):
+                z_copy(k, m).wait_send()
+
     for k in range(2):
-        z_copy(k, 0).wait_send()
-
-        @when(inner)
-        def _():
-            for m in (1, 2, 3, 4):
-                z_copy(k, m).wait_send()
-
         for j in range(4):
             if j:
                 c_copy(k, j).wait_send()
-            x_copy(k, j).wait_send()
+                x_copy(k, j).wait_send()
             if (k, j) not in WHOLE_HALVES:
                 y_copy(k, j).wait_send()
             d_copy(k, j).wait_send()
     for copy in (
-        attn_y, attn_c, query_y, query_c, query_cy, pair_y, pair_c, pair_cy,
-        out_spread[0], wo_y, wo_c, wo_cy, wq_y, wq_c, wq_cy,
+        *attn_y, *attn_c, pair_y, pair_c, pair_cy, out_spread[0], wo_y, wo_c, wo_cy,
     ):
         copy.wait_send()
     for copy in (out_spread[1], out_spread[2]):
@@ -1632,13 +1802,14 @@
     assert used["remote"] <= REMOTE and used["local"] <= LOCAL, used
 
 
-WHOLE_HALVES = ((0, 3), (1, 2), (1, 3))
+WHOLE_HALVES = ()
 REMOTE = 134
-LOCAL = 130
+LOCAL = 150
 
 
 def whole_layer(
-    docs, gains, biases, cosine, sine, x, cot, w_query, w_key, w_value, w_out, w_gate, w_up, w_down
+    docs, places, freq, gain1, gain2, b_query, b_key, b_value,
+    x, cot, w_query, w_key, w_value, w_out, w_gate, w_up, w_down,
 ):
     tok_rows, width = x.shape
     units = w_gate.shape[0]
@@ -1648,32 +1819,35 @@
     shape = jax.ShapeDtypeStruct
     any_ = pl.BlockSpec(memory_space=pl.ANY)
     outs = (
-        shape((3, block, tiles * UNITS), wide),
+        shape((3, block, tiles * UNITS), low),
         shape((block, 384), wide),
         shape((block, 384), wide),
-        shape((block, HD), wide),
-        shape((8, width), wide),
+        shape((2, block, 2 * HD), wide),
+        shape((32, HD), wide),
         shape((tok_rows, width), low),
         shape((tok_rows, width), low),
         shape((tok_rows, width), wide),
-        shape((4, tok_rows, 384), low),
         shape((4, tok_rows, HD), low),
         shape((tiles, tok_rows, 3 * UNITS), low),
-        shape((tok_rows, 3 * UNITS), low),
         shape((4, block, 6 * UNITS), low),
         shape((4,) + w_out.shape, low),
-        shape((4,) + w_query.shape, low),
+        shape(w_query.shape[::-1], low),
         shape((2, 8, width, tok_rows), low),
         shape((width, tok_rows), low),
+        shape((block, 6 * UNITS), low),
     )
     vmem = pltpu.VMEM
     scratch = [
+        vmem((tok_rows, HD), wide),
+        vmem((tok_rows, HD), wide),
+        vmem((2, width), wide),
+        vmem((block, HD), wide),
         vmem((3, tok_rows, HD), low),
         vmem((2, 8, tok_rows, HD), low),
         vmem((3, tok_rows, HD), wide),
         vmem((3, tok_rows, HD), wide),
-        vmem((3, 8, width), wide),
-        vmem((3, 8, width), wide),
+        vmem((32, HD), wide),
+        vmem((8, 32, HD), wide),
         vmem((4, tok_rows, 384), low),
         vmem((tok_rows, 384), low),
         vmem((tok_rows, 384), low),
@@ -1684,18 +1858,17 @@
         vmem((4, width // 2, tok_rows), low),
         vmem((4, 2, half, tok_rows), low),
         vmem((half, 3 * UNITS), low),
-        vmem((half, 3 * UNITS), wide),
+        vmem((half, 3 * UNITS), low),
         vmem((half, 3 * UNITS), low),
         vmem((block, 3 * UNITS), low),
         vmem((block, 3 * UNITS), low),
-        vmem((block, 6 * UNITS), low),
-        vmem((block, 3 * UNITS), wide),
         vmem((width // 2, 6 * UNITS), low),
         vmem((tok_rows, width), low),
         vmem((2, quarter, width), low),
         vmem((quarter, width), low),
         vmem((quarter, width), low),
         vmem((tok_rows, width), low),
+        vmem((quarter, width), low),
         vmem((8, tok_rows, HD), low),
         vmem((15, tok_rows, HD), low),
         vmem((tok_rows, 384), low),
@@ -1704,6 +1877,7 @@
         vmem((half, 896), low),
         vmem((block, 896), low),
         vmem((block, 896), low),
+        vmem((3, block, HD), low),
         pltpu.SemaphoreType.DMA((REMOTE,)),
         pltpu.SemaphoreType.DMA((REMOTE,)),
         pltpu.SemaphoreType.DMA((LOCAL,)),
@@ -1712,8 +1886,8 @@
     return pl.pallas_call(
         functools.partial(back_kernel, width, units),
         out_shape=outs,
-        in_specs=[VMEM] * 5 + [any_] * 9,
-        out_specs=(any_, VMEM, VMEM, VMEM, VMEM) + (any_,) * 12,
+        in_specs=[VMEM] * 8 + [any_] * 9,
+        out_specs=(any_, VMEM, VMEM, any_, VMEM) + (any_,) * 11,
         scratch_shapes=scratch,
         compiler_params=pltpu.CompilerParams(
             vmem_limit_bytes=64 * 1024 * 1024, collective_id=0, has_side_effects=True
@@ -1721,7 +1895,10 @@
         cost_estimate=pl.CostEstimate(
             flops=20 * tok_rows * width * units, bytes_accessed=10 * width * units, transcendentals=0
         ),
-    )(docs, gains, biases, cosine, sine, x, cot, w_query, w_key, w_value, w_out, w_gate, w_up, w_down)
+    )(
+        docs, places, freq, gain1, gain2, b_query, b_key, b_value,
+        x, cot, w_query, w_key, w_value, w_out, w_gate, w_up, w_down,
+    )
 
 
 def on_device(
@@ -1752,6 +1929,36 @@
     kv_index = lane * heads // (H // kv_heads)
     is_key = core == 0
 
+    if shards == 8 and tok_rows == TOK:
+        half = HD // 2
+        freq = ROPE_BASE ** (-(jnp.arange(half, dtype=jnp.float32) * 2.0 / HD))
+        tiles, grad_w_out, grad_w_query, grad_w_pairs, sums, output, grad_input, *_ = whole_layer(
+            doc_ids.reshape(-1, HD), positions.reshape(-1, HD),
+            jnp.concatenate([freq, freq])[None],
+            norm1_gain.reshape(-1, HD), norm2_gain.reshape(-1, HD),
+            b_query.reshape(-1, HD), b_key.reshape(-1, HD), b_value.reshape(-1, HD),
+            layer_input, cotangent, w_query, w_key, w_value, w_out,
+            w_gate.T, w_up.T, w_down,
+        )
+        units = w_gate.shape[1]
+        wide = width // HD
+        return (
+            output,
+            grad_input,
+            sums[:wide].reshape(-1),
+            grad_w_query,
+            sums[24 : 24 + heads].reshape(-1),
+            grad_w_pairs[0],
+            sums[27:29].reshape(-1),
+            grad_w_pairs[1],
+            sums[29:31].reshape(-1),
+            grad_w_out.T,
+            sums[wide : 2 * wide].reshape(-1),
+            tiles[1, :, :units].astype(jnp.float32),
+            tiles[2, :, :units].astype(jnp.float32),
+            tiles[0, :, :units].astype(jnp.float32).T,
+        )
+
     def assemble(parts, axis):
         at = lambda index: lax.dynamic_index_in_dim(parts, reverse_bits(lane ^ index, 2), 0, keepdims=False)
         return (
@@ -1815,35 +2022,6 @@
     cosine, sine = rope_tables(my_pos, HD)
 
     pair_bias = lax.dynamic_slice_in_dim(jnp.where(is_key, b_key, b_value), kv_index * HD, HD)
-
-    if shards == 8 and tok_rows == TOK:
-        tiles, grad_w_out, grad_w_query, grad_w_pair, sums, output, grad_input, *_ = whole_layer(
-            jnp.broadcast_to(middle_docs[:, None], (shards, 2 * HALF)),
-            jnp.stack([norm1_gain, norm2_gain]),
-            jnp.concatenate([b_query, pair_bias])[None],
-            cosine, sine, layer_input, cotangent, w_query, w_key, w_value, w_out,
-            w_gate.T, w_up.T, w_down,
-        )
-        units = w_gate.shape[1]
-        bias_query, bias_pair = sums[2, : heads * HD], sums[2, heads * HD : (heads + 1) * HD]
-        bias_key, bias_value = assemble(gather_tp(bias_pair[None], 0), 0)
-        grad_w_key, grad_w_value = assemble(gather_tp(grad_w_pair[None], 0), 1)
-        return (
-            output,
-            grad_input,
-            sums[0],
-            grad_w_query,
-            bias_query,
-            grad_w_key,
-            bias_key,
-            grad_w_value,
-            bias_value,
-            grad_w_out.T,
-            sums[1],
-            tiles[1, :, :units],
-            tiles[2, :, :units],
-            tiles[0, :, :units].T,
-        )
 
     inputs = layer_input.astype(jnp.float32)
     scale1 = lax.rsqrt(jnp.mean(inputs * inputs, axis=-1, keepdims=True) + EPSILON)

time: 316 us -> 242 us (0.77); the launches traced: 310 us -> 241 us
  Pallas kernels: 282 us -> 225 us
  local copies, waits for them, and re-layouts: 15.3 us -> 10.3 us
    pallas_call x1, Pallas kernels: 282 us -> 225 us  [whole_layer(): pl.pallas_call(functools.partial(back_kernel, width, units), out_shape=ou...]
    transpose x1 -> x0, local copies, waits for them, and re-layouts: 5.06 us -> none  [on_device(): tiles[0, :, :units]]
    concatenate x10 -> x0, other arithmetic: 4.85 us -> none  [the longest x1 1.26 us: on_device(): jnp.concatenate([b_query, pair_bias])[None]]
    transpose x0 -> x1, other arithmetic: none -> 4.3 us  [on_device(): tiles[0, :, :units].astype(jnp.float32)]
    slice x4 -> x0, local copies, waits for them, and re-layouts: 3.6 us -> none  [the longest x1 1.51 us: on_device(): sums[1]]
    reshape x1 -> x3, local copies, waits for them, and re-layouts: 0.72 us -> 3.96 us  [the longest x1 1.38 us: on_device(): sums[wide:2 * wide].reshape(-1)]
  transfers between devices with their start and end apart: 4 -> 0, of which waited for: 2 -> 0; matrix products, arithmetic and copies ran while one was open for 3% -> 0% of each run, Pallas kernels for 0% -> 0%
where the time goes in v4:
time: 242 us; the launch traced here: 241 us
  Pallas kernels  225 us (93%)
  local copies, waits for them, and re-layouts  10.3 us (4%)
  other arithmetic  4.9 us (2%)
    pallas_call x1, Pallas kernels, whole_layer(): pl.pallas_call(functools.partial(back_kernel, width, units), out_shape=ou...  225 us

profile of v4, /device:TPU:0, one launch (start us, length us, event | category | flops | bytes accessed | tf_op | source)
XLA Modules:
  0.0 240.9 jit_solution(486463308023012284)
XLA Ops:
  0.7 0.6 maximum_bitcast_fusion.refs_2_
  1.2 225.0 %shard_map.263 = (bf16[3,192,2304]{2,1,0:T(8,128)(2,1)}, f32[192,384]{1,0:T(8,128)}, f32[192,384]{1,0:T(8,128)}, f32[2,192,256]{2,1,0:T(8,128)}, f32[32,128]{1,0...) custom-call(s32[32,128]{1,0:T(8,128)} %bitcast.40, ...), custom_call_target="tpu_custom_call" | custom-call | flops 35232153600 | bytes 34406400 | tf_op jit(solution)/shard_map/pallas_call | solution.py:1886
  226.3 1.3 slice_bitcast_fusion.4
  227.6 1.3 slice_bitcast_fusion.5
  228.9 1.4 slice_bitcast_fusion.2
  230.3 1.8 slice_bitcast_fusion
  232.0 0.0 copy-start.1
  232.0 4.3 %convert_bitcast_fusion = (f32[2240,192]{0,1:T(8,128)}, f32[192,2240]{1,0:T(8,128)}, f32[192,2240]{1,0:T(8,128)}) fusion(bf16[3,192,2304]{2,1,0:T(8,128)(2,1)} %get-tuple-element.27), kind=kLoop, calls=%fused_computation | loop fusion | flops 1290240 | bytes 7741440 | tf_op jit(solution)/shard_map/transpose | solution.py:1959
  236.4 0.0 copy-start
  236.4 0.0 copy-done.1
  236.4 1.1 copy.34
  237.5 0.8 copy-done
  238.3 0.0 copy-start.3
  238.3 0.0 copy-start.2
  238.3 1.1 copy.35
  239.5 0.0 copy-done.3
  239.5 0.7 copy.36
  240.2 0.0 copy-done.2
  240.2 0.7 copy.37
  (1 shorter events, 0.0 us)
Async XLA Ops:
  232.0 4.3 %copy-start.1 = (bf16[512,1536]{1,0:T(8,128)(2,1)S(1)}, bf16[512,1536]{1,0:T(8,128)(2,1)}, u32[]{:S(2)}) copy-start(bf16[512,1536]{1,0:T(8,128)(2,1)} %get-tuple-element.51) | copy-start | bytes 4718596
  236.4 2.0 copy-start
  238.3 1.1 copy-start.3
  238.3 1.9 copy-start.2

commit v5 on v4

--- a/solution.py
+++ b/solution.py
@@ -475,6 +475,7 @@
         wg_hbm, wu_hbm, wd_hbm,
         tiles_out, wo_out, wq_out, wkv_out, sums_out, output_out, input_out,
         middle_hbm, pair_hbm, own_hbm, near_hbm, wo_all, wq_turned_hbm, all_hbm, n1_hbm, via_hbm,
+        out_core_hbm, out_lane_hbm,
         cosine, sine, gains, w_pair_grad, query, pair, full, log_total, sums, sums_in,
         attn_all, attn_far, query_far, pair_far, middle, acc, turned,
         own_a, far_a, part_s, part_k, near1, part_s2, near2, sent_tile,
@@ -1445,8 +1446,8 @@
             region(*regions()[2])
             lax.fori_loop(0, 8, to_core, 0)
             kv_c.start()
+            prefetch(1, 1)
             arrive_outer(1, 3)
-            prefetch(1, 1)
             prefetch(2, 0)
 
         def stage_4():
@@ -1482,18 +1483,24 @@
             for copy in n1_x:
                 copy.wait()
             n1_forward.start()
-
-        def stage_7():
             z1_tile.wait_recv()
             part_s2[...] = (
                 part_k[block:, :].astype(jnp.float32) + near1[block:, :].astype(jnp.float32)
             ).astype(jnp.bfloat16)
             z2_tile.start()
+
+        def stage_7():
+            for copy in branch_x:
+                copy.wait()
+            branch_forward.start()
             reduce_middle(query_reduction)
             held_query[...] = acc[rows_of(lane), :].astype(jnp.bfloat16)
             take(kv_1, 12, 2)
             pass_on(kv_2, 14, 1)
             pass_core(1, 3)
+            branch_forward.wait()
+            attn_x.wait()
+            small_first("out", attn_all[0], attn_far[...])
             n1_forward.wait()
             prefetch(3, 1)
 
@@ -1517,9 +1524,6 @@
         lax.fori_loop(0, len(order), body, 0)
         sent_tile[...] = total_tile[...].astype(jnp.bfloat16)
         near_copy(2).start()
-        for copy in branch_x:
-            copy.wait()
-        branch_forward.start()
         query_x.wait()
         small_first("query", grad_query[...], query_far[...])
         kv_2.wait()
@@ -1529,9 +1533,6 @@
         grad_pair[...] = turn_back(total, f_cos, f_sin).astype(jnp.bfloat16)
         started(pair_x, pair_y, pair_c, pair_own)
         near_copy(3).start()
-        branch_forward.wait()
-        attn_x.wait()
-        small_first("out", attn_all[0], attn_far[...])
 
     n1_forward = forward(N1)
     branch_x = share(turned, GB)
@@ -1644,13 +1645,20 @@
                 started(*normed_spread[:2])
         acc[rows_of(lane), :] += middle[rows_of(lane), :]
         middle_load.start()
+        reduce_start(out_reduction)
+        for copy in out_reduction[:2]:
+            copy.wait()
+        out_core_load.start()
+        out_core_load.wait()
+        lane_send[...] = (
+            acc[rows_of(lane_y), :] + core_in[1].astype(jnp.float32)
+        ).astype(jnp.bfloat16)
+        out_reduction[2].start()
+        held[...] = acc[rows_of(lane), :] + core_in[0].astype(jnp.float32)
         near_copy(3).wait_recv()
         via_copy.start()
         near_copy(1).start()
         spread_end(normed_spread)
-        reduce_start(out_reduction)
-        reduce_middle(out_reduction)
-        held[...] = acc[rows_of(lane), :]
         for load in (*loads, middle_load):
             load.wait()
 
@@ -1680,8 +1688,12 @@
                 pres[:, lanes].astype(jnp.float32), axis=0, keepdims=True
             )
         started(*sums_copies)
+        small_second("out")
         small_second("query")
-        lane_send[...] = reduce_end(out_reduction, held[...]).astype(jnp.bfloat16)
+        out_reduction[2].wait()
+        out_lane_load.start()
+        out_lane_load.wait()
+        lane_send[...] = (held[...] + lane_in[...].astype(jnp.float32)).astype(jnp.bfloat16)
         started(out_spread[0], out_spread[1], out_own)
         for copy in pair_hops:
             copy.wait()
@@ -1716,12 +1728,10 @@
             else:
                 near_copy(r).wait_recv()
             near_loads[r].start()
-            if r == 1:
-                small_second("out")
-                out_spread[0].wait_recv()
-                out_spread[2].start()
             near_loads[r].wait()
             started(*tile_copies(r))
+        out_spread[0].wait_recv()
+        out_spread[2].start()
         z2_tile.wait_recv()
         final[...] = (
             part_k[:block, :].astype(jnp.float32)
@@ -1745,7 +1755,13 @@
         for copy in last_copies:
             copy.wait()
 
-    out_reduction = reduce_copies()
+    out_reduction = (
+        remote(rel.at[rows_of(lane_c)], out_core_hbm.at[0], c_to),
+        remote(rel.at[rows_of(lane_cy)], out_core_hbm.at[1], c_to),
+        remote(lane_send, out_lane_hbm, y_to),
+    )
+    out_core_load = local(out_core_hbm, core_in)
+    out_lane_load = local(out_lane_hbm, lane_in)
     normed_spread = spread_copies(grad_full)
     sums_copies = [
         remote(sums, sums_in.at[r], {"cp": peers[r]}) for r in range(1, 8)
@@ -1835,6 +1851,8 @@
         shape((2, 8, width, tok_rows), low),
         shape((width, tok_rows), low),
         shape((block, 6 * UNITS), low),
+        shape((2, quarter, width), low),
+        shape((quarter, width), low),
     )
     vmem = pltpu.VMEM
     scratch = [
@@ -1887,7 +1905,7 @@
         functools.partial(back_kernel, width, units),
         out_shape=outs,
         in_specs=[VMEM] * 8 + [any_] * 9,
-        out_specs=(any_, VMEM, VMEM, any_, VMEM) + (any_,) * 11,
+        out_specs=(any_, VMEM, VMEM, any_, VMEM) + (any_,) * 13,
         scratch_shapes=scratch,
         compiler_params=pltpu.CompilerParams(
             vmem_limit_bytes=64 * 1024 * 1024, collective_id=0, has_side_effects=True

time: 242 us -> 237 us (0.979)
  Pallas kernels: 225 us -> 220 us
    pallas_call x1, Pallas kernels: 225 us -> 220 us  [whole_layer(): pl.pallas_call(functools.partial(back_kernel, width, units), out_shape=ou...]
where the time goes in v5:
time: 237 us; the launch traced here: 236 us
  Pallas kernels  220 us (93%)
  local copies, waits for them, and re-layouts  10.3 us (4%)
  other arithmetic  4.9 us (2%)
    pallas_call x1, Pallas kernels, whole_layer(): pl.pallas_call(functools.partial(back_kernel, width, units), out_shape=ou...  220 us

profile of v5, /device:TPU:0, one launch (start us, length us, event | category | flops | bytes accessed | tf_op | source)
XLA Modules:
  0.0 236.0 jit_solution(3898411059245843927)
XLA Ops:
  0.7 0.6 maximum_bitcast_fusion.refs_2_
  1.2 220.2 %shard_map.263 = (bf16[3,192,2304]{2,1,0:T(8,128)(2,1)}, f32[192,384]{1,0:T(8,128)}, f32[192,384]{1,0:T(8,128)}, f32[2,192,256]{2,1,0:T(8,128)}, f32[32,128]{1,0...) custom-call(s32[32,128]{1,0:T(8,128)} %bitcast.40, ...), custom_call_target="tpu_custom_call" | custom-call | flops 35232153600 | bytes 34406400 | tf_op jit(solution)/shard_map/pallas_call | solution.py:1904
  221.4 1.3 slice_bitcast_fusion.4
  222.7 1.3 slice_bitcast_fusion.5
  224.0 1.4 slice_bitcast_fusion.2
  225.4 1.8 slice_bitcast_fusion
  227.2 0.0 copy-start.1
  227.2 4.3 %convert_bitcast_fusion = (f32[2240,192]{0,1:T(8,128)}, f32[192,2240]{1,0:T(8,128)}, f32[192,2240]{1,0:T(8,128)}) fusion(bf16[3,192,2304]{2,1,0:T(8,128)(2,1)} %get-tuple-element.27), kind=kLoop, calls=%fused_computation | loop fusion | flops 1290240 | bytes 7741440 | tf_op jit(solution)/shard_map/transpose | solution.py:1977
  231.5 0.0 copy-start
  231.5 0.0 copy-done.1
  231.5 1.1 copy.34
  232.6 0.8 copy-done
  233.5 0.0 copy-start.3
  233.5 0.0 copy-start.2
  233.5 1.1 copy.35
  234.6 0.0 copy-done.3
  234.6 0.7 copy.36
  235.3 0.0 copy-done.2
  235.3 0.7 copy.37
  (1 shorter events, 0.0 us)
Async XLA Ops:
  227.2 4.3 %copy-start.1 = (bf16[512,1536]{1,0:T(8,128)(2,1)S(1)}, bf16[512,1536]{1,0:T(8,128)(2,1)}, u32[]{:S(2)}) copy-start(bf16[512,1536]{1,0:T(8,128)(2,1)} %get-tuple-element.51) | copy-start | bytes 4718596
  231.5 2.0 copy-start
  233.5 1.1 copy-start.3
  233.5 1.9 copy-start.2

commit v6 on v5

--- a/solution.py
+++ b/solution.py
@@ -1643,6 +1643,8 @@
                     + contract_cols(pres[rows_of(lane), :], w_pres[...])
                 ).astype(jnp.bfloat16)
                 started(*normed_spread[:2])
+            if t == 3:
+                small_second("out")
         acc[rows_of(lane), :] += middle[rows_of(lane), :]
         middle_load.start()
         reduce_start(out_reduction)
@@ -1658,6 +1660,7 @@
         near_copy(3).wait_recv()
         via_copy.start()
         near_copy(1).start()
+        small_second("query")
         spread_end(normed_spread)
         for load in (*loads, middle_load):
             load.wait()
@@ -1688,8 +1691,6 @@
                 pres[:, lanes].astype(jnp.float32), axis=0, keepdims=True
             )
         started(*sums_copies)
-        small_second("out")
-        small_second("query")
         out_reduction[2].wait()
         out_lane_load.start()
         out_lane_load.wait()

time: 237 us -> 238 us (level)
  no operation moved by 1% of the time
where the time goes in v6:
time: 238 us; the launch traced here: 237 us
  Pallas kernels  221 us (93%)
  local copies, waits for them, and re-layouts  10.3 us (4%)
  other arithmetic  4.9 us (2%)
    pallas_call x1, Pallas kernels, whole_layer(): pl.pallas_call(functools.partial(back_kernel, width, units), out_shape=ou...  221 us

profile of v6, /device:TPU:0, one launch (start us, length us, event | category | flops | bytes accessed | tf_op | source)
XLA Modules:
  0.0 237.0 jit_solution(16111642320204114036)
XLA Ops:
  0.7 0.6 maximum_bitcast_fusion.refs_2_
  1.2 221.2 %shard_map.263 = (bf16[3,192,2304]{2,1,0:T(8,128)(2,1)}, f32[192,384]{1,0:T(8,128)}, f32[192,384]{1,0:T(8,128)}, f32[2,192,256]{2,1,0:T(8,128)}, f32[32,128]{1,0...) custom-call(s32[32,128]{1,0:T(8,128)} %bitcast.40, ...), custom_call_target="tpu_custom_call" | custom-call | flops 35232153600 | bytes 34406400 | tf_op jit(solution)/shard_map/pallas_call | solution.py:1905
  222.4 1.3 slice_bitcast_fusion.4
  223.7 1.3 slice_bitcast_fusion.5
  225.0 1.4 slice_bitcast_fusion.2
  226.4 1.8 slice_bitcast_fusion
  228.2 0.0 copy-start.1
  228.2 4.3 %convert_bitcast_fusion = (f32[2240,192]{0,1:T(8,128)}, f32[192,2240]{1,0:T(8,128)}, f32[192,2240]{1,0:T(8,128)}) fusion(bf16[3,192,2304]{2,1,0:T(8,128)(2,1)} %get-tuple-element.27), kind=kLoop, calls=%fused_computation | loop fusion | flops 1290240 | bytes 7741440 | tf_op jit(solution)/shard_map/transpose | solution.py:1978
  232.5 0.0 copy-start
  232.5 0.0 copy-done.1
  232.5 1.1 copy.34
  233.6 0.8 copy-done
  234.5 0.0 copy-start.3
  234.5 0.0 copy-start.2
  234.5 1.1 copy.35
  235.6 0.0 copy-done.3
  235.6 0.7 copy.36
  236.3 0.0 copy-done.2
  236.3 0.7 copy.37
  (1 shorter events, 0.0 us)
Async XLA Ops:
  228.2 4.3 %copy-start.1 = (bf16[512,1536]{1,0:T(8,128)(2,1)S(1)}, bf16[512,1536]{1,0:T(8,128)(2,1)}, u32[]{:S(2)}) copy-start(bf16[512,1536]{1,0:T(8,128)(2,1)} %get-tuple-element.51) | copy-start | bytes 4718596
  232.5 2.0 copy-start
  234.5 1.1 copy-start.3
  234.5 1.9 copy-start.2
